TPU v7x, 32 devices: a whole 2x2x4 slice. The times are simulated.
32 devices in a mesh: rep: 16 (over z, y, x), shard: 2 (over core).
Axes of the slice: x: 2, y: 2, z: 4, core: 2. Of those that a mesh axis runs over, the one named last changes fastest.
Arguments:
- tokens: bfloat16 [8192, 1024], P(('rep', 'shard')), may hold values from -6 to 6
- lengths: int32 [32, 4], P(('rep', 'shard')), may hold values from 1 to 253, as said below
- norm_gain: bfloat16 [1024], P('shard'), may hold values from 0.099609375 to 1.8984375
- in_weight: bfloat16 [1024, 4384], P('shard'), may hold values from -0.1875 to 0.1875
- conv_weight: bfloat16 [2304, 4], P('shard'), may hold values from -3 to 3
- conv_bias: bfloat16 [2304], P('shard'), may hold values from -3 to 3
- step_bias: bfloat16 [32], P('shard'), may hold values from -7 to -2.5
- decay_log: bfloat16 [32], P('shard'), may hold values from 0 to 2.796875
- skip_gain: bfloat16 [32], P('shard'), may hold values from 0.5 to 2
- gate_gain: bfloat16 [2048], P('shard'), may hold values from 0.099609375 to 1.8984375
- out_weight: bfloat16 [2048, 1024], P('shard'), may hold values from -0.125 to 0.125
- cotangent: bfloat16 [8192, 1024], P(('rep', 'shard')), may hold values from -6 to 6
Outputs:
- output: bfloat16 [8192, 1024], P(('rep', 'shard'))
- input_grad: float32 [8192, 1024], P(('rep', 'shard'))
- norm_gain_grad: float32 [1024], P('shard')
- in_weight_grad: float32 [1024, 4384], P('shard')
- conv_weight_grad: float32 [2304, 4], P('shard')
- conv_bias_grad: float32 [2304], P('shard')
- step_bias_grad: float32 [32], P('shard')
- decay_log_grad: float32 [32], P('shard')
- skip_gain_grad: float32 [32], P('shard')
- gate_gain_grad: float32 [2048], P('shard')
- out_weight_grad: float32 [2048, 1024], P('shard')
Inputs may be any that keep to these rules, and one draw needn't show every extreme that they name: `lengths`: each device's sequences fill its first rows in order and hold 256 rows at most, exactly so on some device; the rows after them are padding.
All inputs are finite; a program needn't handle non-finite values.
Results may differ from a plain program's by a relative error of at most 0.0071.
Values may be sent and summed in bfloat16 or wider, within the bound.
No kernel may reach another device: no remote copies, remote signals or barrier semaphores. Data moves between devices by JAX's collectives and lax.ppermute only.
A program may use at most 192 MiB of HBM per device.

v0:
```python
import jax
import jax.numpy as jnp
from jax import lax
from jax.sharding import PartitionSpec as P

HEADS = 32
HEADDIM = 64
NSTATE = 128
CONV_WIDTH = 4
BLOCK = 128
INNER = 2048
CONVDIM = 2304


epsilon = 1e-05
highest = lax.Precision.HIGHEST


def rms_scale(values, gain):
    return values * lax.rsqrt(jnp.mean(values * values, axis=-1, keepdims=True) + epsilon) * gain


def segment_ids(seq_lengths, length_rows):
    seq_ends = jnp.cumsum(seq_lengths)
    places = jnp.arange(length_rows, dtype=jnp.int32)
    return jnp.sum((places[:, None] >= seq_ends[None, :]).astype(jnp.int32), axis=1)


def causal_conv(signal, segment, kernel_taps, kernel_bias):
    summed = kernel_bias[None, :] + signal * kernel_taps[:, CONV_WIDTH - 1][None, :]
    for offset in range(1, CONV_WIDTH):
        shifted = jnp.concatenate(
            [jnp.zeros((offset, signal.shape[1]), signal.dtype), signal[:-offset]], axis=0
        )
        earlier = jnp.concatenate([jnp.full((offset,), -1, jnp.int32), segment[:-offset]])
        joined = (earlier == segment).astype(signal.dtype)
        summed = (
            summed + shifted * joined[:, None] * kernel_taps[:, CONV_WIDTH - 1 - offset][None, :]
        )
    return summed


def block_step(carry, pieces):
    memory, prior_segment = carry
    head_input, write_map, read_map, step_size, log_decay, segment = pieces
    block_rows = read_map.shape[0]
    running = jnp.cumsum(log_decay, axis=0)
    head_major = running.T
    places = jnp.arange(block_rows, dtype=jnp.int32)
    linked = (segment[:, None] == segment[None, :]) & (places[:, None] >= places[None, :])
    spread = head_major[:, :, None] - head_major[:, None, :]
    decays = jnp.exp(jnp.where(linked[None], spread, -1e30))
    scores = jnp.dot(read_map, write_map.T, precision=highest)
    mixing = decays * scores[None] * step_size.T[:, None, :]
    within = jnp.einsum("hij,jhp->ihp", mixing, head_input, precision=highest)
    joined = (segment == prior_segment).astype(read_map.dtype)
    carried = jnp.einsum("in,hpn->ihp", read_map, memory, precision=highest)
    carried = carried * (jnp.exp(running) * joined[:, None])[:, :, None]
    last_segment = segment[block_rows - 1]
    toward_end = jnp.exp(running[block_rows - 1][None, :] - running)
    toward_end = toward_end * (segment == last_segment).astype(read_map.dtype)[:, None] * step_size
    weighted = head_input * toward_end[:, :, None]
    fresh_state = jnp.einsum("jn,jhp->hpn", write_map, weighted, precision=highest)
    passed = (
        memory
        * jnp.where(last_segment == prior_segment, jnp.exp(running[block_rows - 1]), 0.0)[
            :, None, None
        ]
    )
    return ((passed + fresh_state, last_segment), within + carried)


def state_space(head_input, write_map, read_map, step_size, log_decay, segment):
    token_rows = read_map.shape[0]
    block_count = token_rows // BLOCK
    pieces = (
        head_input.reshape(block_count, BLOCK, HEADS, HEADDIM),
        write_map.reshape(block_count, BLOCK, NSTATE),
        read_map.reshape(block_count, BLOCK, NSTATE),
        step_size.reshape(block_count, BLOCK, HEADS),
        log_decay.reshape(block_count, BLOCK, HEADS),
        segment.reshape(block_count, BLOCK),
    )
    initial = (jnp.zeros((HEADS, HEADDIM, NSTATE), read_map.dtype), jnp.array(-1, jnp.int32))
    unused, results = lax.scan(jax.checkpoint(block_step), initial, pieces)
    return results.reshape(token_rows, HEADS, HEADDIM)


def mixer_block(
    projected, segment, kernel_taps, kernel_bias, step_offset, decay_rates, skip_terms, gate_scale
):
    gate_part = projected[:, :INNER]
    signal = projected[:, INNER : INNER + CONVDIM]
    step_raw = projected[:, INNER + CONVDIM :]
    activated = jax.nn.silu(causal_conv(signal, segment, kernel_taps, kernel_bias))
    head_input = activated[:, :INNER].reshape(-1, HEADS, HEADDIM)
    write_map = activated[:, INNER : INNER + NSTATE]
    read_map = activated[:, INNER + NSTATE :]
    step_size = jax.nn.softplus(step_raw + step_offset[None, :])
    log_decay = -step_size * jnp.exp(decay_rates)[None, :]
    heads_out = state_space(head_input, write_map, read_map, step_size, log_decay, segment)
    heads_out = heads_out + skip_terms[None, :, None] * head_input
    gated_in = heads_out.reshape(-1, INNER) * jax.nn.silu(gate_part)
    return rms_scale(gated_in, gate_scale)


def shards(
    tokens,
    lengths,
    norm_gain,
    in_weight,
    conv_weight,
    conv_bias,
    step_bias,
    decay_log,
    skip_gain,
    gate_gain,
    out_weight,
    cotangent,
):
    token_rows = tokens.shape[0]
    segment = segment_ids(lengths[0], token_rows)
    live = (segment < lengths.shape[1]).astype(jnp.float32)
    front_set = (
        lax.all_gather(norm_gain, "shard", axis=0, tiled=True),
        lax.all_gather(in_weight, "shard", axis=0, tiled=True),
        lax.all_gather(conv_weight, "shard", axis=0, tiled=True),
        lax.all_gather(conv_bias, "shard", axis=0, tiled=True),
        lax.all_gather(step_bias, "shard", axis=0, tiled=True),
        lax.all_gather(decay_log, "shard", axis=0, tiled=True),
        lax.all_gather(skip_gain, "shard", axis=0, tiled=True),
        lax.all_gather(gate_gain, "shard", axis=0, tiled=True),
    )
    whole_in = front_set[1]
    norm_scale = front_set[0].astype(jnp.float32)
    small_params = (
        front_set[2].astype(jnp.float32),
        front_set[3].astype(jnp.float32),
        front_set[4].astype(jnp.float32),
        front_set[5].astype(jnp.float32),
        front_set[6].astype(jnp.float32),
        front_set[7].astype(jnp.float32),
    )
    inputs = tokens.astype(jnp.float32)
    normed, norm_back = jax.vjp(rms_scale, inputs, norm_scale)
    normed_low = normed.astype(jnp.bfloat16)
    projected = jnp.dot(normed_low, whole_in, preferred_element_type=jnp.float32)

    def local_mixer(
        projected, kernel_taps, kernel_bias, step_offset, decay_rates, skip_terms, gate_scale
    ):
        return mixer_block(
            projected,
            segment,
            kernel_taps,
            kernel_bias,
            step_offset,
            decay_rates,
            skip_terms,
            gate_scale,
        )

    gated_out, mixer_back = jax.vjp(local_mixer, projected, *small_params)
    gated_low = gated_out.astype(jnp.bfloat16)
    whole_out = lax.all_gather(out_weight, "shard", axis=0, tiled=True)
    branch = jnp.dot(gated_low, whole_out, preferred_element_type=jnp.float32)
    output = (inputs + live[:, None] * branch).astype(jnp.bfloat16)
    upstream = cotangent * live[:, None].astype(jnp.bfloat16)
    out_share = lax.psum_scatter(
        lax.dot_general(
            gated_low, upstream, (((0,), (0,)), ((), ())), preferred_element_type=jnp.float32
        ),
        "shard",
        scatter_dimension=0,
        tiled=True,
    )
    gated_grad = lax.dot_general(
        upstream, whole_out, (((1,), (1,)), ((), ())), preferred_element_type=jnp.float32
    )
    mixer_grads = mixer_back(gated_grad)
    proj_grad = mixer_grads[0].astype(jnp.bfloat16)
    in_local = lax.dot_general(
        normed_low, proj_grad, (((0,), (0,)), ((), ())), preferred_element_type=jnp.float32
    )
    normed_grad = lax.dot_general(
        proj_grad, whole_in, (((1,), (1,)), ((), ())), preferred_element_type=jnp.float32
    )
    input_part, gain_local = norm_back(normed_grad)
    input_grad = cotangent.astype(jnp.float32) + input_part
    shares = (
        lax.psum_scatter(gain_local, "shard", scatter_dimension=0, tiled=True),
        lax.psum_scatter(in_local, "shard", scatter_dimension=0, tiled=True),
        lax.psum_scatter(mixer_grads[1], "shard", scatter_dimension=0, tiled=True),
        lax.psum_scatter(mixer_grads[2], "shard", scatter_dimension=0, tiled=True),
        lax.psum_scatter(mixer_grads[3], "shard", scatter_dimension=0, tiled=True),
        lax.psum_scatter(mixer_grads[4], "shard", scatter_dimension=0, tiled=True),
        lax.psum_scatter(mixer_grads[5], "shard", scatter_dimension=0, tiled=True),
        lax.psum_scatter(mixer_grads[6], "shard", scatter_dimension=0, tiled=True),
    )
    summed = lax.psum(
        (
            shares[0],
            shares[1],
            shares[2],
            shares[3],
            shares[4],
            shares[5],
            shares[6],
            shares[7],
            out_share,
        ),
        "rep",
    )
    out_final = summed[8]
    return (
        output,
        input_grad,
        summed[0],
        summed[1],
        summed[2],
        summed[3],
        summed[4],
        summed[5],
        summed[6],
        summed[7],
        out_final,
    )


def solution(mesh):
    in_specs = (
        P(("rep", "shard"), None),
        P(("rep", "shard"), None),
        P("shard"),
        P("shard", None),
        P("shard", None),
        P("shard"),
        P("shard"),
        P("shard"),
        P("shard"),
        P("shard"),
        P("shard", None),
        P(("rep", "shard"), None),
    )
    out_specs = (
        P(("rep", "shard"), None),
        P(("rep", "shard"), None),
        P("shard"),
        P("shard", None),
        P("shard", None),
        P("shard"),
        P("shard"),
        P("shard"),
        P("shard"),
        P("shard"),
        P("shard", None),
    )
    return jax.shard_map(shards, mesh=mesh, in_specs=in_specs, out_specs=out_specs, check_vma=False)
```

profile of v0, /device:TPU:0, one launch (start us, length us, event | category | flops | bytes accessed | tf_op | source)
XLA Modules:
  0.0 808.2 jit_solution(3238989988094217540)
XLA Ops:
  27.2 6.5 all-gather.5.cloned.1.call-done
  33.7 6.4 fusion.112
  42.6 5.3 fusion.90
  58.9 94.1 %while.45 = (s32[]{:T(128)}, f32[32,64,128]{2,1,0:T(8,128)S(1)}, s32[]{:T(128)}, f32[2,128,32,64]{1,0,3,2:T(2,128)}, f32[2,32,64,128]{3,2,1,0:T(8,128)}, /*index...) while((s32[]{:T(128)}, f32[32,64,128]{2,1,0:T(8,128)S(1)}, ...), condition=%wide.region_5.6_spmd.clone, body=%wide.region_3.5_spmd.clone.sunk | while | flops 1237905920 | bytes 30171580 | solution.py:85
  70.1 5.0 fusion.197
  76.1 24.9 %dynamic_update_slice.86 = f32[2,128,32,64]{1,0,3,2:T(2,128)} dynamic-update-slice(f32[2,128,32,64]{1,0,3,2:T(2,128)} %get-tuple-element.1083, f32[1,128,32,64]{1,0,3,2:T(1,128)S(1)} %bitcast.297, s32[]{:T(128)S(6)} %copy.285, s32[]{:T(128)} %constant.142.clone.1..sunk, s32[]{:T(128)} %constant.142.clone.1..sunk, s32[]{:T(128)} %constant.142.clone.1..sunk) | dynamic-update-slice | bytes 2097156 | tf_op jit(solution)/shard_map/jvp()/while/body/jit(dynamic_update_index_in_dim)/dynamic_update_slice | solution.py:85
  117.2 5.0 fusion.197
  123.2 24.9 %dynamic_update_slice.86 = f32[2,128,32,64]{1,0,3,2:T(2,128)} dynamic-update-slice(f32[2,128,32,64]{1,0,3,2:T(2,128)} %get-tuple-element.1083, f32[1,128,32,64]{1,0,3,2:T(1,128)S(1)} %bitcast.297, s32[]{:T(128)S(6)} %copy.285, s32[]{:T(128)} %constant.142.clone.1..sunk, s32[]{:T(128)} %constant.142.clone.1..sunk, s32[]{:T(128)} %constant.142.clone.1..sunk) | dynamic-update-slice | bytes 2097156 | tf_op jit(solution)/shard_map/jvp()/while/body/jit(dynamic_update_index_in_dim)/dynamic_update_slice | solution.py:85
  153.1 3.3 multiply_reduce_fusion.11
  157.8 4.7 fusion.103
  162.5 6.3 multiply_reduce_fusion.8
  169.5 6.7 multiply_reduce_fusion.9
  176.3 3.3 reshape.476
  184.4 153.9 %while.46 = (s32[]{:T(128)}, f32[32,64,128]{2,1,0:T(8,128)}, f32[2,128,32,64]{1,0,3,2:T(2,128)}, f32[2,128,128]{2,1,0:T(8,128)}, f32[2,128,128]{2,1,0:T(8,128)},...) while((s32[]{:T(128)}, f32[32,64,128]{2,1,0:T(8,128)}, ...), condition=%wide.region_19.20_spmd.clone, body=%wide.region_8.19_spmd.clone.sunk | while | flops 2907832832 | bytes 77721384 | solution.py:85
  214.7 6.2 fusion.220
  226.6 3.0 convolution_bitcast_fusion.4
  229.7 4.1 fusion.225
  242.1 24.9 %dynamic_update_slice.91 = f32[2,128,32,64]{1,0,3,2:T(2,128)} dynamic-update-slice(f32[2,128,32,64]{1,0,3,2:T(2,128)} %get-tuple-element.1131, f32[1,128,32,64]{1,0,3,2:T(1,128)} %bitcast.298, s32[]{:T(128)S(6)} %sub.234, s32[]{:T(128)} %constant.142.clone.1..sunk.1, s32[]{:T(128)} %constant.142.clone.1..sunk.1, s32[]{:T(128)} %constant.142.clone.1..sunk.1) | dynamic-update-slice | bytes 2097156 | tf_op jit(solution)/shard_map/transpose(jvp())/while/body/jit(dynamic_update_index_in_dim)/dynamic_update_slice | solution.py:85
  285.9 6.2 fusion.220
  297.7 3.0 convolution_bitcast_fusion.4
  300.8 4.1 fusion.225
  313.2 24.9 %dynamic_update_slice.91 = f32[2,128,32,64]{1,0,3,2:T(2,128)} dynamic-update-slice(f32[2,128,32,64]{1,0,3,2:T(2,128)} %get-tuple-element.1131, f32[1,128,32,64]{1,0,3,2:T(1,128)} %bitcast.298, s32[]{:T(128)S(6)} %sub.234, s32[]{:T(128)} %constant.142.clone.1..sunk.1, s32[]{:T(128)} %constant.142.clone.1..sunk.1, s32[]{:T(128)} %constant.142.clone.1..sunk.1) | dynamic-update-slice | bytes 2097156 | tf_op jit(solution)/shard_map/transpose(jvp())/while/body/jit(dynamic_update_index_in_dim)/dynamic_update_slice | solution.py:85
  342.6 2.7 bitcast_add_fusion.2
  346.2 6.6 fusion.122
  357.6 8.8 %fusion.110 = f32[1024,4384]{0,1:T(8,128)} fusion(bf16[256,1024]{1,0:T(8,128)(2,1)S(1)} %copy-done.20, f32[1024]{0:T(1024)S(1)} %bitcast.318, f32[256]{0:T(256)S(1)} %copy-done.66, f32[256,2048]{0,1:T(8,128)S(1)} %copy-done.18, f32[256,2304]{0,1:T(8,128)S(1)} %multiply_add_fusion, f32[256,32]{0,1:T(8,128)S(1)} %get-tuple-element.800), kind=kOutput, calls=%fused_computation.182 | convolution fusion | flops 2302894080 | bytes 22975488 | tf_op jit(solution)/shard_map/dot_general | solution.py:182
  368.1 26.9 %reduce-scatter.6.cloned.1.call-done = f32[512,4384]{0,1:T(8,128)} async-done(((f32[1024,4384]{0,1:T(8,128)}), f32[512,4384]{0,1:T(8,128)}) %reduce-scatter.6.cloned.1.call-update) | async-done | bytes 8978448 | tf_op jit(solution)/shard_map/reduce_scatter | solution.py:192
  397.8 7.9 fusion.98
  405.8 4.0 all-reduce.31
  412.7 4.4 fusion.94
  418.3 82.3 %all-reduce.29 = (f32[512]{0:T(512)}, f32[1152,4]{0,1:T(4,128)}, f32[1152]{0:T(1024)}, f32[16]{0:T(128)}, f32[16]{0:T(128)}, /*index=5*/f32[16]{0:T(128)}, f32[1024]{0:T(1024)}) all-reduce(f32[512]{0:T(512)S(1)} %dynamic-slice.4, f32[1152,4]{0,1:T(4,128)S(1)} %copy.193, ...), channel_id=1, replica_groups=mesh['rep'=16,'shard'=2] {'rep'}, use_global_device_ids=true, to_apply=%region_23.24 | all-reduce | flops 7344 | bytes 58752 | tf_op jit(solution)/shard_map/psum | solution.py:200
  500.7 289.8 %all-reduce.35.cloned.1.call-done = (f32[512,4384]{0,1:T(8,128)}, f32[1024,1024]{1,0:T(8,128)}) async-done(((f32[512,4384]{0,1:T(8,128)}, f32[1024,1024]{1,0:T(8,128)}), (f32[512,4384]{0,1:T(8,128)}, f32[1024,1024]{1,0:T(8,128)})) %all-reduce.35.cloned.1.call-update) | async-done | bytes 13172752 | tf_op jit(solution)/shard_map/psum | solution.py:200
  790.5 8.4 %copy.325 = f32[512,4384]{0,1:T(8,128)} copy(f32[512,4384]{0,1:T(8,128)} %get-tuple-element.1170) | data formatting | bytes 17956864
  (432 shorter events, 150.2 us)
Async XLA Ops:
  7.2 26.5 %all-gather.5.cloned.1.call-start = ((), (), s32[]{:S(2)}) async-start(), calls=%async_computation.3 | async-start | bytes 13467648 | tf_op jit(solution)/shard_map/all_gather | solution.py:126
  8.0 8.9 %copy-start.76 = (bf16[1024]{0:T(1024)(128)(2,1)S(1)}, bf16[1024]{0:T(1024)(128)(2,1)}, u32[]{:S(2)}) copy-start(bf16[1024]{0:T(1024)(128)(2,1)} %param.25) | copy-start | bytes 6148
  8.0 11.3 %copy-start.74 = (bf16[1152]{0:T(1024)(128)(2,1)S(1)}, bf16[1152]{0:T(1024)(128)(2,1)}, u32[]{:S(2)}) copy-start(bf16[1152]{0:T(1024)(128)(2,1)} %param.21) | copy-start | bytes 6916
  8.0 17.2 %copy-start.69 = (bf16[1152,4]{0,1:T(4,128)(2,1)S(1)}, bf16[1152,4]{0,1:T(4,128)(2,1)}, u32[]{:S(2)}) copy-start(bf16[1152,4]{0,1:T(4,128)(2,1)} %param.20) | copy-start | bytes 27652
  8.0 154.5 %all-gather.7.cloned.1.call-start = ((), (), s32[]{:S(2)}) async-start(), calls=%async_computation.4 | async-start | bytes 6291456 | tf_op jit(solution)/shard_map/all_gather | solution.py:165
  8.8 359.3 %reduce-scatter.8.cloned.1.call-start = ((), (), s32[]{:S(2)}) async-start(), calls=%async_computation.6 | async-start | bytes 12582912 | tf_op jit(solution)/shard_map/reduce_scatter | solution.py:169
  14.3 34.5 %copy-start.78 = (f32[32]{0:T(128)}, f32[32]{0:T(128)S(1)}, u32[]{:S(2)}) copy-start(f32[32]{0:T(128)S(1)} %convert_element_type.114) | copy-start | bytes 388
  14.3 34.5 %copy-start.79 = (f32[32]{0:T(128)}, f32[32]{0:T(128)S(1)}, u32[]{:S(2)}) copy-start(f32[32]{0:T(128)S(1)} %convert_exponential_fusion) | copy-start | bytes 388
  15.0 25.0 %copy-start.65 = (f32[256]{0:T(256)}, f32[256]{0:T(256)S(1)}, u32[]{:S(2)}) copy-start(f32[256]{0:T(256)S(1)} %fusion.117) | copy-start | bytes 3076
  16.9 23.2 %copy-start.52 = (f32[2,1,512]{2,1,0:T(1,128)}, f32[2,1,512]{2,1,0:T(1,128)S(1)}, u32[]{:S(2)}) copy-start(f32[2,1,512]{2,1,0:T(1,128)S(1)} %convert_element_type.128) | copy-start | bytes 12292
  22.5 18.1 %copy-start.55 = (f32[256]{0:T(256)}, f32[256]{0:T(256)S(1)}, u32[]{:S(2)}) copy-start(f32[256]{0:T(256)S(1)} %get-tuple-element.827) | copy-start | bytes 3076
  22.5 18.1 %copy-start.57 = (f32[256]{0:T(256)}, f32[256]{0:T(256)S(1)}, u32[]{:S(2)}) copy-start(f32[256]{0:T(256)S(1)} %get-tuple-element.828) | copy-start | bytes 3076
  22.5 18.1 %copy-start.59 = (f32[256]{0:T(256)}, f32[256]{0:T(256)S(1)}, u32[]{:S(2)}) copy-start(f32[256]{0:T(256)S(1)} %get-tuple-element.829) | copy-start | bytes 3076
  27.2 13.5 %copy-start.44 = (f32[2304]{0:T(1024)}, f32[2304]{0:T(1024)S(1)}, u32[]{:S(2)}) copy-start(f32[2304]{0:T(1024)S(1)} %get-tuple-element.717) | copy-start | bytes 27652
  27.2 13.5 %copy-start.46 = (f32[2304]{0:T(1024)}, f32[2304]{0:T(1024)S(1)}, u32[]{:S(2)}) copy-start(f32[2304]{0:T(1024)S(1)} %get-tuple-element.718) | copy-start | bytes 27652
  27.2 13.5 %copy-start.48 = (f32[2304]{0:T(1024)}, f32[2304]{0:T(1024)S(1)}, u32[]{:S(2)}) copy-start(f32[2304]{0:T(1024)S(1)} %get-tuple-element.719) | copy-start | bytes 27652
  27.2 13.5 %copy-start.50 = (f32[2304]{0:T(1024)}, f32[2304]{0:T(1024)S(1)}, u32[]{:S(2)}) copy-start(f32[2304]{0:T(1024)S(1)} %get-tuple-element.720) | copy-start | bytes 27652
  40.1 8.7 %copy-start.5 = (f32[256,4384]{0,1:T(8,128)}, f32[256,4384]{0,1:T(8,128)S(1)}, u32[]{:S(2)}) copy-start(f32[256,4384]{0,1:T(8,128)S(1)} %fusion.112) | copy-start | bytes 13467652
  58.9 11.2 %copy-start.1 = (f32[2,128,32,64]{1,3,2,0:T(8,128)}, f32[2,128,32,64]{1,3,2,0:T(8,128)S(1)}, u32[]{:S(2)}) copy-start(f32[2,128,32,64]{1,3,2,0:T(8,128)S(1)} %get-tuple-element.1103) | copy-start | bytes 6291460 | tf_op jit(solution)/shard_map/jvp()/while
  76.1 25.9 %copy-start.64 = (f32[32]{0:T(128)S(1)}, f32[32]{0:T(128)}, u32[]{:S(2)}) copy-start(f32[32]{0:T(128)} %broadcast_select_fusion.7) | copy-start | bytes 388 | tf_op jit(solution)/shard_map/jvp()/while
  106.0 11.2 %copy-start.1 = (f32[2,128,32,64]{1,3,2,0:T(8,128)}, f32[2,128,32,64]{1,3,2,0:T(8,128)S(1)}, u32[]{:S(2)}) copy-start(f32[2,128,32,64]{1,3,2,0:T(8,128)S(1)} %get-tuple-element.1103) | copy-start | bytes 6291460 | tf_op jit(solution)/shard_map/jvp()/while
  123.2 26.0 %copy-start.64 = (f32[32]{0:T(128)S(1)}, f32[32]{0:T(128)}, u32[]{:S(2)}) copy-start(f32[32]{0:T(128)} %broadcast_select_fusion.7) | copy-start | bytes 388 | tf_op jit(solution)/shard_map/jvp()/while
  156.5 12.5 %copy-start.61 = (f32[256]{0:T(256)}, f32[256]{0:T(256)S(1)}, u32[]{:S(2)}) copy-start(f32[256]{0:T(256)S(1)} %fusion.118) | copy-start | bytes 3076
  168.9 226.1 %reduce-scatter.6.cloned.1.call-start = ((), (), s32[]{:S(2)}) async-start(), calls=%async_computation.5 | async-start | bytes 26935296 | tf_op jit(solution)/shard_map/reduce_scatter | solution.py:192
  237.6 29.4 %copy-start.4 = (f32[2,128,32,64]{1,3,2,0:T(8,128)S(1)}, f32[2,128,32,64]{1,3,2,0:T(8,128)}, u32[]{:S(2)}) copy-start(f32[2,128,32,64]{1,3,2,0:T(8,128)} %copy-done.3) | copy-start | bytes 6291460 | tf_op jit(solution)/shard_map/transpose(jvp())/while
  308.8 29.4 %copy-start.4 = (f32[2,128,32,64]{1,3,2,0:T(8,128)S(1)}, f32[2,128,32,64]{1,3,2,0:T(8,128)}, u32[]{:S(2)}) copy-start(f32[2,128,32,64]{1,3,2,0:T(8,128)} %copy-done.3) | copy-start | bytes 6291460 | tf_op jit(solution)/shard_map/transpose(jvp())/while
  366.4 50.7 %reduce-scatter.10.cloned.1.call-start = ((), (), s32[]{:S(2)}) async-start(), calls=%async_computation.7 | async-start | bytes 1769472
  368.0 422.5 %all-reduce.35.cloned.1.call-start = ((), (), s32[]{:S(2)}) async-start(), calls=%async_computation.8 | async-start | bytes 26345472 | tf_op jit(solution)/shard_map/psum | solution.py:200
  397.8 8.0 copy-start.70
  397.8 12.4 %copy-start.68 = (f32[256]{0:T(256)S(1)}, f32[256]{0:T(256)}, u32[]{:S(2)}) copy-start(f32[256]{0:T(256)} %copy-done.67) | copy-start | bytes 3076
  397.8 12.4 %copy-start.24 = (bf16[256,1024]{1,0:T(8,128)(2,1)S(1)}, bf16[256,1024]{1,0:T(8,128)(2,1)}, u32[]{:S(2)}) copy-start(bf16[256,1024]{1,0:T(8,128)(2,1)} %param.27) | copy-start | bytes 1572868
  790.5 8.4 %copy-start.21 = (f32[1024,1024]{1,0:T(8,128)S(1)}, f32[1024,1024]{1,0:T(8,128)}, u32[]{:S(2)}) copy-start(f32[1024,1024]{1,0:T(8,128)} %get-tuple-element.1177) | copy-start | bytes 12582916
  (88 other events, 303.6 us)
Sparse Core Ops, SparseCore 0:
  9.6 24.0 all-gather.4
  35.2 14.8 all-gather.6
  169.0 17.9 reduce-scatter.7
  366.5 28.4 reduce-scatter.5
  397.7 10.0 reduce-scatter.9
  414.0 376.3 all-reduce.34
where the time goes:
time: 821 us; the launch traced here: 808 us
  waiting for transfers between devices  325 us (40%)
  local copies, waits for them, and re-layouts  187 us (23%)
  matrix products  99.3 us (12%)
  blocking collectives  96.1 us (12%)
  other arithmetic  63.1 us (8%)
  between operations  18.7 us (2%)
  loops' own time  18.5 us (2%)
    psum x1, waiting for transfers between devices, shards(): lax.psum((shares[0], shares[1], shares[2], shares[3], shares[4], shares[5...  290 us
    dynamic_update_slice x10, local copies, waits for them, and re-layouts, state_space(): unused, results = lax.scan(jax.checkpoint(block_step), initial, pieces)  106 us
    psum x1, blocking collectives, shards(): lax.psum((shares[0], shares[1], shares[2], shares[3], shares[4], shares[5...  82.3 us
    dot_general x6, matrix products, block_step(): within = jnp.einsum('hij,jhp->ihp', mixing, head_input, precision=highest)  30.7 us
    reduce_scatter x1, waiting for transfers between devices, shards(): lax.psum_scatter(in_local, 'shard', scatter_dimension=0, tiled=True)  26.9 us
    unnamed x147, local copies, waits for them, and re-layouts  26.2 us
    another operation x2, loops' own time, state_space(): unused, results = lax.scan(jax.checkpoint(block_step), initial, pieces)  18.5 us
  transfers between devices with their start and end apart: 6, of which 3 were waited for; matrix products, arithmetic and copies ran while one was open for 40% of the time, Pallas kernels for 0%

commit v1 on v0

v1 whole, which is shorter than its diff:
```python
import jax
import jax.numpy as jnp
from jax import lax
from jax.experimental import pallas as pl
from jax.experimental.pallas import tpu as pltpu
from jax.sharding import PartitionSpec as P

HEADS = 32
HEADDIM = 64
NSTATE = 128
CONV_WIDTH = 4
BLOCK = 128
INNER = 2048
CONVDIM = 2304
STEP_COL = INNER + CONVDIM

GROUP = 4
WIDE = GROUP * HEADDIM
STEPS = HEADS // GROUP
LANES = 128

epsilon = 1e-05
highest = lax.Precision.HIGHEST
f32 = jnp.float32
bf16 = jnp.bfloat16


def mm(left, right, dims=((1,), (0,)), precision=None):
    return lax.dot_general(left, right, (dims, ((), ())), precision=precision, preferred_element_type=f32)


LANE = ((1,), (1,))
ROWS = ((0,), (0,))


def segment_of(places, len_ref):
    end = len_ref[0, 0]
    segment = (places >= end).astype(jnp.int32)
    for slot in range(1, len_ref.shape[1]):
        end = end + len_ref[0, slot]
        segment = segment + (places >= end).astype(jnp.int32)
    return segment


def write_joined(len_ref, joined_ref):
    rows, lanes = joined_ref.shape[1:]
    places = lax.broadcasted_iota(jnp.int32, (rows, lanes), 0)
    segment = segment_of(places, len_ref)
    for offset in range(1, CONV_WIDTH):
        same = (segment_of(places - offset, len_ref) == segment) & (places >= offset)
        joined_ref[offset - 1] = same.astype(f32)


def wide(mask):
    return jnp.concatenate([mask, mask], axis=1)


def linked(len_ref, row_start, col_start):
    rows = lax.broadcasted_iota(jnp.int32, (BLOCK, BLOCK), 0) + row_start
    cols = lax.broadcasted_iota(jnp.int32, (BLOCK, BLOCK), 1) + col_start
    return (segment_of(rows, len_ref) == segment_of(cols, len_ref)) & (rows >= cols)


def step_terms(raw_ref, head_ref):
    lane = lax.broadcasted_iota(jnp.int32, raw_ref.shape, 1)
    shifted = jnp.where(lane < HEADS, raw_ref[...] + head_ref[0:1, :], 0.0)
    step = jnp.maximum(shifted, 0.0) + jnp.log1p(jnp.exp(-jnp.abs(shifted)))
    rate = jnp.exp(head_ref[1:2, :])
    return shifted, step, rate, -step * rate


def lower():
    rows = lax.broadcasted_iota(jnp.int32, (BLOCK, BLOCK), 0)
    cols = lax.broadcasted_iota(jnp.int32, (BLOCK, BLOCK), 1)
    return (rows >= cols).astype(f32)


def write_running(raw_ref, head_ref, step_ref, run_ref, runt_ref):
    unused, step, rate, decay = step_terms(raw_ref, head_ref)
    step_ref[...] = step
    for block in range(2):
        rows = slice(block * BLOCK, (block + 1) * BLOCK)
        running = mm(lower(), decay[rows], precision=highest)
        run_ref[rows, :] = running
        turned = running.T
        for group in range(STEPS):
            runt_ref[group, 0:GROUP, rows] = turned[group * GROUP : (group + 1) * GROUP]


def conv_silu(signal, par, joined_ref):
    summed = par[4:5] + signal * par[3:4]
    for offset in range(1, CONV_WIDTH):
        tap = par[3 - offset : 4 - offset]
        summed = summed + pltpu.roll(signal, offset, 0) * wide(joined_ref[offset - 1]) * tap
    return summed


def conv_back(grad, signal, par, joined_ref, store):
    rows = grad.shape[0]
    back = grad * par[3:4]
    store(3, jnp.sum(grad * signal, axis=0, keepdims=True))
    store(4, jnp.sum(grad, axis=0, keepdims=True))
    for offset in range(1, CONV_WIDTH):
        masked = grad * wide(joined_ref[offset - 1])
        store(3 - offset, jnp.sum(masked * pltpu.roll(signal, offset, 0), axis=0, keepdims=True))
        back = back + pltpu.roll(masked, rows - offset, 0) * par[3 - offset : 4 - offset]
    return back


def logistic(value):
    return 1.0 / (1.0 + jnp.exp(-value))


def head_columns(table, step):
    return pltpu.roll(table, lax.rem(LANES - GROUP * step, LANES), 1)


def spread(columns, head):
    return jnp.broadcast_to(columns[:, head : head + 1], (columns.shape[0], LANES))


def half_lanes(shape):
    return lax.broadcasted_iota(jnp.int32, shape, 1) < HEADDIM


def decay_pair(pair, block, runs, runt_ref, step):
    rows = slice(block * BLOCK, (block + 1) * BLOCK)
    out = []
    for place in (2 * pair, 2 * pair + 1):
        row = runt_ref[step, place : place + 1, rows]
        out.append(jnp.exp(jnp.minimum(runs[place][rows] - row, 0.0)))
    return out


def split_heads(value):
    first = half_lanes(value.shape)
    zero = jnp.zeros_like(value)
    return jnp.concatenate([jnp.where(first, value, zero), jnp.where(first, zero, value)], axis=0)


def pair_terms(pair, runs, steps):
    first = half_lanes(runs[0].shape)
    run = jnp.where(first, runs[2 * pair], runs[2 * pair + 1])
    step = jnp.where(first, steps[2 * pair], steps[2 * pair + 1])
    into = jnp.exp(run[BLOCK:])
    toward = jnp.exp(run[BLOCK - 1 : BLOCK] - run[:BLOCK])
    return step, into, toward


def forward_kernel(
    len_ref, raw_ref, head_ref, sig_ref, bc_ref, gate_ref, grad_ref, par_ref, parbc_ref, gain_ref,
    gated_ref, dgate_ref, dheads_ref, heads_ref, conv_ref, convbc_ref, gaing_ref,
    joined, step_s, run_s, runt_s, score_s, cross_s, u_s, silu_s, slope_s, grad_s, sq_s, mix_s,
):
    step = pl.program_id(0)

    @pl.when(step == 0)
    def prepare():
        write_joined(len_ref, joined)
        write_running(raw_ref, head_ref, step_s, run_s, runt_s)
        summed = conv_silu(bc_ref[...], parbc_ref[...], joined)
        convbc_ref[...] = summed
        active = summed * logistic(summed)
        write_map, read_map = active[:, :NSTATE], active[:, NSTATE:]
        for block in range(2):
            rows = slice(block * BLOCK, (block + 1) * BLOCK)
            scores = mm(read_map[rows], write_map[rows], LANE, highest)
            score_s[block] = jnp.where(linked(len_ref, block * BLOCK, block * BLOCK), scores, 0.0)
        cross = mm(read_map[BLOCK:], write_map[:BLOCK], LANE, highest)
        cross_s[...] = jnp.where(linked(len_ref, BLOCK, 0), cross, 0.0).astype(bf16)
        sq_s[...] = jnp.zeros_like(sq_s)
        mix_s[...] = jnp.zeros_like(mix_s)

    par = par_ref[...]
    summed = conv_silu(sig_ref[...], par, joined)
    conv_ref[...] = summed
    head_in = summed * logistic(summed)
    run_cols = head_columns(run_s[...], step)
    step_cols = head_columns(step_s[...], step)
    runs = [spread(run_cols, head) for head in range(GROUP)]
    steps = [spread(step_cols, head) for head in range(GROUP)]
    tops, bottoms, intos, sources = [], [], [], []
    for pair in range(GROUP // 2):
        lanes = slice(pair * LANES, (pair + 1) * LANES)
        step_size, into, toward = pair_terms(pair, runs, steps)
        scaled = head_in[:, lanes] * step_size
        low = scaled.astype(bf16)
        for block, found in ((0, tops), (1, bottoms)):
            rows = slice(block * BLOCK, (block + 1) * BLOCK)
            first, second = decay_pair(pair, block, runs, runt_s, step)
            mixing = jnp.concatenate([first * score_s[block], second * score_s[block]], axis=1)
            found.append(mm(mixing.astype(bf16), split_heads(low[rows])))
        intos.append(into)
        sources.append((scaled[:BLOCK] * toward).astype(bf16))
    carried = mm(cross_s[...], jnp.concatenate(sources, axis=1)) * jnp.concatenate(intos, axis=1)
    top, bottom = jnp.concatenate(tops, axis=1), jnp.concatenate(bottoms, axis=1)
    heads_ref[:BLOCK] = top
    heads_ref[BLOCK:] = bottom
    heads = jnp.concatenate([top, bottom + carried], axis=0) + par[6:7] * head_in
    gate = gate_ref[...]
    opened = logistic(gate)
    silu = gate * opened
    u = heads * silu
    grad = grad_ref[...]
    mixed = grad * par[5:6] * u
    square = u * u
    sq_s[...] += square[:, :LANES] + square[:, LANES:]
    mix_s[...] += mixed[:, :LANES] + mixed[:, LANES:]
    u_s[step] = u
    silu_s[step] = silu
    slope_s[step] = heads * (opened * (1.0 + gate * (1.0 - opened)))
    grad_s[step] = grad

    @pl.when(step == STEPS - 1)
    def finish():
        scale = lax.rsqrt(jnp.sum(sq_s[...], axis=1, keepdims=True) * (1.0 / INNER) + epsilon)
        drag = scale * scale * scale * (jnp.sum(mix_s[...], axis=1, keepdims=True) * (1.0 / INNER))
        for part in range(STEPS):
            lanes = slice(part * WIDE, (part + 1) * WIDE)
            gain = gain_ref[:, lanes]
            normal = u_s[part] * scale
            grad = grad_s[part]
            gated_ref[:, lanes] = (normal * gain).astype(bf16)
            gaing_ref[:, lanes] = jnp.sum(grad * normal, axis=0, keepdims=True)
            du = scale * (grad * gain) - u_s[part] * drag
            dheads_ref[:, lanes] = du * silu_s[part]
            dgate_ref[:, lanes] = (du * slope_s[part]).astype(bf16)


def backward_kernel(
    len_ref, raw_ref, head_ref, sig_ref, bc_ref, conv_ref, convbc_ref, dheads_ref, heads_ref, par_ref, parbc_ref,
    dx_ref, dr_ref, parg_ref, parbcg_ref, headg_ref,
    joined, step_s, run_s, runt_s, maps_s, score_s, cross_s, dscore_s, dcross_s, dstep_s, ddecay_s,
):
    step = pl.program_id(0)

    @pl.when(step == 0)
    def prepare():
        write_joined(len_ref, joined)
        write_running(raw_ref, head_ref, step_s, run_s, runt_s)
        summed = convbc_ref[...]
        active = summed * logistic(summed)
        maps_s[...] = active
        write_map, read_map = active[:, :NSTATE], active[:, NSTATE:]
        for block in range(2):
            rows = slice(block * BLOCK, (block + 1) * BLOCK)
            scores = mm(read_map[rows], write_map[rows], LANE, highest)
            score_s[block] = jnp.where(linked(len_ref, block * BLOCK, block * BLOCK), scores, 0.0)
        cross = mm(read_map[BLOCK:], write_map[:BLOCK], LANE, highest)
        cross_s[...] = jnp.where(linked(len_ref, BLOCK, 0), cross, 0.0).astype(bf16)
        dscore_s[...] = jnp.zeros_like(dscore_s)
        dcross_s[...] = jnp.zeros_like(dcross_s)
        dstep_s[...] = jnp.zeros_like(dstep_s)
        ddecay_s[...] = jnp.zeros_like(ddecay_s)

    par = par_ref[...]
    summed = conv_ref[...]
    opened = logistic(summed)
    head_in = summed * opened
    slope = opened * (1.0 + summed * (1.0 - opened))
    run_cols = head_columns(run_s[...], step)
    step_cols = head_columns(step_s[...], step)
    runs = [spread(run_cols, head) for head in range(GROUP)]
    steps = [spread(step_cols, head) for head in range(GROUP)]
    dheads = dheads_ref[...]
    dlow = dheads.astype(bf16)
    tops, bottoms, towards, sinks, sources, lows, sizes = [], [], [], [], [], [], []
    for pair in range(GROUP // 2):
        lanes = slice(pair * LANES, (pair + 1) * LANES)
        step_size, into, toward = pair_terms(pair, runs, steps)
        scaled = head_in[:, lanes] * step_size
        low = scaled.astype(bf16)
        for block, found in ((0, tops), (1, bottoms)):
            rows = slice(block * BLOCK, (block + 1) * BLOCK)
            first, second = decay_pair(pair, block, runs, runt_s, step)
            mixing = jnp.concatenate([first * score_s[block], second * score_s[block]], axis=0)
            parted = split_heads(dlow[rows, lanes])
            found.append(mm(mixing.astype(bf16), parted, ROWS))
            dmixing = mm(parted, low[rows], LANE)
            dscore_s[block] += first * dmixing[:BLOCK] + second * dmixing[BLOCK:]
        sinks.append((dheads[BLOCK:, lanes] * into).astype(bf16))
        sources.append((scaled[:BLOCK] * toward).astype(bf16))
        towards.append(toward)
        lows.append(low)
        sizes.append(step_size)
    sink, source = jnp.concatenate(sinks, axis=1), jnp.concatenate(sources, axis=1)
    dcross_s[...] += mm(sink, source, LANE)
    arrived, returned = mm(cross_s[...], source), mm(cross_s[...], sink, ROWS)
    inside = jnp.concatenate([jnp.concatenate(tops, axis=1), jnp.concatenate(bottoms, axis=1)], axis=0)
    dscaled = jnp.concatenate(
        [inside[:BLOCK] + returned * jnp.concatenate(towards, axis=1), inside[BLOCK:]], axis=0
    )
    between = jnp.concatenate([-source.astype(f32) * returned, sink.astype(f32) * arrived], axis=0)
    owner = lax.broadcasted_iota(jnp.int32, (WIDE, LANES), 0) // HEADDIM + GROUP * step
    sums = (owner == lax.broadcasted_iota(jnp.int32, (WIDE, LANES), 1)).astype(f32)
    low = jnp.concatenate(lows, axis=1).astype(f32)
    moved = dlow.astype(f32) * heads_ref[...] - low * inside + between
    ddecay_s[...] += mm(moved, sums, precision=highest)
    dstep_s[...] += mm(head_in * dscaled, sums, precision=highest)
    dhead_in = jnp.concatenate(sizes, axis=1) * dscaled + par[6:7] * dheads

    def store(row, value):
        parg_ref[row : row + 1, :] = value

    store(5, jnp.zeros((1, WIDE), f32))
    store(6, jnp.sum(dheads * head_in, axis=0, keepdims=True))
    store(7, jnp.zeros((1, WIDE), f32))
    dx_ref[...] = conv_back(dhead_in * slope, sig_ref[...], par, joined, store).astype(bf16)

    @pl.when(step == STEPS - 1)
    def finish():
        maps = maps_s[...]
        write_map, read_map = maps[:, :NSTATE], maps[:, NSTATE:]
        w0, w1, r0, r1 = write_map[:BLOCK], write_map[BLOCK:], read_map[:BLOCK], read_map[BLOCK:]
        d0 = jnp.where(linked(len_ref, 0, 0), dscore_s[0], 0.0)
        d1 = jnp.where(linked(len_ref, BLOCK, BLOCK), dscore_s[1], 0.0)
        dc = jnp.where(linked(len_ref, BLOCK, 0), dcross_s[...], 0.0)
        dread = jnp.concatenate(
            [mm(d0, w0, precision=highest), mm(d1, w1, precision=highest) + mm(dc, w0, precision=highest)], axis=0
        )
        dwrite = jnp.concatenate(
            [mm(d0, r0, ROWS, highest) + mm(dc, r1, ROWS, highest), mm(d1, r1, ROWS, highest)], axis=0
        )
        summed = convbc_ref[...]
        opened = logistic(summed)
        slope = opened * (1.0 + summed * (1.0 - opened))

        def store(row, value):
            parbcg_ref[row : row + 1, :] = value

        for row in (5, 6, 7):
            store(row, jnp.zeros((1, WIDE), f32))
        grad = jnp.concatenate([dwrite, dread], axis=1) * slope
        dr_ref[:, :WIDE] = conv_back(grad, bc_ref[...], parbc_ref[...], joined, store).astype(bf16)

        shifted, step_size, rate, decay = step_terms(raw_ref, head_ref)
        change = ddecay_s[...]
        late = mm(lower(), change[BLOCK:], ROWS, highest)
        early = mm(lower(), change[:BLOCK], ROWS, highest) + late[0:1]
        ddecay = jnp.concatenate([early, late], axis=0)
        dshifted = (dstep_s[...] - rate * ddecay) * logistic(shifted)
        lane = lax.broadcasted_iota(jnp.int32, dshifted.shape, 1)
        dshifted = jnp.where(lane < HEADS, dshifted, 0.0)
        dr_ref[:, WIDE:] = dshifted.astype(bf16)
        headg_ref[...] = jnp.zeros_like(headg_ref)
        headg_ref[0:1, :] = jnp.sum(dshifted, axis=0, keepdims=True)
        headg_ref[1:2, :] = jnp.sum(decay * ddecay, axis=0, keepdims=True)


def whole(shape):
    return pl.BlockSpec(shape, lambda step: (0,) * len(shape))


def columns(rows, start=0):
    return pl.BlockSpec((rows, WIDE), lambda step: (0, start + step))


def fixed_columns(rows, start):
    return pl.BlockSpec((rows, WIDE), lambda step: (0, start))


def shape(rows, cols, dtype=f32):
    return jax.ShapeDtypeStruct((rows, cols), dtype)


def params():
    return pltpu.CompilerParams(dimension_semantics=("arbitrary",), vmem_limit_bytes=48 * 1024 * 1024)


def run_forward(lengths, raw, head, projected, gated_grad, par, gain):
    rows = projected.shape[0]
    state = pltpu.VMEM((STEPS, rows, WIDE), f32)
    narrow = pltpu.VMEM((rows, LANES), f32)
    return pl.pallas_call(
        forward_kernel,
        grid=(STEPS,),
        in_specs=[
            pl.BlockSpec(memory_space=pltpu.SMEM),
            whole((rows, LANES)),
            whole((8, LANES)),
            columns(rows, INNER // WIDE),
            fixed_columns(rows, 2 * INNER // WIDE),
            columns(rows),
            columns(rows),
            columns(8),
            fixed_columns(8, INNER // WIDE),
            whole((1, INNER)),
        ],
        out_specs=[
            whole((rows, INNER)), whole((rows, INNER)), whole((rows, INNER)),
            columns(rows), columns(rows), whole((rows, WIDE)), whole((1, INNER)),
        ],
        out_shape=[
            shape(rows, INNER, bf16), shape(rows, INNER, bf16), shape(rows, INNER),
            shape(rows, INNER), shape(rows, INNER), shape(rows, WIDE), shape(1, INNER),
        ],
        scratch_shapes=[
            pltpu.VMEM((CONV_WIDTH - 1, rows, LANES), f32),
            narrow, narrow, pltpu.VMEM((STEPS, 8, rows), f32),
            pltpu.VMEM((2, BLOCK, BLOCK), f32), pltpu.VMEM((BLOCK, BLOCK), bf16),
            state, state, state, state, narrow, narrow,
        ],
        compiler_params=params(),
        cost_estimate=pl.CostEstimate(flops=600_000_000, bytes_accessed=16_000_000, transcendentals=3_000_000),
        name="mixer_forward",
    )(lengths, raw, head, projected, projected, projected, gated_grad, par, par, gain)


def run_backward(lengths, raw, head, projected, conv, convbc, dheads, heads, par):
    rows = projected.shape[0]
    narrow = pltpu.VMEM((rows, LANES), f32)
    square = pltpu.VMEM((2, BLOCK, BLOCK), f32)
    return pl.pallas_call(
        backward_kernel,
        grid=(STEPS,),
        in_specs=[
            pl.BlockSpec(memory_space=pltpu.SMEM),
            whole((rows, LANES)),
            whole((8, LANES)),
            columns(rows, INNER // WIDE),
            fixed_columns(rows, 2 * INNER // WIDE),
            columns(rows), whole((rows, WIDE)), columns(rows), columns(rows),
            columns(8),
            fixed_columns(8, INNER // WIDE),
        ],
        out_specs=[
            columns(rows), whole((rows, WIDE + LANES)), columns(8), whole((8, WIDE)), whole((8, LANES)),
        ],
        out_shape=[
            shape(rows, INNER, bf16), shape(rows, WIDE + LANES, bf16), shape(8, INNER), shape(8, WIDE), shape(8, LANES),
        ],
        scratch_shapes=[
            pltpu.VMEM((CONV_WIDTH - 1, rows, LANES), f32),
            narrow, narrow, pltpu.VMEM((STEPS, 8, rows), f32), pltpu.VMEM((rows, WIDE), f32),
            square, pltpu.VMEM((BLOCK, BLOCK), bf16), square, pltpu.VMEM((BLOCK, BLOCK), f32), narrow, narrow,
        ],
        compiler_params=params(),
        cost_estimate=pl.CostEstimate(flops=1_500_000_000, bytes_accessed=16_000_000, transcendentals=3_000_000),
        name="mixer_backward",
    )(lengths, raw, head, projected, projected, conv, convbc, dheads, heads, par, par)


def make_shards(mesh):
    reps = mesh.shape["rep"]
    bits = reps.bit_length() - 1
    assert reps == 1 << bits and mesh.shape["shard"] == 2
    one_way = tuple(range(bits))
    turn = bits // 4 if bits >= 4 else min(1, bits)
    other_way = one_way[turn : 2 * turn] + one_way[:turn] + one_way[2 * turn :]

    def swap(value):
        return lax.ppermute(value, "shard", [(0, 1), (1, 0)])

    def across(value, bit):
        return lax.ppermute(value, "rep", [(place, place ^ (1 << bit)) for place in range(reps)])

    def scatter_sum(value, order):
        for bit in order:
            half = value.shape[0] // 2
            side = (lax.axis_index("rep") >> bit) & 1
            leaving = lax.dynamic_slice_in_dim(value, (1 - side) * half, half).astype(bf16)
            kept = lax.dynamic_slice_in_dim(value, side * half, half)
            value = kept + across(leaving, bit).astype(f32)
        return value.astype(bf16)

    def gather(value, order):
        for bit in reversed(order):
            side = (lax.axis_index("rep") >> bit) & 1
            value = joined(side, value, across(value, bit), 0)
        return value

    def joined(side, mine, theirs, axis):
        return jnp.where(
            side == 0, jnp.concatenate([mine, theirs], axis=axis), jnp.concatenate([theirs, mine], axis=axis)
        )

    def summed_over_reps(value):
        half = value.shape[0] // 2
        return jnp.concatenate(
            [
                gather(scatter_sum(value[:half], one_way), one_way),
                gather(scatter_sum(value[half:], other_way), other_way),
            ],
            axis=0,
        ).astype(f32)

    def shards(
        tokens, lengths, norm_gain, in_weight, conv_weight, conv_bias, step_bias, decay_log, skip_gain,
        gate_gain, out_weight, cotangent,
    ):
        core = lax.axis_index("shard")
        rows, model = tokens.shape
        half_model, half_inner = model // 2, INNER // 2
        half_conv, half_heads = CONVDIM // 2, HEADS // 2

        def mine(value, size):
            return lax.dynamic_slice_in_dim(value, core * size, size, axis=1)

        def theirs(value, size):
            return lax.dynamic_slice_in_dim(value, (1 - core) * size, size, axis=1)

        def line(value):
            return jnp.pad(value, (0, half_conv - value.shape[0]))[None]

        small = jnp.concatenate(
            [
                conv_weight.T, conv_bias[None], line(gate_gain),
                line(jnp.concatenate([norm_gain, step_bias, decay_log, skip_gain])),
                jnp.zeros((1, half_conv), bf16),
            ],
            axis=0,
        )
        small_o = swap(small)
        in_other = swap(in_weight)
        out_other = swap(out_weight)
        small, small_o = small.astype(f32), small_o.astype(f32)
        low_half, high_half = jnp.where(core == 0, small, small_o), jnp.where(core == 0, small_o, small)
        both = jnp.concatenate([low_half, high_half], axis=1)

        def pick(row, start, size):
            return jnp.concatenate([low_half[row, start : start + size], high_half[row, start : start + size]])

        norm_scale = pick(6, 0, half_model)
        head_lines = [pick(6, half_model + at * half_heads, half_heads) for at in range(3)]
        gate_line = pick(5, 0, half_inner)[None]
        par = jnp.concatenate(
            [
                both[:5],
                jnp.pad(gate_line, ((0, 0), (0, CONVDIM - INNER))),
                jnp.pad(jnp.repeat(head_lines[2], HEADDIM)[None], ((0, 0), (0, CONVDIM - INNER))),
                jnp.zeros((1, CONVDIM), f32),
            ],
            axis=0,
        )
        head = jnp.pad(jnp.stack(head_lines[:2]), ((0, 6), (0, LANES - HEADS)))

        live = (jnp.arange(rows, dtype=jnp.int32) < jnp.sum(lengths))[:, None]
        upstream = jnp.where(live, cotangent, jnp.zeros_like(cotangent))
        up_pair = jnp.concatenate([upstream, swap(upstream)], axis=0)
        inputs = tokens.astype(f32)
        scale = lax.rsqrt(jnp.mean(inputs * inputs, axis=-1, keepdims=True) + epsilon)
        normed = (inputs * scale * norm_scale).astype(bf16)
        normed_m, normed_o = mine(normed, half_model), theirs(normed, half_model)
        normed_pair = jnp.concatenate([normed_m, swap(normed_o)], axis=0)

        gated_grad = joined(core, mm(upstream, out_weight, LANE), mm(upstream, out_other, LANE), 1)
        projected = mm(normed_m, in_weight) + mm(normed_o, in_other)
        raw = jnp.pad(projected[:, STEP_COL:], ((0, 0), (0, LANES - HEADS)))
        gated, dgate, dheads, heads, conv, convbc, gain_g = run_forward(
            lengths, raw, head, projected, gated_grad, par, gate_line
        )

        def pair_of(value):
            return jnp.concatenate([value, swap(value)], axis=0)

        gated_m, gated_o = mine(gated, half_inner), theirs(gated, half_inner)
        gated_pair = jnp.concatenate([gated_m, swap(gated_o)], axis=0)
        out_grad = summed_over_reps(mm(gated_pair, up_pair, ROWS))
        gate_grad = summed_over_reps(mm(normed_pair, pair_of(dgate), ROWS))
        branch = mm(gated_m, out_weight) + mm(gated_o, out_other)
        output = (inputs + jnp.where(live, branch, 0.0)).astype(bf16)

        dx, dr, par_g, parbc_g, head_g = run_backward(
            lengths, raw, head, projected, conv, convbc, dheads, heads, par
        )
        late = jnp.concatenate([dx, dr], axis=1)
        late_grad = summed_over_reps(mm(normed_pair, pair_of(late), ROWS))
        in_grad = jnp.concatenate([gate_grad, late_grad[:, : STEP_COL + HEADS - INNER]], axis=1)

        proj_grad = jnp.concatenate([dgate, late[:, : STEP_COL + HEADS - INNER]], axis=1)
        normed_grad = joined(core, mm(proj_grad, in_weight, LANE), mm(proj_grad, in_other, LANE), 1)
        g = normed_grad * norm_scale
        input_grad = (
            cotangent.astype(f32)
            + scale * g
            - inputs * (scale * scale * scale * jnp.mean(g * inputs, axis=-1, keepdims=True))
        )
        gain_grad = jnp.sum(normed_grad * inputs * scale, axis=0)

        skip_g = jnp.sum(par_g[6].reshape(HEADS, HEADDIM), axis=1)
        tail = jnp.concatenate([gain_grad, head_g[0, :HEADS], head_g[1, :HEADS], skip_g])
        total = jnp.concatenate(
            [
                jnp.concatenate([par_g[:5], parbc_g[:5]], axis=1),
                jnp.pad(gain_g, ((0, 0), (0, CONVDIM - INNER))),
                jnp.pad(tail, (0, CONVDIM - tail.shape[0]))[None],
                jnp.zeros((1, CONVDIM), f32),
            ],
            axis=0,
        )
        total = total + swap(total)
        for bit in one_way:
            total = total + across(total, bit)

        def own(row, start, size):
            return lax.dynamic_slice_in_dim(total[row], start + core * size, size)

        return (
            output,
            input_grad,
            own(6, 0, half_model),
            in_grad,
            lax.dynamic_slice_in_dim(total[:4], core * half_conv, half_conv, axis=1).T,
            own(4, 0, half_conv),
            own(6, model, half_heads),
            own(6, model + HEADS, half_heads),
            own(6, model + 2 * HEADS, half_heads),
            own(5, 0, half_inner),
            out_grad,
        )

    return shards


def solution(mesh):
    split = P(("rep", "shard"), None)
    vector, matrix = P("shard"), P("shard", None)
    in_specs = (
        split, split, vector, matrix, matrix, vector, vector, vector, vector, vector, matrix, split,
    )
    out_specs = (
        split, split, vector, matrix, matrix, vector, vector, vector, vector, vector, matrix,
    )
    return jax.shard_map(make_shards(mesh), mesh=mesh, in_specs=in_specs, out_specs=out_specs, check_vma=False)
```

time: 821 us -> 295 us (0.36)
  waiting for transfers between devices: 325 us -> 92.3 us
  local copies, waits for them, and re-layouts: 187 us -> 25 us
  blocking collectives: 96.1 us -> 0 us
  starting transfers between devices: 0.24 us -> 73.7 us
  matrix products: 99.3 us -> 29.6 us
  Pallas kernels: 0 us -> 32.2 us
  other arithmetic: 63.1 us -> 35.1 us
  loops' own time: 18.5 us -> 0 us
  between operations: 18.7 us -> 1.84 us
    psum x1 -> x0, waiting for transfers between devices: 290 us -> none  [shards(): lax.psum((shares[0], shares[1], shares[2], shares[3], shares[4], shares[5...]
    dynamic_update_slice x10 -> x0, local copies, waits for them, and re-layouts: 106 us -> none  [state_space(): unused, results = lax.scan(jax.checkpoint(block_step), initial, pieces)]
    ppermute x0 -> x61, waiting for transfers between devices: none -> 92.3 us  [the longest x52 90 us: across(): lax.ppermute(value, 'rep', [(place, place ^ 1 << bit) for place in range(...]
    psum x1 -> x0, blocking collectives: 82.3 us -> none  [shards(): lax.psum((shares[0], shares[1], shares[2], shares[3], shares[4], shares[5...]
    ppermute x0 -> x61, starting transfers between devices: none -> 73.7 us  [the longest x52 71.4 us: across(): lax.ppermute(value, 'rep', [(place, place ^ 1 << bit) for place in range(...]
    dot_general x34 -> x11, matrix products: 99.3 us -> 29.6 us  [mm(): lax.dot_general(left, right, (dims, ((), ())), precision=precision, prefe...]
    pallas_call x0 -> x2, Pallas kernels: none -> 32.2 us  [the longest x1 18.7 us: run_backward(): pl.pallas_call(backward_kernel, grid=(STEPS,), in_specs=[pl.BlockSpec(mem...]
    reduce_scatter x2 -> x0, waiting for transfers between devices: 26.9 us -> none  [the longest x1 26.9 us: shards(): lax.psum_scatter(in_local, 'shard', scatter_dimension=0, tiled=True)]
  transfers between devices with their start and end apart: 6 -> 61, of which waited for: 3 -> 34; matrix products, arithmetic and copies ran while one was open for 40% -> 18% of each run, Pallas kernels for 0% -> 11%
where the time goes in v1:
time: 295 us; the launch traced here: 290 us
  waiting for transfers between devices  92.3 us (31%)
  starting transfers between devices  73.7 us (25%)
  other arithmetic  35.1 us (12%)
  Pallas kernels  32.2 us (11%)
  matrix products  29.6 us (10%)
  local copies, waits for them, and re-layouts  25 us (8%)
    ppermute x52, waiting for transfers between devices, across(): lax.ppermute(value, 'rep', [(place, place ^ 1 << bit) for place in range(...  90 us
    ppermute x52, starting transfers between devices, across(): lax.ppermute(value, 'rep', [(place, place ^ 1 << bit) for place in range(...  71.4 us
    dot_general x11, matrix products, mm(): lax.dot_general(left, right, (dims, ((), ())), precision=precision, prefe...  29.6 us
    concatenate x1, other arithmetic, shards(): jnp.concatenate([gate_grad, late_grad[:, :STEP_COL + HEADS - INNER]], axi...  18.9 us
    pallas_call x1, Pallas kernels, run_backward(): pl.pallas_call(backward_kernel, grid=(STEPS,), in_specs=[pl.BlockSpec(mem...  18.7 us
    unnamed x32, local copies, waits for them, and re-layouts  15.4 us
    pallas_call x1, Pallas kernels, run_forward(): pl.pallas_call(forward_kernel, grid=(STEPS,), in_specs=[pl.BlockSpec(memo...  13.4 us
  transfers between devices with their start and end apart: 61, of which 34 were waited for; matrix products, arithmetic and copies ran while one was open for 18% of the time, Pallas kernels for 11%

profile of v1, /device:TPU:0, one launch (start us, length us, event | category | flops | bytes accessed | tf_op | source)
XLA Modules:
  0.0 289.7 jit_solution(13408110338859109618)
XLA Ops:
  9.1 3.4 %fusion.55 = f32[256,1024]{1,0:T(8,128)} fusion(bf16[256,1024]{1,0:T(8,128)(2,1)S(1)} %broadcast_select_fusion, bf16[1024,1024]{1,0:T(8,128)(2,1)} %param.22), kind=kOutput, calls=%fused_computation.187 | convolution fusion | flops 536870912 | bytes 3670016 | tf_op jit(solution)/shard_map/dot_general | solution.py:29
  14.5 3.7 %fusion.54 = f32[256,4384]{1,0:T(8,128)S(1)} fusion(bf16[256,512]{1,0:T(8,128)(2,1)S(1)} %get-tuple-element.57, bf16[512,4384]{0,1:T(8,128)(2,1)} %param.15), kind=kOutput, calls=%fused_computation.186 | convolution fusion | flops 1149239296 | bytes 9240576 | tf_op jit(solution)/shard_map/dot_general | solution.py:29
  21.5 3.8 %convolution_add_fusion.sig_ref.bc_ref.gate_ref = f32[256,4384]{1,0:T(8,128)S(1)} fusion(f32[256,4384]{1,0:T(8,128)S(1)} %fusion.54, bf16[256,512]{1,0:T(8,128)(2,1)} %get-tuple-element.56, bf16[512,4384]{0,1:T(8,128)(2,1)} %collective-permute-done.1), kind=kOutput, calls=%fused_computation | convolution fusion | flops 1150361600 | bytes 13729792 | tf_op jit(solution)/shard_map/dot_general | solution.py:29
  27.5 13.4 %mixer_forward.1 = (bf16[256,2048]{1,0:T(8,128)(2,1)S(1)}, bf16[256,2048]{1,0:T(8,128)(2,1)S(1)}, f32[256,2048]{1,0:T(8,128)S(1)}, f32[256,2048]{1,0:T(8,128)}, ...) custom-call(s32[1,4]{1,0:T(1,128)S(1)} %copy-done.1, f32[256,128]{1,0:T(8,128)S(1)} %pad.32.raw_ref, ...), custom_call_target="tpu_custom_call" | custom-call | flops 600000000 | bytes 16000000 | tf_op jit(solution)/shard_map/mixer_forward/pallas_call | solution.py:374
  42.5 18.7 %mixer_backward.1 = (bf16[256,2048]{1,0:T(8,128)(2,1)S(1)}, bf16[256,384]{1,0:T(8,128)(2,1)S(1)}, f32[8,2048]{1,0:T(8,128)S(1)}, f32[8,256]{1,0:T(8,128)S(1)}, f32[8,128]{1,0:T(8,128)S(1)}) custom-call(s32[1,4]{1,0:T(1,128)S(1)} %copy-done.1, f32[256,128]{1,0:T(8,128)S(1)} %pad.32.raw_ref, f32[8,128]{1,0:T(8,128)S(1)} %select_maximum_fusion.4.head_ref, ...), custom_call_target="tpu_custom_call" | custom-call | flops 1500000000 | bytes 16000000 | tf_op jit(solution)/shard_map/mixer_backward/pallas_call | solution.py:413
  63.5 3.5 %fusion.11 = f32[256,512]{1,0:T(8,128)} fusion(bf16[512,4384]{0,1:T(8,128)(2,1)S(1)} %bitcast.61, bf16[256,2336]{1,0:T(8,128)(2,1)} %bitcast.51, bf16[256,2048]{1,0:T(8,128)(2,1)S(1)} %get-tuple-element.24), kind=kOutput, calls=%fused_computation.22 | convolution fusion | flops 1153728512 | bytes 7258112 | tf_op jit(solution)/shard_map/dot_general | solution.py:29
  67.2 4.1 %fusion.10 = f32[256,512]{1,0:T(8,128)S(1)} fusion(bf16[512,4384]{0,1:T(8,128)(2,1)} %collective-permute-done.1, bf16[256,2336]{1,0:T(8,128)(2,1)} %bitcast.51, bf16[256,2048]{1,0:T(8,128)(2,1)S(1)} %get-tuple-element.24), kind=kOutput, calls=%fused_computation.21 | convolution fusion | flops 1153728512 | bytes 7258112 | tf_op jit(solution)/shard_map/dot_general | solution.py:29
  73.6 2.7 collective-permute-start.4
  85.5 2.5 collective-permute-done.6
  88.0 3.2 %collective-permute-start.7 = (f32[8,2304]{1,0:T(8,128)S(1)}, f32[8,2304]{1,0:T(8,128)S(1)}, u32[]{:S(2)}, u32[]{:S(2)}) collective-permute-start(f32[8,2304]{1,0:T(8,128)S(1)} %add.270), channel_id=1, source_target_pairs={{0,16},{2,18},{4,20},{6,22},{8,24},{10,26},{12,28},{14,30},{16,0},... | collective-permute-start | bytes 221192 | tf_op jit(solution)/shard_map/ppermute | solution.py:455
  104.1 8.3 %collective-permute-done.53 = bf16[256,1024]{1,0:T(8,128)(2,1)S(1)} collective-permute-done((bf16[256,1024]{1,0:T(8,128)(2,1)S(1)}, bf16[256,1024]{1,0:T(8,128)(2,1)S(1)}, u32[]{:S(2)}, u32[]{:S(2)}) %collective-permute-start.53) | collective-permute-done | bytes 524320 | tf_op jit(solution)/shard_map/ppermute | solution.py:455
  116.0 2.6 fusion.6
  121.6 3.3 %fusion.2 = f32[512,2432]{1,0:T(8,128)S(1)} fusion(bf16[256,2432]{1,0:T(8,128)(2,1)} %collective-permute-done.26, bf16[256,2432]{1,0:T(8,128)(2,1)} %constant_dynamic-update-slice_fusion, bf16[256,512]{1,0:T(8,128)(2,1)} %collective-permute-done.8, bf16[256,512]{1,0:T(8,128)(2,1)S(1)} %get-tuple-element.57), kind=kOutput, calls=%fused_computation.4 | convolution fusion | flops 1281097728 | bytes 7995392 | tf_op jit(solution)/shard_map/dot_general | solution.py:29
  129.3 3.9 %collective-permute-done.55 = bf16[64,1024]{1,0:T(8,128)(2,1)S(1)} collective-permute-done((bf16[64,1024]{1,0:T(8,128)(2,1)S(1)}, bf16[64,1024]{1,0:T(8,128)(2,1)S(1)}, u32[]{:S(2)}, u32[]{:S(2)}) %collective-permute-start.55) | collective-permute-done | bytes 131104 | tf_op jit(solution)/shard_map/ppermute | solution.py:455
  134.9 4.0 %collective-permute-done.47 = bf16[64,1024]{1,0:T(8,128)(2,1)S(1)} collective-permute-done((bf16[64,1024]{1,0:T(8,128)(2,1)S(1)}, bf16[64,1024]{1,0:T(8,128)(2,1)S(1)}, u32[]{:S(2)}, u32[]{:S(2)}) %collective-permute-start.47) | collective-permute-done | bytes 131104 | tf_op jit(solution)/shard_map/ppermute | solution.py:455
  138.9 3.0 %collective-permute-start.56 = (bf16[32,1024]{1,0:T(8,128)(2,1)S(1)}, bf16[32,1024]{1,0:T(8,128)(2,1)S(1)}, u32[]{:S(2)}, u32[]{:S(2)}) collective-permute-start(bf16[32,1024]{1,0:T(8,128)(2,1)S(1)} %dynamic-slice_convert_fusion.20), channel_id=1, source_target_pairs={{0,16},{2,18},{4,20},{6,22},{8,24},{10,26},{12,28},{14,30},{16,0},... | collective-permute-start | bytes 196616 | tf_op jit(solution)/shard_map/ppermute | solution.py:455
  144.1 2.9 %collective-permute-start.48 = (bf16[32,1024]{1,0:T(8,128)(2,1)S(1)}, bf16[32,1024]{1,0:T(8,128)(2,1)S(1)}, u32[]{:S(2)}, u32[]{:S(2)}) collective-permute-start(bf16[32,1024]{1,0:T(8,128)(2,1)S(1)} %dynamic-slice_convert_fusion.21), channel_id=1, source_target_pairs={{0,16},{2,18},{4,20},{6,22},{8,24},{10,26},{12,28},{14,30},{16,0},... | collective-permute-start | bytes 196616 | tf_op jit(solution)/shard_map/ppermute | solution.py:455
  147.0 3.2 %collective-permute-done.48 = bf16[32,1024]{1,0:T(8,128)(2,1)S(1)} collective-permute-done((bf16[32,1024]{1,0:T(8,128)(2,1)S(1)}, bf16[32,1024]{1,0:T(8,128)(2,1)S(1)}, u32[]{:S(2)}, u32[]{:S(2)}) %collective-permute-start.48) | collective-permute-done | bytes 65568 | tf_op jit(solution)/shard_map/ppermute | solution.py:455
  160.1 2.8 collective-permute-done.58
  163.7 2.4 collective-permute-done.50
  178.9 2.8 collective-permute-start.21
  189.1 3.4 %collective-permute-done.22 = bf16[16,2048]{1,0:T(8,128)(2,1)S(1)} collective-permute-done((bf16[16,2048]{1,0:T(8,128)(2,1)S(1)}, bf16[16,2048]{1,0:T(8,128)(2,1)S(1)}, u32[]{:S(2)}, u32[]{:S(2)}) %collective-permute-start.22) | collective-permute-done | bytes 65568 | tf_op jit(solution)/shard_map/ppermute | solution.py:455
  194.6 3.8 %collective-permute-done.14 = bf16[16,2048]{1,0:T(8,128)(2,1)S(1)} collective-permute-done((bf16[16,2048]{1,0:T(8,128)(2,1)S(1)}, bf16[16,2048]{1,0:T(8,128)(2,1)S(1)}, u32[]{:S(2)}, u32[]{:S(2)}) %collective-permute-start.14) | collective-permute-done | bytes 65568 | tf_op jit(solution)/shard_map/ppermute | solution.py:455
  211.6 4.4 %collective-permute-done.38 = bf16[16,2432]{1,0:T(8,128)(2,1)S(1)} collective-permute-done((bf16[16,2432]{1,0:T(8,128)(2,1)S(1)}, bf16[16,2432]{1,0:T(8,128)(2,1)S(1)}, u32[]{:S(2)}, u32[]{:S(2)}) %collective-permute-start.38) | collective-permute-done | bytes 77856 | tf_op jit(solution)/shard_map/ppermute | solution.py:455
  217.6 4.3 %collective-permute-done.30 = bf16[16,2432]{1,0:T(8,128)(2,1)S(1)} collective-permute-done((bf16[16,2432]{1,0:T(8,128)(2,1)S(1)}, bf16[16,2432]{1,0:T(8,128)(2,1)S(1)}, u32[]{:S(2)}, u32[]{:S(2)}) %collective-permute-start.30) | collective-permute-done | bytes 77856 | tf_op jit(solution)/shard_map/ppermute | solution.py:455
  223.0 4.9 %collective-permute-done.39 = bf16[16,2432]{1,0:T(8,128)(2,1)S(1)} collective-permute-done((bf16[16,2432]{1,0:T(8,128)(2,1)S(1)}, bf16[16,2432]{1,0:T(8,128)(2,1)S(1)}, u32[]{:S(2)}, u32[]{:S(2)}) %collective-permute-start.39) | collective-permute-done | bytes 77856 | tf_op jit(solution)/shard_map/ppermute | solution.py:455
  228.3 4.9 %collective-permute-done.31 = bf16[16,2432]{1,0:T(8,128)(2,1)S(1)} collective-permute-done((bf16[16,2432]{1,0:T(8,128)(2,1)S(1)}, bf16[16,2432]{1,0:T(8,128)(2,1)S(1)}, u32[]{:S(2)}, u32[]{:S(2)}) %collective-permute-start.31) | collective-permute-done | bytes 77856 | tf_op jit(solution)/shard_map/ppermute | solution.py:455
  239.0 2.5 maximum_convert_fusion
  243.5 5.1 %collective-permute-done.41 = bf16[64,2432]{1,0:T(8,128)(2,1)S(1)} collective-permute-done((bf16[64,2432]{1,0:T(8,128)(2,1)S(1)}, bf16[64,2432]{1,0:T(8,128)(2,1)S(1)}, u32[]{:S(2)}, u32[]{:S(2)}) %collective-permute-start.41) | collective-permute-done | bytes 311328 | tf_op jit(solution)/shard_map/ppermute | solution.py:455
  251.5 7.5 %collective-permute-done.42 = bf16[128,2432]{1,0:T(8,128)(2,1)S(1)} collective-permute-done((bf16[128,2432]{1,0:T(8,128)(2,1)S(1)}, bf16[128,2432]{1,0:T(8,128)(2,1)S(1)}, u32[]{:S(2)}, u32[]{:S(2)}) %collective-permute-start.42) | collective-permute-done | bytes 622624 | tf_op jit(solution)/shard_map/ppermute | solution.py:455
  261.1 18.9 %fusion.1 = f32[512,4384]{1,0:T(8,128)} fusion(bf16[256,2432]{1,0:T(8,128)(2,1)S(1)} %maximum_select_fusion.2, bf16[256,2432]{1,0:T(8,128)(2,1)S(1)} %maximum_select_fusion.1, bf16[256,2048]{1,0:T(8,128)(2,1)S(1)} %maximum_select_fusion.5, bf16[256,2048]{1,0:T(8,128)(2,1)S(1)} %maximum_select_fusion.4), kind=kLoop, calls=%fused_computation.3 | loop fusion | flops 17956864 | bytes 13565952 | tf_op jit(solution)/shard_map/concatenate | solution.py:568
  280.0 9.4 %copy.25 = f32[512,4384]{0,1:T(8,128)} copy(f32[512,4384]{1,0:T(8,128)} %fusion.1) | data formatting | bytes 17956864
  (271 shorter events, 120.7 us)
Async XLA Ops:
  3.6 8.9 %collective-permute-start = (bf16[8,1152]{1,0:T(8,128)(2,1)S(1)}, bf16[8,1152]{1,0:T(8,128)(2,1)S(1)}, u32[]{:S(2)}, u32[]{:S(2)}) collective-permute-start(bf16[8,1152]{1,0:T(8,128)(2,1)S(1)} %concatenate.229), channel_id=1, source_target_pairs={{0,1},{1,0},{2,3},{3,2},{4,5},{5,4},{6,7},{7,6},{8,9},{9,8},{10,11... | collective-permute-start | bytes 55304 | tf_op jit(solution)/shard_map/ppermute | solution.py:452
  4.1 17.4 %collective-permute-start.1 = (bf16[512,4384]{0,1:T(8,128)(2,1)}, bf16[512,4384]{0,1:T(8,128)(2,1)}, u32[]{:S(2)}, u32[]{:S(2)}) collective-permute-start(bf16[512,4384]{0,1:T(8,128)(2,1)} %param.15), channel_id=1, source_target_pairs={{0,1},{1,0},{2,3},{3,2},{4,5},{5,4},{6,7},{7,6},{8,9},{9,8},{10,11... | collective-permute-start | bytes 13467656 | tf_op jit(solution)/shard_map/ppermute | solution.py:452
  4.2 14.1 %collective-permute-start.2 = (bf16[1024,1024]{1,0:T(8,128)(2,1)}, bf16[1024,1024]{1,0:T(8,128)(2,1)S(1)}, u32[]{:S(2)}, u32[]{:S(2)}) collective-permute-start(bf16[1024,1024]{1,0:T(8,128)(2,1)} %param.22), channel_id=1, source_target_pairs={{0,1},{1,0},{2,3},{3,2},{4,5},{5,4},{6,7},{7,6},{8,9},{9,8},{10,11... | collective-permute-start | bytes 6291464 | tf_op jit(solution)/shard_map/ppermute | solution.py:452
  7.7 86.4 %collective-permute-start.44 = (bf16[256,1024]{1,0:T(8,128)(2,1)S(1)}, bf16[256,1024]{1,0:T(8,128)(2,1)}, u32[]{:S(2)}, u32[]{:S(2)}) collective-permute-start(bf16[256,1024]{1,0:T(8,128)(2,1)S(1)} %broadcast_select_fusion), channel_id=1, source_target_pairs={{0,1},{1,0},{2,3},{3,2},{4,5},{5,4},{6,7},{7,6},{8,9},{9,8},{10,11... | collective-permute-start | bytes 1572872 | tf_op jit(solution)/shard_map/ppermute | solution.py:452
  13.9 102.1 %collective-permute-start.8 = (bf16[256,512]{1,0:T(8,128)(2,1)}, bf16[256,512]{1,0:T(8,128)(2,1)}, u32[]{:S(2)}, u32[]{:S(2)}) collective-permute-start(bf16[256,512]{1,0:T(8,128)(2,1)} %get-tuple-element.56), channel_id=1, source_target_pairs={{0,1},{1,0},{2,3},{3,2},{4,5},{5,4},{6,7},{7,6},{8,9},{9,8},{10,11... | collective-permute-start | bytes 786440 | tf_op jit(solution)/shard_map/ppermute | solution.py:452
  63.0 58.6 %collective-permute-start.26 = (bf16[256,2432]{1,0:T(8,128)(2,1)}, bf16[256,2432]{1,0:T(8,128)(2,1)}, u32[]{:S(2)}, u32[]{:S(2)}) collective-permute-start(bf16[256,2432]{1,0:T(8,128)(2,1)} %constant_dynamic-update-slice_fusion), channel_id=1, source_target_pairs={{0,1},{1,0},{2,3},{3,2},{4,5},{5,4},{6,7},{7,6},{8,9},{9,8},{10,11... | collective-permute-start | bytes 3735560 | tf_op jit(solution)/shard_map/ppermute | solution.py:452
  63.1 53.0 %collective-permute-start.9 = (bf16[256,2048]{1,0:T(8,128)(2,1)S(1)}, bf16[256,2048]{1,0:T(8,128)(2,1)}, u32[]{:S(2)}, u32[]{:S(2)}) collective-permute-start(bf16[256,2048]{1,0:T(8,128)(2,1)S(1)} %get-tuple-element.24), channel_id=1, source_target_pairs={{0,1},{1,0},{2,3},{3,2},{4,5},{5,4},{6,7},{7,6},{8,9},{9,8},{10,11... | collective-permute-start | bytes 3145736 | tf_op jit(solution)/shard_map/ppermute | solution.py:452
  98.4 14.0 %collective-permute-start.53 = (bf16[256,1024]{1,0:T(8,128)(2,1)S(1)}, bf16[256,1024]{1,0:T(8,128)(2,1)S(1)}, u32[]{:S(2)}, u32[]{:S(2)}) collective-permute-start(bf16[256,1024]{1,0:T(8,128)(2,1)S(1)} %dynamic-slice_convert_fusion.2), channel_id=1, source_target_pairs={{0,4},{2,6},{4,0},{6,2},{8,12},{10,14},{12,8},{14,10},{16,20},{18,... | collective-permute-start | bytes 1572872 | tf_op jit(solution)/shard_map/ppermute | solution.py:455
  100.8 13.7 %collective-permute-start.45 = (bf16[256,1024]{1,0:T(8,128)(2,1)S(1)}, bf16[256,1024]{1,0:T(8,128)(2,1)S(1)}, u32[]{:S(2)}, u32[]{:S(2)}) collective-permute-start(bf16[256,1024]{1,0:T(8,128)(2,1)S(1)} %dynamic-slice_convert_fusion.3), channel_id=1, source_target_pairs={{0,2},{2,0},{4,6},{6,4},{8,10},{10,8},{12,14},{14,12},{16,18},{18,... | collective-permute-start | bytes 1572872 | tf_op jit(solution)/shard_map/ppermute | solution.py:455
  112.6 13.4 %collective-permute-start.54 = (bf16[128,1024]{1,0:T(8,128)(2,1)S(1)}, bf16[128,1024]{1,0:T(8,128)(2,1)S(1)}, u32[]{:S(2)}, u32[]{:S(2)}) collective-permute-start(bf16[128,1024]{1,0:T(8,128)(2,1)S(1)} %dynamic-slice_convert_fusion.8), channel_id=1, source_target_pairs={{0,2},{2,0},{4,6},{6,4},{8,10},{10,8},{12,14},{14,12},{16,18},{18,... | collective-permute-start | bytes 786440 | tf_op jit(solution)/shard_map/ppermute | solution.py:455
  114.7 12.8 %collective-permute-start.46 = (bf16[128,1024]{1,0:T(8,128)(2,1)S(1)}, bf16[128,1024]{1,0:T(8,128)(2,1)S(1)}, u32[]{:S(2)}, u32[]{:S(2)}) collective-permute-start(bf16[128,1024]{1,0:T(8,128)(2,1)S(1)} %dynamic-slice_convert_fusion.9), channel_id=1, source_target_pairs={{0,4},{2,6},{4,0},{6,2},{8,12},{10,14},{12,8},{14,10},{16,20},{18,... | collective-permute-start | bytes 786440 | tf_op jit(solution)/shard_map/ppermute | solution.py:455
  119.2 33.1 %collective-permute-start.18 = (bf16[128,2048]{1,0:T(8,128)(2,1)S(1)}, bf16[128,2048]{1,0:T(8,128)(2,1)S(1)}, u32[]{:S(2)}, u32[]{:S(2)}) collective-permute-start(bf16[128,2048]{1,0:T(8,128)(2,1)S(1)} %dynamic-slice_convert_fusion.4), channel_id=1, source_target_pairs={{0,4},{2,6},{4,0},{6,2},{8,12},{10,14},{12,8},{14,10},{16,20},{18,... | collective-permute-start | bytes 1572872 | tf_op jit(solution)/shard_map/ppermute | solution.py:455
  120.1 39.7 %collective-permute-start.10 = (bf16[128,2048]{1,0:T(8,128)(2,1)S(1)}, bf16[128,2048]{1,0:T(8,128)(2,1)S(1)}, u32[]{:S(2)}, u32[]{:S(2)}) collective-permute-start(bf16[128,2048]{1,0:T(8,128)(2,1)S(1)} %dynamic-slice_convert_fusion.5), channel_id=1, source_target_pairs={{0,2},{2,0},{4,6},{6,4},{8,10},{10,8},{12,14},{14,12},{16,18},{18,... | collective-permute-start | bytes 1572872 | tf_op jit(solution)/shard_map/ppermute | solution.py:455
  125.4 47.8 %collective-permute-start.35 = (bf16[128,2432]{1,0:T(8,128)(2,1)S(1)}, bf16[128,2432]{1,0:T(8,128)(2,1)S(1)}, u32[]{:S(2)}, u32[]{:S(2)}) collective-permute-start(bf16[128,2432]{1,0:T(8,128)(2,1)S(1)} %dynamic-slice_convert_fusion), channel_id=1, source_target_pairs={{0,4},{2,6},{4,0},{6,2},{8,12},{10,14},{12,8},{14,10},{16,20},{18,... | collective-permute-start | bytes 1867784 | tf_op jit(solution)/shard_map/ppermute | solution.py:455
  126.1 47.4 %collective-permute-start.27 = (bf16[128,2432]{1,0:T(8,128)(2,1)S(1)}, bf16[128,2432]{1,0:T(8,128)(2,1)S(1)}, u32[]{:S(2)}, u32[]{:S(2)}) collective-permute-start(bf16[128,2432]{1,0:T(8,128)(2,1)S(1)} %dynamic-slice_convert_fusion.1), channel_id=1, source_target_pairs={{0,2},{2,0},{4,6},{6,4},{8,10},{10,8},{12,14},{14,12},{16,18},{18,... | collective-permute-start | bytes 1867784 | tf_op jit(solution)/shard_map/ppermute | solution.py:455
  155.5 11.8 %collective-permute-start.19 = (bf16[64,2048]{1,0:T(8,128)(2,1)S(1)}, bf16[64,2048]{1,0:T(8,128)(2,1)S(1)}, u32[]{:S(2)}, u32[]{:S(2)}) collective-permute-start(bf16[64,2048]{1,0:T(8,128)(2,1)S(1)} %dynamic-slice_convert_fusion.10), channel_id=1, source_target_pairs={{0,2},{2,0},{4,6},{6,4},{8,10},{10,8},{12,14},{14,12},{16,18},{18,... | collective-permute-start | bytes 786440 | tf_op jit(solution)/shard_map/ppermute | solution.py:455
  162.9 8.0 %collective-permute-start.11 = (bf16[64,2048]{1,0:T(8,128)(2,1)S(1)}, bf16[64,2048]{1,0:T(8,128)(2,1)S(1)}, u32[]{:S(2)}, u32[]{:S(2)}) collective-permute-start(bf16[64,2048]{1,0:T(8,128)(2,1)S(1)} %dynamic-slice_convert_fusion.11), channel_id=1, source_target_pairs={{0,4},{2,6},{4,0},{6,2},{8,12},{10,14},{12,8},{14,10},{16,20},{18,... | collective-permute-start | bytes 786440 | tf_op jit(solution)/shard_map/ppermute | solution.py:455
  166.2 15.7 %collective-permute-start.59 = (bf16[128,1024]{1,0:T(8,128)(2,1)S(1)}, bf16[128,1024]{1,0:T(8,128)(2,1)S(1)}, u32[]{:S(2)}, u32[]{:S(2)}) collective-permute-start(bf16[128,1024]{1,0:T(8,128)(2,1)S(1)} %maximum_select_fusion.19), channel_id=1, source_target_pairs={{0,2},{2,0},{4,6},{6,4},{8,10},{10,8},{12,14},{14,12},{16,18},{18,... | collective-permute-start | bytes 786440 | tf_op jit(solution)/shard_map/ppermute | solution.py:455
  167.2 14.9 %collective-permute-start.51 = (bf16[128,1024]{1,0:T(8,128)(2,1)S(1)}, bf16[128,1024]{1,0:T(8,128)(2,1)S(1)}, u32[]{:S(2)}, u32[]{:S(2)}) collective-permute-start(bf16[128,1024]{1,0:T(8,128)(2,1)S(1)} %maximum_select_fusion.18), channel_id=1, source_target_pairs={{0,4},{2,6},{4,0},{6,2},{8,12},{10,14},{12,8},{14,10},{16,20},{18,... | collective-permute-start | bytes 786440 | tf_op jit(solution)/shard_map/ppermute | solution.py:455
  173.5 26.3 %collective-permute-start.36 = (bf16[64,2432]{1,0:T(8,128)(2,1)S(1)}, bf16[64,2432]{1,0:T(8,128)(2,1)S(1)}, u32[]{:S(2)}, u32[]{:S(2)}) collective-permute-start(bf16[64,2432]{1,0:T(8,128)(2,1)S(1)} %dynamic-slice_convert_fusion.6), channel_id=1, source_target_pairs={{0,2},{2,0},{4,6},{6,4},{8,10},{10,8},{12,14},{14,12},{16,18},{18,... | collective-permute-start | bytes 933896 | tf_op jit(solution)/shard_map/ppermute | solution.py:455
  176.3 24.3 %collective-permute-start.28 = (bf16[64,2432]{1,0:T(8,128)(2,1)S(1)}, bf16[64,2432]{1,0:T(8,128)(2,1)S(1)}, u32[]{:S(2)}, u32[]{:S(2)}) collective-permute-start(bf16[64,2432]{1,0:T(8,128)(2,1)S(1)} %dynamic-slice_convert_fusion.7), channel_id=1, source_target_pairs={{0,4},{2,6},{4,0},{6,2},{8,12},{10,14},{12,8},{14,10},{16,20},{18,... | collective-permute-start | bytes 933896 | tf_op jit(solution)/shard_map/ppermute | solution.py:455
  182.1 53.5 %collective-permute-start.60 = (bf16[256,1024]{1,0:T(8,128)(2,1)S(1)}, bf16[256,1024]{1,0:T(8,128)(2,1)S(1)}, u32[]{:S(2)}, u32[]{:S(2)}) collective-permute-start(bf16[256,1024]{1,0:T(8,128)(2,1)S(1)} %maximum_select_fusion.13), channel_id=1, source_target_pairs={{0,4},{2,6},{4,0},{6,2},{8,12},{10,14},{12,8},{14,10},{16,20},{18,... | collective-permute-start | bytes 1572872 | tf_op jit(solution)/shard_map/ppermute | solution.py:455
  184.1 54.4 %collective-permute-start.52 = (bf16[256,1024]{1,0:T(8,128)(2,1)S(1)}, bf16[256,1024]{1,0:T(8,128)(2,1)S(1)}, u32[]{:S(2)}, u32[]{:S(2)}) collective-permute-start(bf16[256,1024]{1,0:T(8,128)(2,1)S(1)} %maximum_select_fusion.12), channel_id=1, source_target_pairs={{0,2},{2,0},{4,6},{6,4},{8,10},{10,8},{12,14},{14,12},{16,18},{18,... | collective-permute-start | bytes 1572872 | tf_op jit(solution)/shard_map/ppermute | solution.py:455
  205.6 27.6 %collective-permute-start.24 = (bf16[64,2048]{1,0:T(8,128)(2,1)S(1)}, bf16[64,2048]{1,0:T(8,128)(2,1)S(1)}, u32[]{:S(2)}, u32[]{:S(2)}) collective-permute-start(bf16[64,2048]{1,0:T(8,128)(2,1)S(1)} %maximum_select_fusion.17), channel_id=1, source_target_pairs={{0,2},{2,0},{4,6},{6,4},{8,10},{10,8},{12,14},{14,12},{16,18},{18,... | collective-permute-start | bytes 786440 | tf_op jit(solution)/shard_map/ppermute | solution.py:455
  208.1 27.3 %collective-permute-start.16 = (bf16[64,2048]{1,0:T(8,128)(2,1)S(1)}, bf16[64,2048]{1,0:T(8,128)(2,1)S(1)}, u32[]{:S(2)}, u32[]{:S(2)}) collective-permute-start(bf16[64,2048]{1,0:T(8,128)(2,1)S(1)} %maximum_select_fusion.16), channel_id=1, source_target_pairs={{0,4},{2,6},{4,0},{6,2},{8,12},{10,14},{12,8},{14,10},{16,20},{18,... | collective-permute-start | bytes 786440 | tf_op jit(solution)/shard_map/ppermute | solution.py:455
  233.2 8.3 %collective-permute-start.40 = (bf16[32,2432]{1,0:T(8,128)(2,1)S(1)}, bf16[32,2432]{1,0:T(8,128)(2,1)S(1)}, u32[]{:S(2)}, u32[]{:S(2)}) collective-permute-start(bf16[32,2432]{1,0:T(8,128)(2,1)S(1)} %maximum_select_fusion.21), channel_id=1, source_target_pairs={{0,8},{2,10},{4,12},{6,14},{8,0},{10,2},{12,4},{14,6},{16,24},{18,... | collective-permute-start | bytes 466952 | tf_op jit(solution)/shard_map/ppermute | solution.py:455
  233.3 8.4 %collective-permute-start.32 = (bf16[32,2432]{1,0:T(8,128)(2,1)S(1)}, bf16[32,2432]{1,0:T(8,128)(2,1)S(1)}, u32[]{:S(2)}, u32[]{:S(2)}) collective-permute-start(bf16[32,2432]{1,0:T(8,128)(2,1)S(1)} %maximum_select_fusion.20), channel_id=1, source_target_pairs={{0,8},{2,10},{4,12},{6,14},{8,0},{10,2},{12,4},{14,6},{16,24},{18,... | collective-permute-start | bytes 466952 | tf_op jit(solution)/shard_map/ppermute | solution.py:455
  235.5 15.5 %collective-permute-start.25 = (bf16[128,2048]{1,0:T(8,128)(2,1)S(1)}, bf16[128,2048]{1,0:T(8,128)(2,1)S(1)}, u32[]{:S(2)}, u32[]{:S(2)}) collective-permute-start(bf16[128,2048]{1,0:T(8,128)(2,1)S(1)} %maximum_select_fusion.11), channel_id=1, source_target_pairs={{0,4},{2,6},{4,0},{6,2},{8,12},{10,14},{12,8},{14,10},{16,20},{18,... | collective-permute-start | bytes 1572872 | tf_op jit(solution)/shard_map/ppermute | solution.py:455
  235.7 15.6 %collective-permute-start.17 = (bf16[128,2048]{1,0:T(8,128)(2,1)S(1)}, bf16[128,2048]{1,0:T(8,128)(2,1)S(1)}, u32[]{:S(2)}, u32[]{:S(2)}) collective-permute-start(bf16[128,2048]{1,0:T(8,128)(2,1)S(1)} %maximum_select_fusion.10), channel_id=1, source_target_pairs={{0,2},{2,0},{4,6},{6,4},{8,10},{10,8},{12,14},{14,12},{16,18},{18,... | collective-permute-start | bytes 1572872 | tf_op jit(solution)/shard_map/ppermute | solution.py:455
  241.7 8.7 %collective-permute-start.33 = (bf16[64,2432]{1,0:T(8,128)(2,1)S(1)}, bf16[64,2432]{1,0:T(8,128)(2,1)S(1)}, u32[]{:S(2)}, u32[]{:S(2)}) collective-permute-start(bf16[64,2432]{1,0:T(8,128)(2,1)S(1)} %maximum_select_fusion.14), channel_id=1, source_target_pairs={{0,4},{2,6},{4,0},{6,2},{8,12},{10,14},{12,8},{14,10},{16,20},{18,... | collective-permute-start | bytes 933896 | tf_op jit(solution)/shard_map/ppermute | solution.py:455
  248.7 10.3 %collective-permute-start.42 = (bf16[128,2432]{1,0:T(8,128)(2,1)S(1)}, bf16[128,2432]{1,0:T(8,128)(2,1)S(1)}, u32[]{:S(2)}, u32[]{:S(2)}) collective-permute-start(bf16[128,2432]{1,0:T(8,128)(2,1)S(1)} %maximum_select_fusion.9), channel_id=1, source_target_pairs={{0,4},{2,6},{4,0},{6,2},{8,12},{10,14},{12,8},{14,10},{16,20},{18,... | collective-permute-start | bytes 1867784 | tf_op jit(solution)/shard_map/ppermute | solution.py:455
  250.6 10.3 %collective-permute-start.34 = (bf16[128,2432]{1,0:T(8,128)(2,1)S(1)}, bf16[128,2432]{1,0:T(8,128)(2,1)S(1)}, u32[]{:S(2)}, u32[]{:S(2)}) collective-permute-start(bf16[128,2432]{1,0:T(8,128)(2,1)S(1)} %maximum_select_fusion.8), channel_id=1, source_target_pairs={{0,2},{2,0},{4,6},{6,4},{8,10},{10,8},{12,14},{14,12},{16,18},{18,... | collective-permute-start | bytes 1867784 | tf_op jit(solution)/shard_map/ppermute | solution.py:455
  (44 other events, 279.6 us)

commit v2 on v1

--- a/solution.py
+++ b/solution.py
@@ -17,6 +17,8 @@
 GROUP = 4
 WIDE = GROUP * HEADDIM
 STEPS = HEADS // GROUP
+QUARTERS = 4
+LATE = INNER // QUARTERS + NSTATE
 LANES = 128
 
 epsilon = 1e-05
@@ -108,7 +110,7 @@
 
 
 def logistic(value):
-    return 1.0 / (1.0 + jnp.exp(-value))
+    return 0.5 * jnp.tanh(0.5 * value) + 0.5
 
 
 def head_columns(table, step):
@@ -149,7 +151,7 @@
 
 def forward_kernel(
     len_ref, raw_ref, head_ref, sig_ref, bc_ref, gate_ref, grad_ref, par_ref, parbc_ref, gain_ref,
-    gated_ref, dgate_ref, dheads_ref, heads_ref, conv_ref, convbc_ref, gaing_ref,
+    gated_ref, dgate_ref, sent_ref, dheads_ref, heads_ref, conv_ref, convbc_ref, gaing_ref,
     joined, step_s, run_s, runt_s, score_s, cross_s, u_s, silu_s, slope_s, grad_s, sq_s, mix_s,
 ):
     step = pl.program_id(0)
@@ -214,22 +216,29 @@
     @pl.when(step == STEPS - 1)
     def finish():
         scale = lax.rsqrt(jnp.sum(sq_s[...], axis=1, keepdims=True) * (1.0 / INNER) + epsilon)
+        rows = scale.shape[0]
         drag = scale * scale * scale * (jnp.sum(mix_s[...], axis=1, keepdims=True) * (1.0 / INNER))
         for part in range(STEPS):
             lanes = slice(part * WIDE, (part + 1) * WIDE)
             gain = gain_ref[:, lanes]
             normal = u_s[part] * scale
             grad = grad_s[part]
-            gated_ref[:, lanes] = (normal * gain).astype(bf16)
+            gated = (normal * gain).astype(bf16)
+            gated_ref[:, lanes] = gated
+            core, place = part // QUARTERS, part % QUARTERS
+            sent_ref[place, rows:, core * WIDE : (core + 1) * WIDE] = gated
             gaing_ref[:, lanes] = jnp.sum(grad * normal, axis=0, keepdims=True)
             du = scale * (grad * gain) - u_s[part] * drag
             dheads_ref[:, lanes] = du * silu_s[part]
-            dgate_ref[:, lanes] = (du * slope_s[part]).astype(bf16)
+            dgate = (du * slope_s[part]).astype(bf16)
+            dgate_ref[:, lanes] = dgate
+            half = part % 2
+            sent_ref[part // 2, :rows, half * WIDE : (half + 1) * WIDE] = dgate
 
 
 def backward_kernel(
     len_ref, raw_ref, head_ref, sig_ref, bc_ref, conv_ref, convbc_ref, dheads_ref, heads_ref, par_ref, parbc_ref,
-    dx_ref, dr_ref, parg_ref, parbcg_ref, headg_ref,
+    dx_ref, dr_ref, late_ref, parg_ref, parbcg_ref, headg_ref,
     joined, step_s, run_s, runt_s, maps_s, score_s, cross_s, dscore_s, dcross_s, dstep_s, ddecay_s,
 ):
     step = pl.program_id(0)
@@ -305,7 +314,9 @@
     store(5, jnp.zeros((1, WIDE), f32))
     store(6, jnp.sum(dheads * head_in, axis=0, keepdims=True))
     store(7, jnp.zeros((1, WIDE), f32))
-    dx_ref[...] = conv_back(dhead_in * slope, sig_ref[...], par, joined, store).astype(bf16)
+    dx = conv_back(dhead_in * slope, sig_ref[...], par, joined, store).astype(bf16)
+    dx_ref[...] = dx
+    late_ref[step // 2, :, pl.ds(pl.multiple_of(lax.rem(step, 2) * WIDE, WIDE), WIDE)] = dx
 
     @pl.when(step == STEPS - 1)
     def finish():
@@ -331,7 +342,10 @@
         for row in (5, 6, 7):
             store(row, jnp.zeros((1, WIDE), f32))
         grad = jnp.concatenate([dwrite, dread], axis=1) * slope
-        dr_ref[:, :WIDE] = conv_back(grad, bc_ref[...], parbc_ref[...], joined, store).astype(bf16)
+        dmaps = conv_back(grad, bc_ref[...], parbc_ref[...], joined, store).astype(bf16)
+        dr_ref[:, :WIDE] = dmaps
+        late_ref[0, :, 2 * WIDE :] = dmaps[:, :NSTATE]
+        late_ref[1, :, 2 * WIDE :] = dmaps[:, NSTATE:]
 
         shifted, step_size, rate, decay = step_terms(raw_ref, head_ref)
         change = ddecay_s[...]
@@ -342,6 +356,8 @@
         lane = lax.broadcasted_iota(jnp.int32, dshifted.shape, 1)
         dshifted = jnp.where(lane < HEADS, dshifted, 0.0)
         dr_ref[:, WIDE:] = dshifted.astype(bf16)
+        late_ref[2, :, 2 * WIDE :] = dshifted.astype(bf16)
+        late_ref[3, :, 2 * WIDE :] = jnp.zeros_like(dshifted, bf16)
         headg_ref[...] = jnp.zeros_like(headg_ref)
         headg_ref[0:1, :] = jnp.sum(dshifted, axis=0, keepdims=True)
         headg_ref[1:2, :] = jnp.sum(decay * ddecay, axis=0, keepdims=True)
@@ -363,8 +379,8 @@
     return jax.ShapeDtypeStruct((rows, cols), dtype)
 
 
-def params():
-    return pltpu.CompilerParams(dimension_semantics=("arbitrary",), vmem_limit_bytes=48 * 1024 * 1024)
+def params(mebibytes):
+    return pltpu.CompilerParams(dimension_semantics=("arbitrary",), vmem_limit_bytes=mebibytes * 1024 * 1024)
 
 
 def run_forward(lengths, raw, head, projected, gated_grad, par, gain):
@@ -387,11 +403,12 @@
             whole((1, INNER)),
         ],
         out_specs=[
-            whole((rows, INNER)), whole((rows, INNER)), whole((rows, INNER)),
+            whole((rows, INNER)), whole((rows, INNER)), whole((QUARTERS, 2 * rows, 2 * WIDE)), whole((rows, INNER)),
             columns(rows), columns(rows), whole((rows, WIDE)), whole((1, INNER)),
         ],
         out_shape=[
-            shape(rows, INNER, bf16), shape(rows, INNER, bf16), shape(rows, INNER),
+            shape(rows, INNER, bf16), shape(rows, INNER, bf16),
+            jax.ShapeDtypeStruct((QUARTERS, 2 * rows, 2 * WIDE), bf16), shape(rows, INNER),
             shape(rows, INNER), shape(rows, INNER), shape(rows, WIDE), shape(1, INNER),
         ],
         scratch_shapes=[
@@ -400,8 +417,8 @@
             pltpu.VMEM((2, BLOCK, BLOCK), f32), pltpu.VMEM((BLOCK, BLOCK), bf16),
             state, state, state, state, narrow, narrow,
         ],
-        compiler_params=params(),
-        cost_estimate=pl.CostEstimate(flops=600_000_000, bytes_accessed=16_000_000, transcendentals=3_000_000),
+        compiler_params=params(28),
+        cost_estimate=pl.CostEstimate(flops=15_000_000_000, bytes_accessed=16_000_000, transcendentals=3_000_000),
         name="mixer_forward",
     )(lengths, raw, head, projected, projected, projected, gated_grad, par, par, gain)
 
@@ -424,65 +441,192 @@
             fixed_columns(8, INNER // WIDE),
         ],
         out_specs=[
-            columns(rows), whole((rows, WIDE + LANES)), columns(8), whole((8, WIDE)), whole((8, LANES)),
+            columns(rows), whole((rows, WIDE + LANES)), whole((QUARTERS, rows, LATE)), columns(8), whole((8, WIDE)), whole((8, LANES)),
         ],
         out_shape=[
-            shape(rows, INNER, bf16), shape(rows, WIDE + LANES, bf16), shape(8, INNER), shape(8, WIDE), shape(8, LANES),
+            shape(rows, INNER, bf16), shape(rows, WIDE + LANES, bf16),
+            jax.ShapeDtypeStruct((QUARTERS, rows, LATE), bf16), shape(8, INNER), shape(8, WIDE), shape(8, LANES),
         ],
         scratch_shapes=[
             pltpu.VMEM((CONV_WIDTH - 1, rows, LANES), f32),
             narrow, narrow, pltpu.VMEM((STEPS, 8, rows), f32), pltpu.VMEM((rows, WIDE), f32),
             square, pltpu.VMEM((BLOCK, BLOCK), bf16), square, pltpu.VMEM((BLOCK, BLOCK), f32), narrow, narrow,
         ],
-        compiler_params=params(),
-        cost_estimate=pl.CostEstimate(flops=1_500_000_000, bytes_accessed=16_000_000, transcendentals=3_000_000),
+        compiler_params=params(20),
+        cost_estimate=pl.CostEstimate(flops=20_000_000_000, bytes_accessed=16_000_000, transcendentals=3_000_000),
         name="mixer_backward",
     )(lengths, raw, head, projected, projected, conv, convbc, dheads, heads, par, par)
+
+
+def normalized(value, gain):
+    scale = lax.rsqrt(jnp.mean(value * value, axis=-1, keepdims=True) + epsilon)
+    return scale, (value * scale * gain).astype(bf16)
+
+
+def known_kernel(core_ref, gain_ref, first, second, third, fourth, mine_ref, theirs_ref, up_ref):
+    half = mine_ref.shape[1]
+    for at, ref in enumerate((first, second, third, fourth)):
+        count = ref.shape[0] // 2
+        rows = slice(at * count, (at + 1) * count)
+        unused, normed = normalized(ref[:count].astype(f32), gain_ref[...])
+        low, high = normed[:, :half], normed[:, half:]
+        is_first = core_ref[0] == 0
+        mine_ref[rows] = jnp.where(is_first, low, high)
+        theirs_ref[rows] = jnp.where(is_first, high, low)
+        up_ref[rows] = ref[count:]
+
+
+def run_known(core, gain, known):
+    count, model = known[0].shape[0] // 2, known[0].shape[1]
+    every = QUARTERS * count
+    return pl.pallas_call(
+        known_kernel,
+        in_specs=[pl.BlockSpec(memory_space=pltpu.SMEM)] + [pl.BlockSpec(memory_space=pltpu.VMEM)] * 5,
+        out_specs=[pl.BlockSpec(memory_space=pltpu.VMEM)] * 3,
+        out_shape=[shape(every, model // 2, bf16), shape(every, model // 2, bf16), shape(every, model, bf16)],
+        compiler_params=pltpu.CompilerParams(vmem_limit_bytes=32 * 1024 * 1024),
+        cost_estimate=pl.CostEstimate(flops=1, bytes_accessed=1, transcendentals=0),
+        name="known_rows",
+    )(core, gain, *known)
+
+
+def early_kernel(core_ref, first, second, third, fourth, send_ref, own_ref):
+    gate = 2 * WIDE
+    for at, ref in enumerate((first, second, third, fourth)):
+        count = ref.shape[0] // 2
+        rows = slice(at * count, (at + 1) * count)
+        low, high = ref[count:, :WIDE], ref[count:, WIDE:]
+        is_first = core_ref[0] == 0
+        send_ref[rows, :gate] = ref[:count]
+        send_ref[rows, gate:] = jnp.where(is_first, high, low)
+        own_ref[rows] = jnp.where(is_first, low, high)
+
+
+def run_early(core, got):
+    every = QUARTERS * got[0].shape[0] // 2
+    return pl.pallas_call(
+        early_kernel,
+        in_specs=[pl.BlockSpec(memory_space=pltpu.SMEM)] + [pl.BlockSpec(memory_space=pltpu.VMEM)] * 4,
+        out_specs=[pl.BlockSpec(memory_space=pltpu.VMEM)] * 2,
+        out_shape=[shape(every, 3 * WIDE, bf16), shape(every, WIDE, bf16)],
+        compiler_params=pltpu.CompilerParams(vmem_limit_bytes=32 * 1024 * 1024),
+        cost_estimate=pl.CostEstimate(flops=1, bytes_accessed=1, transcendentals=0),
+        name="early_factors",
+    )(core, *got)
+
+
+def finish_kernel(side_ref, base_ref, first, first_got, second, second_got, out_ref, rows_s, sems):
+    half = first.shape[0] // 2
+    body, wide_cols = half - NSTATE, 2 * WIDE
+    sizes = [wide_cols] * QUARTERS + [rows_s.shape[0] - INNER]
+    moves = [
+        pltpu.make_async_copy(
+            rows_s.at[pl.ds(at * wide_cols, size)], out_ref.at[pl.ds(INNER + at * wide_cols, size)], sems.at[at]
+        )
+        for at, size in enumerate(sizes)
+    ]
+    for place in range(QUARTERS):
+        x, y = place // 2, place % 2
+        top = slice(y * half, (y + 1) * half)
+        start = place * wide_cols
+        rows_s[start : start + half] = jnp.where(side_ref[0] == x, first[top], first_got[top]).astype(f32)
+        low = slice(x * half, (x + 1) * half)
+        value = jnp.where(side_ref[1] == y, second[low], second_got[low]).astype(f32)
+        rows_s[start + half : start + wide_cols] = value[:body]
+        keep = min(NSTATE, max(0, rows_s.shape[0] - INNER - place * NSTATE))
+        if keep:
+            rows_s[INNER + place * NSTATE : INNER + place * NSTATE + keep] = value[body : body + keep]
+        moves[place].start()
+    moves[QUARTERS].start()
+    for move in moves:
+        move.wait()
+
+
+def run_finish(sides, base, first, first_got, second, second_got):
+    late_rows = base.shape[0] - INNER
+    return pl.pallas_call(
+        finish_kernel,
+        in_specs=[pl.BlockSpec(memory_space=pltpu.SMEM), pl.BlockSpec(memory_space=pl.ANY)]
+        + [pl.BlockSpec(memory_space=pltpu.VMEM)] * 4,
+        out_specs=pl.BlockSpec(memory_space=pl.ANY),
+        out_shape=jax.ShapeDtypeStruct(base.shape, f32),
+        scratch_shapes=[pltpu.VMEM((late_rows, base.shape[1]), f32), pltpu.SemaphoreType.DMA((QUARTERS + 1,))],
+        input_output_aliases={1: 0},
+        compiler_params=pltpu.CompilerParams(vmem_limit_bytes=24 * 1024 * 1024),
+        cost_estimate=pl.CostEstimate(flops=1, bytes_accessed=8_000_000, transcendentals=0),
+        name="late_rows",
+    )(sides, base, first, first_got, second, second_got)
 
 
 def make_shards(mesh):
     reps = mesh.shape["rep"]
     bits = reps.bit_length() - 1
-    assert reps == 1 << bits and mesh.shape["shard"] == 2
-    one_way = tuple(range(bits))
-    turn = bits // 4 if bits >= 4 else min(1, bits)
-    other_way = one_way[turn : 2 * turn] + one_way[:turn] + one_way[2 * turn :]
+    assert reps == 1 << bits and bits >= 2 and mesh.shape["shard"] == 2
+    up_order, down_order = tuple(range(2, bits)), tuple(reversed(range(2, bits)))
+    far = len(up_order)
 
     def swap(value):
         return lax.ppermute(value, "shard", [(0, 1), (1, 0)])
 
-    def across(value, bit):
-        return lax.ppermute(value, "rep", [(place, place ^ (1 << bit)) for place in range(reps)])
-
-    def scatter_sum(value, order):
-        for bit in order:
-            half = value.shape[0] // 2
-            side = (lax.axis_index("rep") >> bit) & 1
-            leaving = lax.dynamic_slice_in_dim(value, (1 - side) * half, half).astype(bf16)
-            kept = lax.dynamic_slice_in_dim(value, side * half, half)
-            value = kept + across(leaving, bit).astype(f32)
-        return value.astype(bf16)
-
-    def gather(value, order):
-        for bit in reversed(order):
-            side = (lax.axis_index("rep") >> bit) & 1
-            value = joined(side, value, across(value, bit), 0)
-        return value
+    def across(value, flip):
+        return lax.ppermute(value, "rep", [(place, place ^ flip) for place in range(reps)])
+
+    def side_of(bit):
+        return (lax.axis_index("rep") >> bit) & 1
+
+    def quarter_of(flip):
+        place = lax.axis_index("rep") ^ flip
+        return (place & 1) * 2 + ((place >> 1) & 1)
 
     def joined(side, mine, theirs, axis):
         return jnp.where(
             side == 0, jnp.concatenate([mine, theirs], axis=axis), jnp.concatenate([theirs, mine], axis=axis)
         )
 
-    def summed_over_reps(value):
+    def part(value, bit, flip):
         half = value.shape[0] // 2
-        return jnp.concatenate(
-            [
-                gather(scatter_sum(value[:half], one_way), one_way),
-                gather(scatter_sum(value[half:], other_way), other_way),
-            ],
-            axis=0,
-        ).astype(f32)
+        return lax.dynamic_slice_in_dim(value, (side_of(bit) ^ flip) * half, half)
+
+    def terms(smalls):
+        high = lax.reduce_precision(smalls, 8, 7)
+        return jnp.concatenate([high.astype(bf16), (smalls - high).astype(bf16)], axis=0)
+
+    def exchange(value, bit, smalls):
+        if smalls is None:
+            return across(value, 1 << bit), None
+        rows, count = value.shape[0], smalls.shape[0]
+        got = across(jnp.concatenate([value, terms(smalls)], axis=0), 1 << bit)
+        added = got[rows:].astype(f32)
+        return got[:rows], smalls + added[:count] + added[count:]
+
+    def scatter(value, bit, smalls=None):
+        got, smalls = exchange(part(value, bit, 1).astype(bf16), bit, smalls)
+        return part(value, bit, 0) + got.astype(f32), smalls
+
+    def gather(value, bit, smalls=None):
+        got, smalls = exchange(value, bit, smalls)
+        return joined(side_of(bit), value, got, 0), smalls
+
+    def pair_step(pieces, at, smalls=None, carrier=1):
+        beside = [None, None]
+        beside[carrier] = smalls
+        moved = []
+        for which, value in enumerate(pieces):
+            order = (up_order, down_order)[which]
+            if at < far:
+                moved.append(scatter(value, order[at], beside[which]))
+            else:
+                value = value.astype(bf16) if at == far else value
+                late_at = at - 2 * far
+                bit = order[2 * far - 1 - at] if late_at < 0 else (1 - late_at, late_at)[which]
+                moved.append(gather(value, bit, beside[which]))
+        return tuple(value for value, _ in moved), moved[carrier][1]
+
+    steps = 2 * far + 2
+
+    def turned(value):
+        size = value.shape[0] // QUARTERS
+        return [value[at * size : (at + 1) * size] for at in (0, 2, 1, 3)]
 
     def shards(
         tokens, lengths, norm_gain, in_weight, conv_weight, conv_bias, step_bias, decay_log, skip_gain,
@@ -498,6 +642,11 @@
 
         def theirs(value, size):
             return lax.dynamic_slice_in_dim(value, (1 - core) * size, size, axis=1)
+
+        live = (jnp.arange(rows, dtype=jnp.int32) < jnp.sum(lengths))[:, None]
+        upstream = jnp.where(live, cotangent, jnp.zeros_like(cotangent))
+        known = jnp.concatenate([tokens, upstream], axis=0)
+        known = [known, *(across(known, flip) for flip in (1, 2, 3))]
 
         def line(value):
             return jnp.pad(value, (0, half_conv - value.shape[0]))[None]
@@ -534,41 +683,58 @@
         )
         head = jnp.pad(jnp.stack(head_lines[:2]), ((0, 6), (0, LANES - HEADS)))
 
-        live = (jnp.arange(rows, dtype=jnp.int32) < jnp.sum(lengths))[:, None]
-        upstream = jnp.where(live, cotangent, jnp.zeros_like(cotangent))
-        up_pair = jnp.concatenate([upstream, swap(upstream)], axis=0)
         inputs = tokens.astype(f32)
-        scale = lax.rsqrt(jnp.mean(inputs * inputs, axis=-1, keepdims=True) + epsilon)
-        normed = (inputs * scale * norm_scale).astype(bf16)
+        scale, normed = normalized(inputs, norm_scale)
         normed_m, normed_o = mine(normed, half_model), theirs(normed, half_model)
-        normed_pair = jnp.concatenate([normed_m, swap(normed_o)], axis=0)
 
         gated_grad = joined(core, mm(upstream, out_weight, LANE), mm(upstream, out_other, LANE), 1)
         projected = mm(normed_m, in_weight) + mm(normed_o, in_other)
         raw = jnp.pad(projected[:, STEP_COL:], ((0, 0), (0, LANES - HEADS)))
-        gated, dgate, dheads, heads, conv, convbc, gain_g = run_forward(
+        gated, dgate, leaving, dheads, heads, conv, convbc, gain_g = run_forward(
             lengths, raw, head, projected, gated_grad, par, gate_line
         )
 
-        def pair_of(value):
-            return jnp.concatenate([value, swap(value)], axis=0)
-
+        def quarters(value):
+            return [lax.dynamic_index_in_dim(value, quarter_of(flip), 0, keepdims=False) for flip in range(QUARTERS)]
+
+        early_sent = quarters(leaving)
+        early_got = [early_sent[0], *(across(early_sent[flip], flip) for flip in (1, 2, 3))]
+        dx, dr, late, par_g, parbc_g, head_g = run_backward(
+            lengths, raw, head, projected, conv, convbc, dheads, heads, par
+        )
+
+        late_sent = quarters(late)
+        late_sent, known = lax.optimization_barrier((late_sent, known))
+        place = core.astype(jnp.int32)[None]
+        known_m, known_t, known_up = run_known(place, norm_scale[None], known)
+        known_o, known_up_o = swap(known_t), swap(known_up)
+        late_got = [late_sent[0], *(across(late_sent[flip], flip) for flip in (1, 2, 3))]
+        early_m, early_out_m = run_early(place, early_got)
+        early_o = swap(early_m)
+        gate_cols = 2 * WIDE
+        early = (
+            mm(early_out_m, known_up, ROWS) + mm(early_o[:, gate_cols:], known_up_o, ROWS),
+            mm(early_m[:, :gate_cols], known_m, ROWS) + mm(early_o[:, :gate_cols], known_o, ROWS),
+        )
+        early, gated, late_got = lax.optimization_barrier((early, gated, late_got))
+        early, _ = pair_step(early, 0)
         gated_m, gated_o = mine(gated, half_inner), theirs(gated, half_inner)
-        gated_pair = jnp.concatenate([gated_m, swap(gated_o)], axis=0)
-        out_grad = summed_over_reps(mm(gated_pair, up_pair, ROWS))
-        gate_grad = summed_over_reps(mm(normed_pair, pair_of(dgate), ROWS))
         branch = mm(gated_m, out_weight) + mm(gated_o, out_other)
         output = (inputs + jnp.where(live, branch, 0.0)).astype(bf16)
-
-        dx, dr, par_g, parbc_g, head_g = run_backward(
-            lengths, raw, head, projected, conv, convbc, dheads, heads, par
-        )
-        late = jnp.concatenate([dx, dr], axis=1)
-        late_grad = summed_over_reps(mm(normed_pair, pair_of(late), ROWS))
-        in_grad = jnp.concatenate([gate_grad, late_grad[:, : STEP_COL + HEADS - INNER]], axis=1)
-
-        proj_grad = jnp.concatenate([dgate, late[:, : STEP_COL + HEADS - INNER]], axis=1)
-        normed_grad = joined(core, mm(proj_grad, in_weight, LANE), mm(proj_grad, in_other, LANE), 1)
+        late_all = jnp.concatenate(late_got, axis=0)
+        late_all_o = swap(late_all)
+
+        early, dx, dr, dgate, late_all, output = lax.optimization_barrier((early, dx, dr, dgate, late_all, output))
+        early, _ = pair_step(early, 1)
+        late_grad = mm(late_all, known_m, ROWS) + mm(late_all_o, known_o, ROWS)
+        late_tail = dr[:, : CONVDIM - INNER + HEADS]
+        proj_grad = jnp.concatenate([dgate, dx, late_tail], axis=1)
+        early, late_grad, proj_grad = lax.optimization_barrier((early, late_grad, proj_grad))
+        early, _ = pair_step(early, 2)
+        normed_grad_m = mm(proj_grad, in_weight, LANE)
+        early, normed_grad_m, proj_grad = lax.optimization_barrier((early, normed_grad_m, proj_grad))
+        early, _ = pair_step(early, 3)
+        normed_grad = joined(core, normed_grad_m, mm(proj_grad, in_other, LANE), 1)
         g = normed_grad * norm_scale
         input_grad = (
             cotangent.astype(f32)
@@ -588,25 +754,51 @@
             ],
             axis=0,
         )
-        total = total + swap(total)
-        for bit in one_way:
-            total = total + across(total, bit)
+        smalls = (total + swap(total)).reshape(-1, half_model)
+        early, late_grad, input_grad, smalls = lax.optimization_barrier((early, late_grad, input_grad, smalls))
+        half_late = LATE // 2
+        late_parts = (late_grad[:half_late], late_grad[half_late:])
+        last = 2 * far + 1
+        last = 2 * far + 1
+        for at in range(4, steps):
+            early, smalls = pair_step(early, at, smalls) if at == last - 1 else (pair_step(early, at)[0], smalls)
+            for late_at in {last - 1: range(1), last: range(1, 2 * far)}.get(at, ()):
+                if 1 <= late_at < far or late_at == 2 * far - 1:
+                    late_parts, smalls = pair_step(late_parts, late_at, smalls)
+                else:
+                    late_parts, _ = pair_step(late_parts, late_at)
+            if at >= last - 1:
+                early, late_parts = lax.optimization_barrier((early, late_parts))
+        late_parts, smalls = pair_step(late_parts, steps - 2, smalls, 0)
+        out_grad = early[0].astype(f32)
+        late_parts, out_grad = lax.optimization_barrier((late_parts, out_grad))
+        in_grad = jnp.concatenate(
+            [*turned(early[1]), jnp.zeros((STEP_COL + HEADS - INNER, half_model), bf16)], axis=0
+        ).astype(f32)
+        total = smalls.reshape(total.shape)
 
         def own(row, start, size):
             return lax.dynamic_slice_in_dim(total[row], start + core * size, size)
 
-        return (
-            output,
-            input_grad,
+        small_grads = (
             own(6, 0, half_model),
-            in_grad,
             lax.dynamic_slice_in_dim(total[:4], core * half_conv, half_conv, axis=1).T,
             own(4, 0, half_conv),
             own(6, model, half_heads),
             own(6, model + HEADS, half_heads),
             own(6, model + 2 * HEADS, half_heads),
             own(5, 0, half_inner),
-            out_grad,
+        )
+        in_grad, small_grads = lax.optimization_barrier((in_grad, small_grads))
+        sides = jnp.stack([side_of(0), side_of(1)]).astype(jnp.int32)
+        in_grad = run_finish(
+            sides, in_grad, late_parts[0], across(late_parts[0], 1), late_parts[1], across(late_parts[1], 2)
+        ).T
+        norm_grad, conv_grad, bias_grad, step_grad, decay_grad, skip_grad, gate_grad = small_grads
+
+        return (
+            output, input_grad, norm_grad, in_grad, conv_grad, bias_grad, step_grad, decay_grad, skip_grad,
+            gate_grad, out_grad,
         )
 
     return shards

time: 295 us -> 238 us (0.81); the launches traced: 290 us -> 237 us
  starting transfers between devices: 73.7 us -> 45.5 us
  local copies, waits for them, and re-layouts: 25 us -> 13 us
  other arithmetic: 35.1 us -> 23.6 us
  waiting for transfers between devices: 92.3 us -> 81.6 us
  matrix products: 29.6 us -> 34.3 us
  Pallas kernels: 32.2 us -> 36.9 us
    ppermute x52 -> x33, starting transfers between devices: 71.4 us -> 43.8 us  [across(): lax.ppermute(value, 'rep', [(place, place ^ flip) for place in range(reps)])]
    concatenate x1 -> x6, other arithmetic: 18.9 us -> 1.6 us  [the longest x1 1.3 us: shards(): known = jnp.concatenate([tokens, upstream], axis=0)]
    ppermute x52 -> x33, waiting for transfers between devices: 90 us -> 81.6 us  [across(): lax.ppermute(value, 'rep', [(place, place ^ flip) for place in range(reps)])]
    unnamed x32 -> x69, local copies, waits for them, and re-layouts: 15.4 us -> 7.29 us
    pallas_call x0 -> x3, Pallas kernels: none -> 7.42 us  [the longest x1 3.26 us: run_known(): pl.pallas_call(known_kernel, in_specs=[pl.BlockSpec(memory_space=pltpu.SM...]
    convert_element_type x8 -> x16, other arithmetic: 2.73 us -> 8.78 us  [the longest x1 4.87 us: shards(): in_grad = jnp.concatenate([*turned(early[1]), jnp.zeros((STEP_COL + HEADS...]
    dot_general x11 -> x14, matrix products: 29.6 us -> 34.3 us  [mm(): lax.dot_general(left, right, (dims, ((), ())), precision=precision, prefe...]
    select_n x25 -> x15, other arithmetic: 4.71 us -> 6.1 us  [joined(): jnp.where(side == 0, jnp.concatenate([mine, theirs], axis=axis), jnp.conc...]
  transfers between devices with their start and end apart: 61 -> 41, of which waited for: 34 -> 25; matrix products, arithmetic and copies ran while one was open for 18% -> 25% of each run, Pallas kernels for 11% -> 14%
where the time goes in v2:
time: 238 us; the launch traced here: 237 us
  waiting for transfers between devices  81.6 us (34%)
  starting transfers between devices  45.5 us (19%)
  Pallas kernels  36.9 us (16%)
  matrix products  34.3 us (14%)
  other arithmetic  23.6 us (10%)
  local copies, waits for them, and re-layouts  13 us (5%)
    ppermute x33, waiting for transfers between devices, across(): lax.ppermute(value, 'rep', [(place, place ^ flip) for place in range(reps)])  81.6 us
    ppermute x33, starting transfers between devices, across(): lax.ppermute(value, 'rep', [(place, place ^ flip) for place in range(reps)])  43.8 us
    dot_general x14, matrix products, mm(): lax.dot_general(left, right, (dims, ((), ())), precision=precision, prefe...  34.3 us
    pallas_call x1, Pallas kernels, run_backward(): pl.pallas_call(backward_kernel, grid=(STEPS,), in_specs=[pl.BlockSpec(mem...  18.4 us
    pallas_call x1, Pallas kernels, run_forward(): pl.pallas_call(forward_kernel, grid=(STEPS,), in_specs=[pl.BlockSpec(memo...  11.1 us
    unnamed x69, local copies, waits for them, and re-layouts  7.29 us
    select_n x15, other arithmetic, joined(): jnp.where(side == 0, jnp.concatenate([mine, theirs], axis=axis), jnp.conc...  6.1 us
    convert_element_type x1, other arithmetic, shards(): in_grad = jnp.concatenate([*turned(early[1]), jnp.zeros((STEP_COL + HEADS...  4.87 us
  transfers between devices with their start and end apart: 41, of which 25 were waited for; matrix products, arithmetic and copies ran while one was open for 25% of the time, Pallas kernels for 14%

profile of v2, /device:TPU:0, one launch (start us, length us, event | category | flops | bytes accessed | tf_op | source)
XLA Modules:
  0.0 236.9 jit_solution(16727092090924458915)
XLA Ops:
  5.7 2.6 %collective-permute-start.6 = (bf16[512,1024]{1,0:T(8,128)(2,1)S(1)}, bf16[512,1024]{1,0:T(8,128)(2,1)S(1)}, u32[]{:S(2)}, u32[]{:S(2)}) collective-permute-start(bf16[512,1024]{1,0:T(8,128)(2,1)S(1)} %pad_maximum_fusion.1.first), channel_id=1, source_target_pairs={{0,2},{2,0},{4,6},{6,4},{8,10},{10,8},{12,14},{14,12},{16,18},{18,... | collective-permute-start | bytes 3145736 | tf_op jit(solution)/shard_map/ppermute | solution.py:572
  11.8 3.5 %fusion.47 = f32[256,1024]{1,0:T(8,128)} fusion(bf16[256,1024]{1,0:T(8,128)(2,1)} %copy-done.15, bf16[1024,1024]{1,0:T(8,128)(2,1)} %param.22), kind=kOutput, calls=%fused_computation.174 | convolution fusion | flops 536870912 | bytes 3670016 | tf_op jit(solution)/shard_map/dot_general | solution.py:31
  17.2 3.8 %fusion.18 = f32[256,4384]{1,0:T(8,128)S(1)} fusion(bf16[512,4384]{0,1:T(8,128)(2,1)} %param.15, bf16[256,1024]{1,0:T(8,128)(2,1)S(1)} %fusion.4, s32[]{:T(128)S(6)} %select_n.238), kind=kOutput, calls=%fused_computation.73 | convolution fusion | flops 1149239296 | bytes 9240580 | tf_op jit(solution)/shard_map/dot_general | solution.py:31
  23.9 3.7 %convolution_add_fusion.sig_ref.bc_ref.gate_ref = f32[256,4384]{1,0:T(8,128)S(1)} fusion(f32[256,4384]{1,0:T(8,128)S(1)} %fusion.18, bf16[512,4384]{0,1:T(8,128)(2,1)} %collective-permute-done.1, bf16[256,1024]{1,0:T(8,128)(2,1)S(1)} %fusion.4, s32[]{:T(128)S(6)} %select_n.239), kind=kOutput, calls=%fused_computation | convolution fusion | flops 1150361600 | bytes 13828100 | tf_op jit(solution)/shard_map/dot_general | solution.py:31
  27.6 11.1 %mixer_forward.1 = (bf16[256,2048]{1,0:T(8,128)(2,1)S(1)}, bf16[256,2048]{1,0:T(8,128)(2,1)S(1)}, bf16[4,512,512]{2,1,0:T(8,128)(2,1)S(1)}, f32[256,2048]{1,0:T(...) custom-call(s32[1,4]{1,0:T(1,128)S(1)} %copy-done.12, ...), custom_call_target="tpu_custom_call" | custom-call | flops 15000000512 | bytes 16000000 | tf_op jit(solution)/shard_map/mixer_forward/pallas_call | solution.py:390
  38.7 18.4 %mixer_backward.1 = (bf16[256,2048]{1,0:T(8,128)(2,1)S(1)}, bf16[256,384]{1,0:T(8,128)(2,1)S(1)}, bf16[4,256,640]{2,1,0:T(8,128)(2,1)S(1)}, f32[8,2048]{1,0:T(8,...) custom-call(s32[1,4]{1,0:T(1,128)S(1)} %copy-done.12, f32[256,128]{1,0:T(8,128)S(1)} %pad.32.raw_ref, ...), custom_call_target="tpu_custom_call" | custom-call | flops 20000000000 | bytes 16000000 | tf_op jit(solution)/shard_map/mixer_backward/pallas_call | solution.py:430
  65.8 3.3 %known_rows.1 = (bf16[1024,512]{1,0:T(8,128)(2,1)S(1)}, bf16[1024,512]{1,0:T(8,128)(2,1)}, bf16[1024,1024]{1,0:T(8,128)(2,1)S(1)}) custom-call(s32[1]{0:T(128)} %bitcast.core_ref, f32[1,1024]{1,0:T(1,128)S(1)} %bitcast.85, bf16[512,1024]{1,0:T(8,128)(2,1)S(1)} %pad_maximum_fusion.1.first, bf16[512,1024]{1,0:T(8,128)(2,1)S(1)} %copy-done.1, ...), custom_call_target="tpu_custom_call" | custom-call | flops 1 | bytes 1 | tf_op jit(solution)/shard_map/known_rows/pallas_call | solution.py:482
  70.0 4.6 %collective-permute-done.3.second = bf16[512,512]{1,0:T(8,128)(2,1)S(1)} collective-permute-done((bf16[512,512]{1,0:T(8,128)(2,1)S(1)}, bf16[512,512]{1,0:T(8,128)(2,1)S(1)}, u32[]{:S(2)}, u32[]{:S(2)}) %collective-permute-start.3) | collective-permute-done | bytes 524320 | tf_op jit(solution)/shard_map/ppermute | solution.py:572
  74.6 11.8 %collective-permute-done.4.third = bf16[512,512]{1,0:T(8,128)(2,1)S(1)} collective-permute-done((bf16[512,512]{1,0:T(8,128)(2,1)S(1)}, bf16[512,512]{1,0:T(8,128)(2,1)S(1)}, u32[]{:S(2)}, u32[]{:S(2)}) %collective-permute-start.4) | collective-permute-done | bytes 524320 | tf_op jit(solution)/shard_map/ppermute | solution.py:572
  92.0 2.5 %fusion.12 = f32[256,1024]{1,0:T(8,128)S(1)} fusion(bf16[1024,1024]{1,0:T(8,128)(2,1)} %collective-permute-done.10, bf16[1024,768]{1,0:T(8,128)(2,1)} %collective-permute-done.9), kind=kOutput, calls=%fused_computation.35 | convolution fusion | flops 536870912 | bytes 3670016 | tf_op jit(solution)/shard_map/dot_general | solution.py:31
  99.6 4.8 %collective-permute-done.13 = bf16[256,640]{1,0:T(8,128)(2,1)} collective-permute-done((bf16[256,640]{1,0:T(8,128)(2,1)}, bf16[256,640]{1,0:T(8,128)(2,1)}, u32[]{:S(2)}, u32[]{:S(2)}) %collective-permute-start.13) | collective-permute-done | bytes 327712 | tf_op jit(solution)/shard_map/ppermute | solution.py:572
  107.7 2.6 %collective-permute-start.16 = (bf16[256,512]{1,0:T(8,128)(2,1)S(1)}, bf16[256,512]{1,0:T(8,128)(2,1)S(1)}, u32[]{:S(2)}, u32[]{:S(2)}) collective-permute-start(bf16[256,512]{1,0:T(8,128)(2,1)S(1)} %dynamic-slice_convert_fusion), channel_id=1, source_target_pairs={{0,16},{2,18},{4,20},{6,22},{8,24},{10,26},{12,28},{14,30},{16,0},... | collective-permute-start | bytes 786440 | tf_op jit(solution)/shard_map/ppermute | solution.py:572
  118.9 2.6 %collective-permute-done.16 = bf16[256,512]{1,0:T(8,128)(2,1)S(1)} collective-permute-done((bf16[256,512]{1,0:T(8,128)(2,1)S(1)}, bf16[256,512]{1,0:T(8,128)(2,1)S(1)}, u32[]{:S(2)}, u32[]{:S(2)}) %collective-permute-start.16) | collective-permute-done | bytes 262176 | tf_op jit(solution)/shard_map/ppermute | solution.py:572
  121.8 2.9 %collective-permute-start.18 = (bf16[128,512]{1,0:T(8,128)(2,1)S(1)}, bf16[128,512]{1,0:T(8,128)(2,1)S(1)}, u32[]{:S(2)}, u32[]{:S(2)}) collective-permute-start(bf16[128,512]{1,0:T(8,128)(2,1)S(1)} %dynamic-slice_convert_fusion.4), channel_id=1, source_target_pairs={{0,8},{2,10},{4,12},{6,14},{8,0},{10,2},{12,4},{14,6},{16,24},{18,... | collective-permute-start | bytes 393224 | tf_op jit(solution)/shard_map/ppermute | solution.py:572
  125.7 3.3 %collective-permute-done.18 = bf16[128,512]{1,0:T(8,128)(2,1)S(1)} collective-permute-done((bf16[128,512]{1,0:T(8,128)(2,1)S(1)}, bf16[128,512]{1,0:T(8,128)(2,1)S(1)}, u32[]{:S(2)}, u32[]{:S(2)}) %collective-permute-start.18) | collective-permute-done | bytes 131104 | tf_op jit(solution)/shard_map/ppermute | solution.py:572
  129.2 3.3 %convolution_add_fusion.1 = f32[640,512]{1,0:T(8,128)} fusion(f32[640,512]{1,0:T(8,128)S(1)} %fusion.49, bf16[1024,640]{1,0:T(8,128)(2,1)S(1)} %collective-permute-done.19, bf16[1024,512]{1,0:T(8,128)(2,1)} %collective-permute-done.11), kind=kOutput, calls=%fused_computation.11 | convolution fusion | flops 671416320 | bytes 4980736 | tf_op jit(solution)/shard_map/dot_general | solution.py:31
  136.1 4.4 %collective-permute-done.20 = bf16[64,1024]{1,0:T(8,128)(2,1)S(1)} collective-permute-done((bf16[64,1024]{1,0:T(8,128)(2,1)S(1)}, bf16[64,1024]{1,0:T(8,128)(2,1)S(1)}, u32[]{:S(2)}, u32[]{:S(2)}) %collective-permute-start.20) | collective-permute-done | bytes 131104 | tf_op jit(solution)/shard_map/ppermute | solution.py:572
  140.6 3.0 %collective-permute-done.21 = bf16[128,512]{1,0:T(8,128)(2,1)S(1)} collective-permute-done((bf16[128,512]{1,0:T(8,128)(2,1)S(1)}, bf16[128,512]{1,0:T(8,128)(2,1)S(1)}, u32[]{:S(2)}, u32[]{:S(2)}) %collective-permute-start.21) | collective-permute-done | bytes 131104 | tf_op jit(solution)/shard_map/ppermute | solution.py:572
  143.7 2.8 %collective-permute-start.23 = (bf16[256,512]{1,0:T(8,128)(2,1)S(1)}, bf16[256,512]{1,0:T(8,128)(2,1)S(1)}, u32[]{:S(2)}, u32[]{:S(2)}) collective-permute-start(bf16[256,512]{1,0:T(8,128)(2,1)S(1)} %maximum_select_fusion.13), channel_id=1, source_target_pairs={{0,16},{2,18},{4,20},{6,22},{8,24},{10,26},{12,28},{14,30},{16,0},... | collective-permute-start | bytes 786440 | tf_op jit(solution)/shard_map/ppermute | solution.py:572
  146.5 3.7 %fusion.51 = f32[256,512]{1,0:T(8,128)S(1)} fusion(bf16[256,4384]{1,0:T(8,128)(2,1)S(1)} %pad_maximum_fusion, bf16[512,4384]{0,1:T(8,128)(2,1)} %collective-permute-done.1), kind=kOutput, calls=%fused_computation.178 | convolution fusion | flops 1149239296 | bytes 7258112 | tf_op jit(solution)/shard_map/dot_general | solution.py:31
  157.1 3.0 %collective-permute-start.28 = (bf16[160,512]{1,0:T(8,128)(2,1)S(1)}, bf16[160,512]{1,0:T(8,128)(2,1)S(1)}, u32[]{:S(2)}, u32[]{:S(2)}) collective-permute-start(bf16[160,512]{1,0:T(8,128)(2,1)S(1)} %dynamic-slice_convert_fusion.2), channel_id=1, source_target_pairs={{0,16},{2,18},{4,20},{6,22},{8,24},{10,26},{12,28},{14,30},{16,0},... | collective-permute-start | bytes 491528 | tf_op jit(solution)/shard_map/ppermute | solution.py:572
  161.8 4.6 %collective-permute-done.28 = bf16[160,512]{1,0:T(8,128)(2,1)S(1)} collective-permute-done((bf16[160,512]{1,0:T(8,128)(2,1)S(1)}, bf16[160,512]{1,0:T(8,128)(2,1)S(1)}, u32[]{:S(2)}, u32[]{:S(2)}) %collective-permute-start.28) | collective-permute-done | bytes 163872 | tf_op jit(solution)/shard_map/ppermute | solution.py:572
  174.1 3.3 %collective-permute-done.31 = bf16[80,512]{1,0:T(8,128)(2,1)S(1)} collective-permute-done((bf16[80,512]{1,0:T(8,128)(2,1)S(1)}, bf16[80,512]{1,0:T(8,128)(2,1)S(1)}, u32[]{:S(2)}, u32[]{:S(2)}) %collective-permute-start.31) | collective-permute-done | bytes 81952 | tf_op jit(solution)/shard_map/ppermute | solution.py:572
  182.9 2.9 %collective-permute-start.33 = (bf16[160,512]{1,0:T(8,128)(2,1)S(1)}, bf16[160,512]{1,0:T(8,128)(2,1)S(1)}, u32[]{:S(2)}, u32[]{:S(2)}) collective-permute-start(bf16[160,512]{1,0:T(8,128)(2,1)S(1)} %maximum_select_fusion.14), channel_id=1, source_target_pairs={{0,8},{2,10},{4,12},{6,14},{8,0},{10,2},{12,4},{14,6},{16,24},{18,... | collective-permute-start | bytes 491528 | tf_op jit(solution)/shard_map/ppermute | solution.py:572
  190.5 5.3 %collective-permute-done.36 = bf16[232,512]{1,0:T(8,128)(2,1)S(1)} collective-permute-done((bf16[232,512]{1,0:T(8,128)(2,1)S(1)}, bf16[232,512]{1,0:T(8,128)(2,1)S(1)}, u32[]{:S(2)}, u32[]{:S(2)}) %collective-permute-start.36) | collective-permute-done | bytes 237600 | tf_op jit(solution)/shard_map/ppermute | solution.py:572
  196.1 2.7 %maximum_select_fusion.1 = bf16[1024,1024]{1,0:T(8,128)(2,1)S(1)} fusion(bf16[512,1024]{1,0:T(8,128)(2,1)} %collective-permute-done.29, bf16[512,1024]{1,0:T(8,128)(2,1)S(1)} %maximum_select_fusion.4, pred[]{:T(512)S(6)} %eq.13), kind=kLoop, calls=%fused_computation.9 | loop fusion | flops 9437184 | bytes 4194305 | tf_op jit(solution)/shard_map/jit(_where)/select_n | solution.py:582
  198.8 11.8 %collective-permute-done.30 = bf16[1024,512]{1,0:T(8,128)(2,1)S(1)} collective-permute-done((bf16[1024,512]{1,0:T(8,128)(2,1)S(1)}, bf16[1024,512]{1,0:T(8,128)(2,1)S(1)}, u32[]{:S(2)}, u32[]{:S(2)}) %collective-permute-start.30) | collective-permute-done | bytes 1048608 | tf_op jit(solution)/shard_map/ppermute | solution.py:572
  212.3 4.9 %convert_element_type.168.base_ref = f32[4384,512]{1,0:T(8,128)} convert(bf16[4384,512]{1,0:T(8,128)(2,1)S(1)} %broadcast_dynamic-update-slice_fusion) | non-fusion elementwise | flops 2244608 | bytes 13467648 | tf_op jit(solution)/shard_map/convert_element_type | solution.py:777
  217.2 2.5 %convert_element_type.173 = f32[1024,1024]{1,0:T(8,128)} convert(bf16[1024,1024]{1,0:T(8,128)(2,1)S(1)} %maximum_select_fusion.1) | non-fusion elementwise | flops 1048576 | bytes 6291456 | tf_op jit(solution)/shard_map/convert_element_type | solution.py:773
  219.7 2.6 %collective-permute-done.38 = bf16[320,512]{1,0:T(8,128)(2,1)S(1)} collective-permute-done((bf16[320,512]{1,0:T(8,128)(2,1)S(1)}, bf16[320,512]{1,0:T(8,128)(2,1)S(1)}, u32[]{:S(2)}, u32[]{:S(2)}) %collective-permute-start.38) | collective-permute-done | bytes 327712 | tf_op jit(solution)/shard_map/ppermute | solution.py:572
  228.2 5.5 %collective-permute-done.39.first_got = bf16[640,512]{1,0:T(8,128)(2,1)S(1)} collective-permute-done((bf16[640,512]{1,0:T(8,128)(2,1)S(1)}, bf16[640,512]{1,0:T(8,128)(2,1)S(1)}, u32[]{:S(2)}, u32[]{:S(2)}) %collective-permute-start.39) | collective-permute-done | bytes 655392 | tf_op jit(solution)/shard_map/ppermute | solution.py:572
  233.8 2.9 %late_rows.1 = f32[4384,512]{1,0:T(8,128)} custom-call(s32[2]{0:T(128)S(1)} %pad_add_fusion.side_ref, f32[4384,512]{1,0:T(8,128)} %convert_element_type.168.base_ref, bf16[640,512]{1,0:T(8,128)(2,1)S(1)} %maximum_select_fusion.6.first, bf16[640,512]{1,0:T(8,128)(2,1)S(1)} %collective-permute-done.39.first_got, ...), custom_call_target="tpu_custom_call", output_to_operand_aliasing={{}: (1, {})} | custom-call | flops 1 | bytes 8000000 | tf_op jit(solution)/shard_map/late_rows/pallas_call | solution.py:547
  (252 shorter events, 84.4 us)
Async XLA Ops:
  0.7 23.2 %collective-permute-start.1 = (bf16[512,4384]{0,1:T(8,128)(2,1)}, bf16[512,4384]{0,1:T(8,128)(2,1)}, u32[]{:S(2)}, u32[]{:S(2)}) collective-permute-start(bf16[512,4384]{0,1:T(8,128)(2,1)} %param.15), channel_id=1, source_target_pairs={{0,1},{1,0},{2,3},{3,2},{4,5},{5,4},{6,7},{7,6},{8,9},{9,8},{10,11... | collective-permute-start | bytes 13467656 | tf_op jit(solution)/shard_map/ppermute | solution.py:569
  5.7 52.8 %collective-permute-start.6 = (bf16[512,1024]{1,0:T(8,128)(2,1)S(1)}, bf16[512,1024]{1,0:T(8,128)(2,1)S(1)}, u32[]{:S(2)}, u32[]{:S(2)}) collective-permute-start(bf16[512,1024]{1,0:T(8,128)(2,1)S(1)} %pad_maximum_fusion.1.first), channel_id=1, source_target_pairs={{0,2},{2,0},{4,6},{6,4},{8,10},{10,8},{12,14},{14,12},{16,18},{18,... | collective-permute-start | bytes 3145736 | tf_op jit(solution)/shard_map/ppermute | solution.py:572
  8.2 50.2 %collective-permute-start.7 = (bf16[512,1024]{1,0:T(8,128)(2,1)S(1)}, bf16[512,1024]{1,0:T(8,128)(2,1)S(1)}, u32[]{:S(2)}, u32[]{:S(2)}) collective-permute-start(bf16[512,1024]{1,0:T(8,128)(2,1)S(1)} %pad_maximum_fusion.1.first), channel_id=1, source_target_pairs={{0,4},{2,6},{4,0},{6,2},{8,12},{10,14},{12,8},{14,10},{16,20},{18,... | collective-permute-start | bytes 3145736 | tf_op jit(solution)/shard_map/ppermute | solution.py:572
  10.1 11.0 %collective-permute-start.2 = (bf16[1024,1024]{1,0:T(8,128)(2,1)}, bf16[1024,1024]{1,0:T(8,128)(2,1)}, u32[]{:S(2)}, u32[]{:S(2)}) collective-permute-start(bf16[1024,1024]{1,0:T(8,128)(2,1)} %param.22), channel_id=1, source_target_pairs={{0,1},{1,0},{2,3},{3,2},{4,5},{5,4},{6,7},{7,6},{8,9},{9,8},{10,11... | collective-permute-start | bytes 6291464 | tf_op jit(solution)/shard_map/ppermute | solution.py:569
  15.4 43.1 %collective-permute-start.8 = (bf16[512,1024]{1,0:T(8,128)(2,1)S(1)}, bf16[512,1024]{1,0:T(8,128)(2,1)}, u32[]{:S(2)}, u32[]{:S(2)}) collective-permute-start(bf16[512,1024]{1,0:T(8,128)(2,1)S(1)} %pad_maximum_fusion.1.first), channel_id=1, source_target_pairs={{0,6},{2,4},{4,2},{6,0},{8,14},{10,12},{12,10},{14,8},{16,22},{18,... | collective-permute-start | bytes 3145736 | tf_op jit(solution)/shard_map/ppermute | solution.py:572
  59.8 14.8 %collective-permute-start.3 = (bf16[512,512]{1,0:T(8,128)(2,1)S(1)}, bf16[512,512]{1,0:T(8,128)(2,1)S(1)}, u32[]{:S(2)}, u32[]{:S(2)}) collective-permute-start(bf16[512,512]{1,0:T(8,128)(2,1)S(1)} %get-tuple-element.167), channel_id=1, source_target_pairs={{0,2},{2,0},{4,6},{6,4},{8,10},{10,8},{12,14},{14,12},{16,18},{18,... | collective-permute-start | bytes 1572872 | tf_op jit(solution)/shard_map/ppermute | solution.py:572
  61.8 24.6 %collective-permute-start.4 = (bf16[512,512]{1,0:T(8,128)(2,1)S(1)}, bf16[512,512]{1,0:T(8,128)(2,1)S(1)}, u32[]{:S(2)}, u32[]{:S(2)}) collective-permute-start(bf16[512,512]{1,0:T(8,128)(2,1)S(1)} %get-tuple-element.166), channel_id=1, source_target_pairs={{0,4},{2,6},{4,0},{6,2},{8,12},{10,14},{12,8},{14,10},{16,20},{18,... | collective-permute-start | bytes 1572872 | tf_op jit(solution)/shard_map/ppermute | solution.py:572
  63.3 23.1 %collective-permute-start.5 = (bf16[512,512]{1,0:T(8,128)(2,1)S(1)}, bf16[512,512]{1,0:T(8,128)(2,1)S(1)}, u32[]{:S(2)}, u32[]{:S(2)}) collective-permute-start(bf16[512,512]{1,0:T(8,128)(2,1)S(1)} %get-tuple-element.165), channel_id=1, source_target_pairs={{0,6},{2,4},{4,2},{6,0},{8,14},{10,12},{12,10},{14,8},{16,22},{18,... | collective-permute-start | bytes 1572872 | tf_op jit(solution)/shard_map/ppermute | solution.py:572
  70.0 20.4 %collective-permute-start.10 = (bf16[1024,1024]{1,0:T(8,128)(2,1)S(1)}, bf16[1024,1024]{1,0:T(8,128)(2,1)}, u32[]{:S(2)}, u32[]{:S(2)}) collective-permute-start(bf16[1024,1024]{1,0:T(8,128)(2,1)S(1)} %get-tuple-element.95), channel_id=1, source_target_pairs={{0,1},{1,0},{2,3},{3,2},{4,5},{5,4},{6,7},{7,6},{8,9},{9,8},{10,11... | collective-permute-start | bytes 6291464 | tf_op jit(solution)/shard_map/ppermute | solution.py:569
  87.6 7.6 %collective-permute-start.11 = (bf16[1024,512]{1,0:T(8,128)(2,1)}, bf16[1024,512]{1,0:T(8,128)(2,1)}, u32[]{:S(2)}, u32[]{:S(2)}) collective-permute-start(bf16[1024,512]{1,0:T(8,128)(2,1)} %get-tuple-element.98), channel_id=1, source_target_pairs={{0,1},{1,0},{2,3},{3,2},{4,5},{5,4},{6,7},{7,6},{8,9},{9,8},{10,11... | collective-permute-start | bytes 3145736 | tf_op jit(solution)/shard_map/ppermute | solution.py:569
  88.1 11.5 %collective-permute-start.12 = (bf16[256,640]{1,0:T(8,128)(2,1)}, bf16[256,640]{1,0:T(8,128)(2,1)}, u32[]{:S(2)}, u32[]{:S(2)}) collective-permute-start(bf16[256,640]{1,0:T(8,128)(2,1)} %get-tuple-element.101), channel_id=1, source_target_pairs={{0,2},{2,0},{4,6},{6,4},{8,10},{10,8},{12,14},{14,12},{16,18},{18,... | collective-permute-start | bytes 983048 | tf_op jit(solution)/shard_map/ppermute | solution.py:572
  89.4 15.0 %collective-permute-start.13 = (bf16[256,640]{1,0:T(8,128)(2,1)}, bf16[256,640]{1,0:T(8,128)(2,1)}, u32[]{:S(2)}, u32[]{:S(2)}) collective-permute-start(bf16[256,640]{1,0:T(8,128)(2,1)} %get-tuple-element.102), channel_id=1, source_target_pairs={{0,4},{2,6},{4,0},{6,2},{8,12},{10,14},{12,8},{14,10},{16,20},{18,... | collective-permute-start | bytes 983048 | tf_op jit(solution)/shard_map/ppermute | solution.py:572
  90.4 15.5 %collective-permute-start.14 = (bf16[256,640]{1,0:T(8,128)(2,1)S(1)}, bf16[256,640]{1,0:T(8,128)(2,1)S(1)}, u32[]{:S(2)}, u32[]{:S(2)}) collective-permute-start(bf16[256,640]{1,0:T(8,128)(2,1)S(1)} %copy-done.21), channel_id=1, source_target_pairs={{0,6},{2,4},{4,2},{6,0},{8,14},{10,12},{12,10},{14,8},{16,22},{18,... | collective-permute-start | bytes 983048 | tf_op jit(solution)/shard_map/ppermute | solution.py:572
  106.0 12.8 %collective-permute-start.15 = (bf16[128,1024]{1,0:T(8,128)(2,1)S(1)}, bf16[128,1024]{1,0:T(8,128)(2,1)S(1)}, u32[]{:S(2)}, u32[]{:S(2)}) collective-permute-start(bf16[128,1024]{1,0:T(8,128)(2,1)S(1)} %dynamic-slice_convert_fusion.1), channel_id=1, source_target_pairs={{0,8},{2,10},{4,12},{6,14},{8,0},{10,2},{12,4},{14,6},{16,24},{18,... | collective-permute-start | bytes 786440 | tf_op jit(solution)/shard_map/ppermute | solution.py:572
  107.7 13.9 %collective-permute-start.16 = (bf16[256,512]{1,0:T(8,128)(2,1)S(1)}, bf16[256,512]{1,0:T(8,128)(2,1)S(1)}, u32[]{:S(2)}, u32[]{:S(2)}) collective-permute-start(bf16[256,512]{1,0:T(8,128)(2,1)S(1)} %dynamic-slice_convert_fusion), channel_id=1, source_target_pairs={{0,16},{2,18},{4,20},{6,22},{8,24},{10,26},{12,28},{14,30},{16,0},... | collective-permute-start | bytes 786440 | tf_op jit(solution)/shard_map/ppermute | solution.py:572
  112.5 16.7 %collective-permute-start.19 = (bf16[1024,640]{1,0:T(8,128)(2,1)S(1)}, bf16[1024,640]{1,0:T(8,128)(2,1)S(1)}, u32[]{:S(2)}, u32[]{:S(2)}) collective-permute-start(bf16[1024,640]{1,0:T(8,128)(2,1)S(1)} %constant_dynamic-update-slice_fusion), channel_id=1, source_target_pairs={{0,1},{1,0},{2,3},{3,2},{4,5},{5,4},{6,7},{7,6},{8,9},{9,8},{10,11... | collective-permute-start | bytes 3932168 | tf_op jit(solution)/shard_map/ppermute | solution.py:569
  121.6 7.4 %collective-permute-start.17 = (bf16[64,1024]{1,0:T(8,128)(2,1)S(1)}, bf16[64,1024]{1,0:T(8,128)(2,1)S(1)}, u32[]{:S(2)}, u32[]{:S(2)}) collective-permute-start(bf16[64,1024]{1,0:T(8,128)(2,1)S(1)} %dynamic-slice_convert_fusion.5), channel_id=1, source_target_pairs={{0,16},{2,18},{4,20},{6,22},{8,24},{10,26},{12,28},{14,30},{16,0},... | collective-permute-start | bytes 393224 | tf_op jit(solution)/shard_map/ppermute | solution.py:572
  132.5 8.0 %collective-permute-start.20 = (bf16[64,1024]{1,0:T(8,128)(2,1)S(1)}, bf16[64,1024]{1,0:T(8,128)(2,1)S(1)}, u32[]{:S(2)}, u32[]{:S(2)}) collective-permute-start(bf16[64,1024]{1,0:T(8,128)(2,1)S(1)} %convert_add_fusion.6), channel_id=1, source_target_pairs={{0,16},{2,18},{4,20},{6,22},{8,24},{10,26},{12,28},{14,30},{16,0},... | collective-permute-start | bytes 393224 | tf_op jit(solution)/shard_map/ppermute | solution.py:572
  133.1 10.4 %collective-permute-start.21 = (bf16[128,512]{1,0:T(8,128)(2,1)S(1)}, bf16[128,512]{1,0:T(8,128)(2,1)S(1)}, u32[]{:S(2)}, u32[]{:S(2)}) collective-permute-start(bf16[128,512]{1,0:T(8,128)(2,1)S(1)} %convert_add_fusion.5), channel_id=1, source_target_pairs={{0,8},{2,10},{4,12},{6,14},{8,0},{10,2},{12,4},{14,6},{16,24},{18,... | collective-permute-start | bytes 393224 | tf_op jit(solution)/shard_map/ppermute | solution.py:572
  143.6 9.0 %collective-permute-start.22 = (bf16[128,1024]{1,0:T(8,128)(2,1)S(1)}, bf16[128,1024]{1,0:T(8,128)(2,1)S(1)}, u32[]{:S(2)}, u32[]{:S(2)}) collective-permute-start(bf16[128,1024]{1,0:T(8,128)(2,1)S(1)} %maximum_select_fusion.12), channel_id=1, source_target_pairs={{0,8},{2,10},{4,12},{6,14},{8,0},{10,2},{12,4},{14,6},{16,24},{18,... | collective-permute-start | bytes 786440 | tf_op jit(solution)/shard_map/ppermute | solution.py:572
  143.7 10.2 %collective-permute-start.23 = (bf16[256,512]{1,0:T(8,128)(2,1)S(1)}, bf16[256,512]{1,0:T(8,128)(2,1)S(1)}, u32[]{:S(2)}, u32[]{:S(2)}) collective-permute-start(bf16[256,512]{1,0:T(8,128)(2,1)S(1)} %maximum_select_fusion.13), channel_id=1, source_target_pairs={{0,16},{2,18},{4,20},{6,22},{8,24},{10,26},{12,28},{14,30},{16,0},... | collective-permute-start | bytes 786440 | tf_op jit(solution)/shard_map/ppermute | solution.py:572
  154.1 13.0 %collective-permute-start.25 = (bf16[256,1024]{1,0:T(8,128)(2,1)S(1)}, bf16[256,1024]{1,0:T(8,128)(2,1)S(1)}, u32[]{:S(2)}, u32[]{:S(2)}) collective-permute-start(bf16[256,1024]{1,0:T(8,128)(2,1)S(1)} %maximum_select_fusion.8), channel_id=1, source_target_pairs={{0,4},{2,6},{4,0},{6,2},{8,12},{10,14},{12,8},{14,10},{16,20},{18,... | collective-permute-start | bytes 1572872 | tf_op jit(solution)/shard_map/ppermute | solution.py:572
  155.2 14.6 %collective-permute-start.26 = (bf16[584,512]{1,0:T(8,128)(2,1)S(1)}, bf16[584,512]{1,0:T(8,128)(2,1)S(1)}, u32[]{:S(2)}, u32[]{:S(2)}) collective-permute-start(bf16[584,512]{1,0:T(8,128)(2,1)S(1)} %pad_maximum_fusion.2), channel_id=1, source_target_pairs={{0,2},{2,0},{4,6},{6,4},{8,10},{10,8},{12,14},{14,12},{16,18},{18,... | collective-permute-start | bytes 1794056 | tf_op jit(solution)/shard_map/ppermute | solution.py:572
  157.1 9.3 %collective-permute-start.28 = (bf16[160,512]{1,0:T(8,128)(2,1)S(1)}, bf16[160,512]{1,0:T(8,128)(2,1)S(1)}, u32[]{:S(2)}, u32[]{:S(2)}) collective-permute-start(bf16[160,512]{1,0:T(8,128)(2,1)S(1)} %dynamic-slice_convert_fusion.2), channel_id=1, source_target_pairs={{0,16},{2,18},{4,20},{6,22},{8,24},{10,26},{12,28},{14,30},{16,0},... | collective-permute-start | bytes 491528 | tf_op jit(solution)/shard_map/ppermute | solution.py:572
  170.2 25.8 %collective-permute-start.29 = (bf16[512,1024]{1,0:T(8,128)(2,1)S(1)}, bf16[512,1024]{1,0:T(8,128)(2,1)}, u32[]{:S(2)}, u32[]{:S(2)}) collective-permute-start(bf16[512,1024]{1,0:T(8,128)(2,1)S(1)} %maximum_select_fusion.4), channel_id=1, source_target_pairs={{0,2},{2,0},{4,6},{6,4},{8,10},{10,8},{12,14},{14,12},{16,18},{18,... | collective-permute-start | bytes 3145736 | tf_op jit(solution)/shard_map/ppermute | solution.py:572
  182.9 7.5 %collective-permute-start.33 = (bf16[160,512]{1,0:T(8,128)(2,1)S(1)}, bf16[160,512]{1,0:T(8,128)(2,1)S(1)}, u32[]{:S(2)}, u32[]{:S(2)}) collective-permute-start(bf16[160,512]{1,0:T(8,128)(2,1)S(1)} %maximum_select_fusion.14), channel_id=1, source_target_pairs={{0,8},{2,10},{4,12},{6,14},{8,0},{10,2},{12,4},{14,6},{16,24},{18,... | collective-permute-start | bytes 491528 | tf_op jit(solution)/shard_map/ppermute | solution.py:572
  186.2 9.6 %collective-permute-start.36 = (bf16[232,512]{1,0:T(8,128)(2,1)S(1)}, bf16[232,512]{1,0:T(8,128)(2,1)S(1)}, u32[]{:S(2)}, u32[]{:S(2)}) collective-permute-start(bf16[232,512]{1,0:T(8,128)(2,1)S(1)} %pad_maximum_fusion.4), channel_id=1, source_target_pairs={{0,16},{2,18},{4,20},{6,22},{8,24},{10,26},{12,28},{14,30},{16,0},... | collective-permute-start | bytes 712712 | tf_op jit(solution)/shard_map/ppermute | solution.py:572
  188.2 22.3 %collective-permute-start.30 = (bf16[1024,512]{1,0:T(8,128)(2,1)S(1)}, bf16[1024,512]{1,0:T(8,128)(2,1)S(1)}, u32[]{:S(2)}, u32[]{:S(2)}) collective-permute-start(bf16[1024,512]{1,0:T(8,128)(2,1)S(1)} %maximum_select_fusion.5), channel_id=1, source_target_pairs={{0,4},{2,6},{4,0},{6,2},{8,12},{10,14},{12,8},{14,10},{16,20},{18,... | collective-permute-start | bytes 3145736 | tf_op jit(solution)/shard_map/ppermute | solution.py:572
  211.5 11.2 %collective-permute-start.37 = (bf16[392,512]{1,0:T(8,128)(2,1)S(1)}, bf16[392,512]{1,0:T(8,128)(2,1)S(1)}, u32[]{:S(2)}, u32[]{:S(2)}) collective-permute-start(bf16[392,512]{1,0:T(8,128)(2,1)S(1)} %pad_maximum_fusion.3), channel_id=1, source_target_pairs={{0,4},{2,6},{4,0},{6,2},{8,12},{10,14},{12,8},{14,10},{16,20},{18,... | collective-permute-start | bytes 1204232 | tf_op jit(solution)/shard_map/ppermute | solution.py:572
  211.8 10.5 %collective-permute-start.38 = (bf16[320,512]{1,0:T(8,128)(2,1)S(1)}, bf16[320,512]{1,0:T(8,128)(2,1)S(1)}, u32[]{:S(2)}, u32[]{:S(2)}) collective-permute-start(bf16[320,512]{1,0:T(8,128)(2,1)S(1)} %maximum_select_fusion.11), channel_id=1, source_target_pairs={{0,2},{2,0},{4,6},{6,4},{8,10},{10,8},{12,14},{14,12},{16,18},{18,... | collective-permute-start | bytes 983048 | tf_op jit(solution)/shard_map/ppermute | solution.py:572
  223.1 10.7 %collective-permute-start.39 = (bf16[640,512]{1,0:T(8,128)(2,1)S(1)}, bf16[640,512]{1,0:T(8,128)(2,1)S(1)}, u32[]{:S(2)}, u32[]{:S(2)}) collective-permute-start(bf16[640,512]{1,0:T(8,128)(2,1)S(1)} %maximum_select_fusion.6.first), channel_id=1, source_target_pairs={{0,2},{2,0},{4,6},{6,4},{8,10},{10,8},{12,14},{14,12},{16,18},{18,... | collective-permute-start | bytes 1966088 | tf_op jit(solution)/shard_map/ppermute | solution.py:572
  223.2 10.6 %collective-permute-start.40 = (bf16[640,512]{1,0:T(8,128)(2,1)S(1)}, bf16[640,512]{1,0:T(8,128)(2,1)S(1)}, u32[]{:S(2)}, u32[]{:S(2)}) collective-permute-start(bf16[640,512]{1,0:T(8,128)(2,1)S(1)} %maximum_select_fusion.7.second), channel_id=1, source_target_pairs={{0,4},{2,6},{4,0},{6,2},{8,12},{10,14},{12,8},{14,10},{16,20},{18,... | collective-permute-start | bytes 1966088 | tf_op jit(solution)/shard_map/ppermute | solution.py:572
  (40 other events, 252.5 us)

commit v3 on v2

--- a/solution.py
+++ b/solution.py
@@ -463,6 +463,29 @@
     return scale, (value * scale * gain).astype(bf16)
 
 
+def pack_kernel(len_ref, tokens_ref, cotangent_ref, out_ref):
+    rows = tokens_ref.shape[0]
+    out_ref[:rows] = tokens_ref[...]
+    places = lax.broadcasted_iota(jnp.int32, cotangent_ref.shape, 0)
+    total = len_ref[0, 0]
+    for slot in range(1, len_ref.shape[1]):
+        total = total + len_ref[0, slot]
+    out_ref[rows:] = jnp.where(places < total, cotangent_ref[...].astype(f32), 0.0).astype(bf16)
+
+
+def run_pack(lengths, tokens, cotangent):
+    rows, model = tokens.shape
+    return pl.pallas_call(
+        pack_kernel,
+        in_specs=[pl.BlockSpec(memory_space=pltpu.SMEM)] + [pl.BlockSpec(memory_space=pltpu.VMEM)] * 2,
+        out_specs=pl.BlockSpec(memory_space=pltpu.VMEM),
+        out_shape=shape(2 * rows, model, bf16),
+        compiler_params=pltpu.CompilerParams(vmem_limit_bytes=16 * 1024 * 1024),
+        cost_estimate=pl.CostEstimate(flops=1, bytes_accessed=2_000_000, transcendentals=0),
+        name="known_pack",
+    )(lengths, tokens, cotangent)
+
+
 def known_kernel(core_ref, gain_ref, first, second, third, fourth, mine_ref, theirs_ref, up_ref):
     half = mine_ref.shape[1]
     for at, ref in enumerate((first, second, third, fourth)):
@@ -643,9 +666,8 @@
         def theirs(value, size):
             return lax.dynamic_slice_in_dim(value, (1 - core) * size, size, axis=1)
 
-        live = (jnp.arange(rows, dtype=jnp.int32) < jnp.sum(lengths))[:, None]
-        upstream = jnp.where(live, cotangent, jnp.zeros_like(cotangent))
-        known = jnp.concatenate([tokens, upstream], axis=0)
+        known = run_pack(lengths, tokens, cotangent)
+        upstream = known[rows:]
         known = [known, *(across(known, flip) for flip in (1, 2, 3))]
 
         def line(value):
@@ -708,33 +730,12 @@
         place = core.astype(jnp.int32)[None]
         known_m, known_t, known_up = run_known(place, norm_scale[None], known)
         known_o, known_up_o = swap(known_t), swap(known_up)
-        late_got = [late_sent[0], *(across(late_sent[flip], flip) for flip in (1, 2, 3))]
-        early_m, early_out_m = run_early(place, early_got)
-        early_o = swap(early_m)
-        gate_cols = 2 * WIDE
-        early = (
-            mm(early_out_m, known_up, ROWS) + mm(early_o[:, gate_cols:], known_up_o, ROWS),
-            mm(early_m[:, :gate_cols], known_m, ROWS) + mm(early_o[:, :gate_cols], known_o, ROWS),
-        )
-        early, gated, late_got = lax.optimization_barrier((early, gated, late_got))
-        early, _ = pair_step(early, 0)
         gated_m, gated_o = mine(gated, half_inner), theirs(gated, half_inner)
         branch = mm(gated_m, out_weight) + mm(gated_o, out_other)
+        live = (jnp.arange(rows, dtype=jnp.int32) < jnp.sum(lengths))[:, None]
         output = (inputs + jnp.where(live, branch, 0.0)).astype(bf16)
-        late_all = jnp.concatenate(late_got, axis=0)
-        late_all_o = swap(late_all)
-
-        early, dx, dr, dgate, late_all, output = lax.optimization_barrier((early, dx, dr, dgate, late_all, output))
-        early, _ = pair_step(early, 1)
-        late_grad = mm(late_all, known_m, ROWS) + mm(late_all_o, known_o, ROWS)
-        late_tail = dr[:, : CONVDIM - INNER + HEADS]
-        proj_grad = jnp.concatenate([dgate, dx, late_tail], axis=1)
-        early, late_grad, proj_grad = lax.optimization_barrier((early, late_grad, proj_grad))
-        early, _ = pair_step(early, 2)
-        normed_grad_m = mm(proj_grad, in_weight, LANE)
-        early, normed_grad_m, proj_grad = lax.optimization_barrier((early, normed_grad_m, proj_grad))
-        early, _ = pair_step(early, 3)
-        normed_grad = joined(core, normed_grad_m, mm(proj_grad, in_other, LANE), 1)
+        proj_grad = jnp.concatenate([dgate, dx, dr[:, : CONVDIM - INNER + HEADS]], axis=1)
+        normed_grad = joined(core, mm(proj_grad, in_weight, LANE), mm(proj_grad, in_other, LANE), 1)
         g = normed_grad * norm_scale
         input_grad = (
             cotangent.astype(f32)
@@ -755,19 +756,35 @@
             axis=0,
         )
         smalls = (total + swap(total)).reshape(-1, half_model)
-        early, late_grad, input_grad, smalls = lax.optimization_barrier((early, late_grad, input_grad, smalls))
+        early_got, output, input_grad, smalls = lax.optimization_barrier((early_got, output, input_grad, smalls))
+        late_got = [late_sent[0], *(across(late_sent[flip], flip) for flip in (1, 2, 3))]
+        early_m, early_out_m = run_early(place, early_got)
+        early_o = swap(early_m)
+        gate_cols = 2 * WIDE
+        early = (
+            mm(early_out_m, known_up, ROWS) + mm(early_o[:, gate_cols:], known_up_o, ROWS),
+            mm(early_m[:, :gate_cols], known_m, ROWS) + mm(early_o[:, :gate_cols], known_o, ROWS),
+        )
+        early, _ = pair_step(early, 0)
+        early, _ = pair_step(early, 1)
+        early, late_got = lax.optimization_barrier((early, late_got))
+        early, _ = pair_step(early, 2)
+        late_all = jnp.concatenate(late_got, axis=0)
+        late_all_o = swap(late_all)
+        early, late_all, late_all_o = lax.optimization_barrier((early, late_all, late_all_o))
+        early, _ = pair_step(early, 3)
+        late_grad = mm(late_all, known_m, ROWS) + mm(late_all_o, known_o, ROWS)
+        early, late_grad = lax.optimization_barrier((early, late_grad))
         half_late = LATE // 2
         late_parts = (late_grad[:half_late], late_grad[half_late:])
         last = 2 * far + 1
         last = 2 * far + 1
         for at in range(4, steps):
             early, smalls = pair_step(early, at, smalls) if at == last - 1 else (pair_step(early, at)[0], smalls)
-            for late_at in {last - 1: range(1), last: range(1, 2 * far)}.get(at, ()):
-                if 1 <= late_at < far or late_at == 2 * far - 1:
-                    late_parts, smalls = pair_step(late_parts, late_at, smalls)
-                else:
-                    late_parts, _ = pair_step(late_parts, late_at)
-            if at >= last - 1:
+            for late_at in {last - 1: range(far), last: range(far, 2 * far)}.get(at, ()):
+                late_parts, added = pair_step(late_parts, late_at, smalls if late_at >= far else None)
+                smalls = smalls if added is None else added
+            if at >= last:
                 early, late_parts = lax.optimization_barrier((early, late_parts))
         late_parts, smalls = pair_step(late_parts, steps - 2, smalls, 0)
         out_grad = early[0].astype(f32)

time: 238 us -> 226 us (0.950)
  other arithmetic: 23.6 us -> 16.5 us
  waiting for transfers between devices: 81.6 us -> 76.7 us
  starting transfers between devices: 45.5 us -> 42 us
  Pallas kernels: 36.9 us -> 40.1 us
    ppermute x33, waiting for transfers between devices: 81.6 us -> 76.7 us  [across(): lax.ppermute(value, 'rep', [(place, place ^ flip) for place in range(reps)])]
    ppermute x33, starting transfers between devices: 43.8 us -> 39.9 us  [across(): lax.ppermute(value, 'rep', [(place, place ^ flip) for place in range(reps)])]
    unnamed x69 -> x63, local copies, waits for them, and re-layouts: 7.29 us -> 5.79 us
  transfers between devices with their start and end apart: 41 -> 41, of which waited for: 25 -> 21; matrix products, arithmetic and copies ran while one was open for 25% -> 25% of each run, Pallas kernels for 14% -> 17%
where the time goes in v3:
time: 226 us; the launch traced here: 225 us
  waiting for transfers between devices  76.7 us (34%)
  starting transfers between devices  42 us (19%)
  Pallas kernels  40.1 us (18%)
  matrix products  34.7 us (15%)
  other arithmetic  16.5 us (7%)
  local copies, waits for them, and re-layouts  13.2 us (6%)
    ppermute x33, waiting for transfers between devices, across(): lax.ppermute(value, 'rep', [(place, place ^ flip) for place in range(reps)])  76.7 us
    ppermute x33, starting transfers between devices, across(): lax.ppermute(value, 'rep', [(place, place ^ flip) for place in range(reps)])  39.9 us
    dot_general x14, matrix products, mm(): lax.dot_general(left, right, (dims, ((), ())), precision=precision, prefe...  34.7 us
    pallas_call x1, Pallas kernels, run_backward(): pl.pallas_call(backward_kernel, grid=(STEPS,), in_specs=[pl.BlockSpec(mem...  18.4 us
    pallas_call x1, Pallas kernels, run_forward(): pl.pallas_call(forward_kernel, grid=(STEPS,), in_specs=[pl.BlockSpec(memo...  11 us
    unnamed x63, local copies, waits for them, and re-layouts  5.79 us
    convert_element_type x1, other arithmetic, shards(): in_grad = jnp.concatenate([*turned(early[1]), jnp.zeros((STEP_COL + HEADS...  4.87 us
    pallas_call x1, Pallas kernels, run_known(): pl.pallas_call(known_kernel, in_specs=[pl.BlockSpec(memory_space=pltpu.SM...  4.67 us
  transfers between devices with their start and end apart: 41, of which 21 were waited for; matrix products, arithmetic and copies ran while one was open for 25% of the time, Pallas kernels for 17%

profile of v3, /device:TPU:0, one launch (start us, length us, event | category | flops | bytes accessed | tf_op | source)
XLA Modules:
  0.0 225.1 jit_solution(917817527418067084)
XLA Ops:
  4.6 2.6 %collective-permute-start.7 = (bf16[512,1024]{1,0:T(8,128)(2,1)S(1)}, bf16[512,1024]{1,0:T(8,128)(2,1)}, u32[]{:S(2)}, u32[]{:S(2)}) collective-permute-start(bf16[512,1024]{1,0:T(8,128)(2,1)S(1)} %known_pack.1.first), channel_id=1, source_target_pairs={{0,2},{2,0},{4,6},{6,4},{8,10},{10,8},{12,14},{14,12},{16,18},{18,... | collective-permute-start | bytes 3145736 | tf_op jit(solution)/shard_map/ppermute | solution.py:595
  14.3 3.7 %fusion.23 = f32[256,4384]{1,0:T(8,128)S(1)} fusion(bf16[512,4384]{0,1:T(8,128)(2,1)} %param.15, bf16[256,1024]{1,0:T(8,128)(2,1)S(1)} %fusion.4, s32[]{:T(128)S(6)} %select_n.234), kind=kOutput, calls=%fused_computation.76 | convolution fusion | flops 1149239296 | bytes 9240580 | tf_op jit(solution)/shard_map/dot_general | solution.py:31
  20.7 3.8 %convolution_add_fusion.sig_ref.bc_ref.gate_ref = f32[256,4384]{1,0:T(8,128)S(1)} fusion(f32[256,4384]{1,0:T(8,128)S(1)} %fusion.23, bf16[512,4384]{0,1:T(8,128)(2,1)} %collective-permute-done.1, bf16[256,1024]{1,0:T(8,128)(2,1)S(1)} %fusion.4, s32[]{:T(128)S(6)} %select_n.235), kind=kOutput, calls=%fused_computation | convolution fusion | flops 1150361600 | bytes 13828100 | tf_op jit(solution)/shard_map/dot_general | solution.py:31
  24.6 11.0 %mixer_forward.1 = (bf16[256,2048]{1,0:T(8,128)(2,1)S(1)}, bf16[256,2048]{1,0:T(8,128)(2,1)S(1)}, bf16[4,512,512]{2,1,0:T(8,128)(2,1)S(1)}, f32[256,2048]{1,0:T(...) custom-call(s32[1,4]{1,0:T(1,128)S(1)} %copy-done.7, ...), custom_call_target="tpu_custom_call" | custom-call | flops 15000000512 | bytes 16000000 | tf_op jit(solution)/shard_map/mixer_forward/pallas_call | solution.py:390
  40.5 18.4 %mixer_backward.1 = (bf16[256,2048]{1,0:T(8,128)(2,1)S(1)}, bf16[256,384]{1,0:T(8,128)(2,1)S(1)}, bf16[4,256,640]{2,1,0:T(8,128)(2,1)S(1)}, f32[8,2048]{1,0:T(8,...) custom-call(s32[1,4]{1,0:T(1,128)S(1)} %copy-done.7, f32[256,128]{1,0:T(8,128)S(1)} %pad.32.raw_ref, ...), custom_call_target="tpu_custom_call" | custom-call | flops 20000000000 | bytes 16000000 | tf_op jit(solution)/shard_map/mixer_backward/pallas_call | solution.py:430
  60.4 3.9 %fusion.12 = f32[256,512]{1,0:T(8,128)S(1)} fusion(bf16[512,4384]{0,1:T(8,128)(2,1)} %collective-permute-done.1, bf16[256,288]{1,0:T(8,128)(2,1)S(1)} %bitcast.86, bf16[256,2048]{1,0:T(8,128)(2,1)S(1)} %get-tuple-element.80, bf16[256,2048]{1,0:T(8,128)(2,1)S(1)} %get-tuple-element.75), kind=kOutput, calls=%fused_computation.31 | convolution fusion | flops 1155973120 | bytes 7258112 | tf_op jit(solution)/shard_map/dot_general | solution.py:31
  66.7 4.7 %known_rows.1 = (bf16[1024,512]{1,0:T(8,128)(2,1)S(1)}, bf16[1024,512]{1,0:T(8,128)(2,1)}, bf16[1024,1024]{1,0:T(8,128)(2,1)}) custom-call(s32[1]{0:T(128)} %bitcast.20.core_ref, f32[1,1024]{1,0:T(1,128)S(1)} %bitcast.80, bf16[512,1024]{1,0:T(8,128)(2,1)S(1)} %known_pack.1.first, bf16[512,1024]{1,0:T(8,128)(2,1)} %collective-permute-done.7.second, ...), custom_call_target="tpu_custom_call" | custom-call | flops 1 | bytes 1 | tf_op jit(solution)/shard_map/known_rows/pallas_call | solution.py:505
  72.6 3.3 %fusion.1 = bf16[256,1024]{1,0:T(8,128)(2,1)} fusion(f32[256,1024]{1,0:T(8,128)S(1)} %fusion.16, bf16[1024,1024]{1,0:T(8,128)(2,1)} %collective-permute-done.2, bf16[256,1024]{1,0:T(8,128)(2,1)S(1)} %copy-done.1, bf16[256,2048]{1,0:T(8,128)(2,1)S(1)} %copy-done.5, s32[]{:T(128)S(6)} %select_n.243, pred[256]{0:T(512)(128)(4,1)S(1)} %iota_compare_fusion.8), kind=kOutput, calls=%fused_computation.16 | convolution fusion | flops 538181632 | bytes 4719108 | tf_op jit(solution)/shard_map/dot_general | solution.py:31
  77.4 3.4 %collective-permute-done.5.fourth = bf16[512,512]{1,0:T(8,128)(2,1)S(1)} collective-permute-done((bf16[512,512]{1,0:T(8,128)(2,1)}, bf16[512,512]{1,0:T(8,128)(2,1)S(1)}, u32[]{:S(2)}, u32[]{:S(2)}) %collective-permute-start.5) | collective-permute-done | bytes 524320 | tf_op jit(solution)/shard_map/ppermute | solution.py:595
  80.8 2.5 %early_factors.1 = (bf16[1024,768]{1,0:T(8,128)(2,1)}, bf16[1024,256]{1,0:T(8,128)(2,1)S(1)}) custom-call(s32[1]{0:T(128)} %bitcast.20.core_ref, bf16[512,512]{1,0:T(8,128)(2,1)S(1)} %get-tuple-element.88.first, bf16[512,512]{1,0:T(8,128)(2,1)} %collective-permute-done.3.second, bf16[512,512]{1,0:T(8,128)(2,1)} %collective-permute-done.4.third, ...), custom_call_target="tpu_custom_call" | custom-call | flops 1 | bytes 1 | tf_op jit(solution)/shard_map/early_factors/pallas_call | solution.py:530
  89.0 2.7 %collective-permute-start.19 = (bf16[256,640]{1,0:T(8,128)(2,1)S(1)}, bf16[256,640]{1,0:T(8,128)(2,1)S(1)}, u32[]{:S(2)}, u32[]{:S(2)}) collective-permute-start(bf16[256,640]{1,0:T(8,128)(2,1)S(1)} %copy-done.16), channel_id=1, source_target_pairs={{0,6},{2,4},{4,2},{6,0},{8,14},{10,12},{12,10},{14,8},{16,22},{18,... | collective-permute-start | bytes 983048 | tf_op jit(solution)/shard_map/ppermute | solution.py:595
  94.0 2.7 %collective-permute-start.15 = (bf16[256,512]{1,0:T(8,128)(2,1)S(1)}, bf16[256,512]{1,0:T(8,128)(2,1)S(1)}, u32[]{:S(2)}, u32[]{:S(2)}) collective-permute-start(bf16[256,512]{1,0:T(8,128)(2,1)S(1)} %dynamic-slice_convert_fusion), channel_id=1, source_target_pairs={{0,16},{2,18},{4,20},{6,22},{8,24},{10,26},{12,28},{14,30},{16,0},... | collective-permute-start | bytes 786440 | tf_op jit(solution)/shard_map/ppermute | solution.py:595
  96.7 2.5 %convolution_add_fusion.3 = f32[256,1024]{1,0:T(8,128)S(1)} fusion(f32[256,1024]{1,0:T(8,128)S(1)} %fusion.54, bf16[1024,1024]{1,0:T(8,128)(2,1)} %collective-permute-done.11, bf16[1024,768]{1,0:T(8,128)(2,1)} %collective-permute-done.10), kind=kOutput, calls=%fused_computation.13 | convolution fusion | flops 537133056 | bytes 4718592 | tf_op jit(solution)/shard_map/dot_general | solution.py:31
  100.9 7.2 %collective-permute-done.15 = bf16[256,512]{1,0:T(8,128)(2,1)S(1)} collective-permute-done((bf16[256,512]{1,0:T(8,128)(2,1)S(1)}, bf16[256,512]{1,0:T(8,128)(2,1)S(1)}, u32[]{:S(2)}, u32[]{:S(2)}) %collective-permute-start.15) | collective-permute-done | bytes 262176 | tf_op jit(solution)/shard_map/ppermute | solution.py:595
  108.9 3.1 %collective-permute-done.12 = bf16[128,1024]{1,0:T(8,128)(2,1)S(1)} collective-permute-done((bf16[128,1024]{1,0:T(8,128)(2,1)S(1)}, bf16[128,1024]{1,0:T(8,128)(2,1)S(1)}, u32[]{:S(2)}, u32[]{:S(2)}) %collective-permute-start.12) | collective-permute-done | bytes 262176 | tf_op jit(solution)/shard_map/ppermute | solution.py:595
  112.5 2.6 %collective-permute-done.16 = bf16[128,512]{1,0:T(8,128)(2,1)S(1)} collective-permute-done((bf16[128,512]{1,0:T(8,128)(2,1)S(1)}, bf16[128,512]{1,0:T(8,128)(2,1)S(1)}, u32[]{:S(2)}, u32[]{:S(2)}) %collective-permute-start.16) | collective-permute-done | bytes 131104 | tf_op jit(solution)/shard_map/ppermute | solution.py:595
  115.2 4.4 %collective-permute-done.13 = bf16[64,1024]{1,0:T(8,128)(2,1)S(1)} collective-permute-done((bf16[64,1024]{1,0:T(8,128)(2,1)S(1)}, bf16[64,1024]{1,0:T(8,128)(2,1)S(1)}, u32[]{:S(2)}, u32[]{:S(2)}) %collective-permute-start.13) | collective-permute-done | bytes 131104 | tf_op jit(solution)/shard_map/ppermute | solution.py:595
  124.8 6.5 %collective-permute-done.20 = bf16[64,1024]{1,0:T(8,128)(2,1)S(1)} collective-permute-done((bf16[64,1024]{1,0:T(8,128)(2,1)S(1)}, bf16[64,1024]{1,0:T(8,128)(2,1)S(1)}, u32[]{:S(2)}, u32[]{:S(2)}) %collective-permute-start.20) | collective-permute-done | bytes 131104 | tf_op jit(solution)/shard_map/ppermute | solution.py:595
  131.9 2.6 %collective-permute-start.24 = (bf16[256,512]{1,0:T(8,128)(2,1)S(1)}, bf16[256,512]{1,0:T(8,128)(2,1)S(1)}, u32[]{:S(2)}, u32[]{:S(2)}) collective-permute-start(bf16[256,512]{1,0:T(8,128)(2,1)S(1)} %maximum_select_fusion.13), channel_id=1, source_target_pairs={{0,16},{2,18},{4,20},{6,22},{8,24},{10,26},{12,28},{14,30},{16,0},... | collective-permute-start | bytes 786440 | tf_op jit(solution)/shard_map/ppermute | solution.py:595
  138.8 6.2 %collective-permute-done.23 = bf16[128,1024]{1,0:T(8,128)(2,1)S(1)} collective-permute-done((bf16[128,1024]{1,0:T(8,128)(2,1)S(1)}, bf16[128,1024]{1,0:T(8,128)(2,1)S(1)}, u32[]{:S(2)}, u32[]{:S(2)}) %collective-permute-start.23) | collective-permute-done | bytes 262176 | tf_op jit(solution)/shard_map/ppermute | solution.py:595
  148.3 2.7 %collective-permute-start.33 = (bf16[160,512]{1,0:T(8,128)(2,1)S(1)}, bf16[160,512]{1,0:T(8,128)(2,1)S(1)}, u32[]{:S(2)}, u32[]{:S(2)}) collective-permute-start(bf16[160,512]{1,0:T(8,128)(2,1)S(1)} %dynamic-slice_convert_fusion.2), channel_id=1, source_target_pairs={{0,16},{2,18},{4,20},{6,22},{8,24},{10,26},{12,28},{14,30},{16,0},... | collective-permute-start | bytes 491528 | tf_op jit(solution)/shard_map/ppermute | solution.py:595
  151.0 3.4 %collective-permute-done.29 = bf16[160,512]{1,0:T(8,128)(2,1)S(1)} collective-permute-done((bf16[160,512]{1,0:T(8,128)(2,1)S(1)}, bf16[160,512]{1,0:T(8,128)(2,1)S(1)}, u32[]{:S(2)}, u32[]{:S(2)}) %collective-permute-start.29) | collective-permute-done | bytes 163872 | tf_op jit(solution)/shard_map/ppermute | solution.py:595
  155.3 4.6 %collective-permute-done.33 = bf16[160,512]{1,0:T(8,128)(2,1)S(1)} collective-permute-done((bf16[160,512]{1,0:T(8,128)(2,1)S(1)}, bf16[160,512]{1,0:T(8,128)(2,1)S(1)}, u32[]{:S(2)}, u32[]{:S(2)}) %collective-permute-start.33) | collective-permute-done | bytes 163872 | tf_op jit(solution)/shard_map/ppermute | solution.py:595
  168.7 2.7 %collective-permute-start.26 = (bf16[512,1024]{1,0:T(8,128)(2,1)S(1)}, bf16[512,1024]{1,0:T(8,128)(2,1)S(1)}, u32[]{:S(2)}, u32[]{:S(2)}) collective-permute-start(bf16[512,1024]{1,0:T(8,128)(2,1)S(1)} %maximum_select_fusion.4), channel_id=1, source_target_pairs={{0,2},{2,0},{4,6},{6,4},{8,10},{10,8},{12,14},{14,12},{16,18},{18,... | collective-permute-start | bytes 3145736 | tf_op jit(solution)/shard_map/ppermute | solution.py:595
  176.6 5.6 %collective-permute-done.36 = bf16[232,512]{1,0:T(8,128)(2,1)S(1)} collective-permute-done((bf16[232,512]{1,0:T(8,128)(2,1)S(1)}, bf16[232,512]{1,0:T(8,128)(2,1)S(1)}, u32[]{:S(2)}, u32[]{:S(2)}) %collective-permute-start.36) | collective-permute-done | bytes 237600 | tf_op jit(solution)/shard_map/ppermute | solution.py:595
  182.4 7.8 %collective-permute-done.26 = bf16[512,1024]{1,0:T(8,128)(2,1)S(1)} collective-permute-done((bf16[512,1024]{1,0:T(8,128)(2,1)S(1)}, bf16[512,1024]{1,0:T(8,128)(2,1)S(1)}, u32[]{:S(2)}, u32[]{:S(2)}) %collective-permute-start.26) | collective-permute-done | bytes 1048608 | tf_op jit(solution)/shard_map/ppermute | solution.py:595
  191.1 6.2 %collective-permute-done.28 = bf16[1024,512]{1,0:T(8,128)(2,1)S(1)} collective-permute-done((bf16[1024,512]{1,0:T(8,128)(2,1)S(1)}, bf16[1024,512]{1,0:T(8,128)(2,1)S(1)}, u32[]{:S(2)}, u32[]{:S(2)}) %collective-permute-start.28) | collective-permute-done | bytes 1048608 | tf_op jit(solution)/shard_map/ppermute | solution.py:595
  200.3 4.9 %convert_element_type.168.base_ref = f32[4384,512]{1,0:T(8,128)} convert(bf16[4384,512]{1,0:T(8,128)(2,1)S(1)} %broadcast_dynamic-update-slice_fusion) | non-fusion elementwise | flops 2244608 | bytes 13467648 | tf_op jit(solution)/shard_map/convert_element_type | solution.py:794
  205.2 2.5 %convert_element_type.173 = f32[1024,1024]{1,0:T(8,128)} convert(bf16[1024,1024]{1,0:T(8,128)(2,1)S(1)} %maximum_select_fusion.1) | non-fusion elementwise | flops 1048576 | bytes 6291456 | tf_op jit(solution)/shard_map/convert_element_type | solution.py:790
  207.6 2.8 %collective-permute-done.38 = bf16[320,512]{1,0:T(8,128)(2,1)S(1)} collective-permute-done((bf16[320,512]{1,0:T(8,128)(2,1)S(1)}, bf16[320,512]{1,0:T(8,128)(2,1)S(1)}, u32[]{:S(2)}, u32[]{:S(2)}) %collective-permute-start.38) | collective-permute-done | bytes 327712 | tf_op jit(solution)/shard_map/ppermute | solution.py:595
  215.5 6.2 %collective-permute-done.39.first_got = bf16[640,512]{1,0:T(8,128)(2,1)S(1)} collective-permute-done((bf16[640,512]{1,0:T(8,128)(2,1)S(1)}, bf16[640,512]{1,0:T(8,128)(2,1)S(1)}, u32[]{:S(2)}, u32[]{:S(2)}) %collective-permute-start.39) | collective-permute-done | bytes 655392 | tf_op jit(solution)/shard_map/ppermute | solution.py:595
  222.1 2.9 %late_rows.1 = f32[4384,512]{1,0:T(8,128)} custom-call(s32[2]{0:T(128)S(1)} %pad_add_fusion.side_ref, f32[4384,512]{1,0:T(8,128)} %convert_element_type.168.base_ref, bf16[640,512]{1,0:T(8,128)(2,1)S(1)} %maximum_select_fusion.6.first, bf16[640,512]{1,0:T(8,128)(2,1)S(1)} %collective-permute-done.39.first_got, ...), custom_call_target="tpu_custom_call", output_to_operand_aliasing={{}: (1, {})} | custom-call | flops 1 | bytes 8000000 | tf_op jit(solution)/shard_map/late_rows/pallas_call | solution.py:570
  (245 shorter events, 73.2 us)
Async XLA Ops:
  0.6 20.1 %collective-permute-start.1 = (bf16[512,4384]{0,1:T(8,128)(2,1)}, bf16[512,4384]{0,1:T(8,128)(2,1)}, u32[]{:S(2)}, u32[]{:S(2)}) collective-permute-start(bf16[512,4384]{0,1:T(8,128)(2,1)} %param.15), channel_id=1, source_target_pairs={{0,1},{1,0},{2,3},{3,2},{4,5},{5,4},{6,7},{7,6},{8,9},{9,8},{10,11... | collective-permute-start | bytes 13467656 | tf_op jit(solution)/shard_map/ppermute | solution.py:592
  4.6 61.9 %collective-permute-start.7 = (bf16[512,1024]{1,0:T(8,128)(2,1)S(1)}, bf16[512,1024]{1,0:T(8,128)(2,1)}, u32[]{:S(2)}, u32[]{:S(2)}) collective-permute-start(bf16[512,1024]{1,0:T(8,128)(2,1)S(1)} %known_pack.1.first), channel_id=1, source_target_pairs={{0,2},{2,0},{4,6},{6,4},{8,10},{10,8},{12,14},{14,12},{16,18},{18,... | collective-permute-start | bytes 3145736 | tf_op jit(solution)/shard_map/ppermute | solution.py:595
  7.2 59.4 %collective-permute-start.8 = (bf16[512,1024]{1,0:T(8,128)(2,1)S(1)}, bf16[512,1024]{1,0:T(8,128)(2,1)}, u32[]{:S(2)}, u32[]{:S(2)}) collective-permute-start(bf16[512,1024]{1,0:T(8,128)(2,1)S(1)} %known_pack.1.first), channel_id=1, source_target_pairs={{0,4},{2,6},{4,0},{6,2},{8,12},{10,14},{12,8},{14,10},{16,20},{18,... | collective-permute-start | bytes 3145736 | tf_op jit(solution)/shard_map/ppermute | solution.py:595
  9.1 9.0 %collective-permute-start.2 = (bf16[1024,1024]{1,0:T(8,128)(2,1)}, bf16[1024,1024]{1,0:T(8,128)(2,1)}, u32[]{:S(2)}, u32[]{:S(2)}) collective-permute-start(bf16[1024,1024]{1,0:T(8,128)(2,1)} %param.22), channel_id=1, source_target_pairs={{0,1},{1,0},{2,3},{3,2},{4,5},{5,4},{6,7},{7,6},{8,9},{9,8},{10,11... | collective-permute-start | bytes 6291464 | tf_op jit(solution)/shard_map/ppermute | solution.py:592
  13.5 53.2 %collective-permute-start.9 = (bf16[512,1024]{1,0:T(8,128)(2,1)S(1)}, bf16[512,1024]{1,0:T(8,128)(2,1)}, u32[]{:S(2)}, u32[]{:S(2)}) collective-permute-start(bf16[512,1024]{1,0:T(8,128)(2,1)S(1)} %known_pack.1.first), channel_id=1, source_target_pairs={{0,6},{2,4},{4,2},{6,0},{8,14},{10,12},{12,10},{14,8},{16,22},{18,... | collective-permute-start | bytes 3145736 | tf_op jit(solution)/shard_map/ppermute | solution.py:595
  37.1 40.3 %collective-permute-start.3 = (bf16[512,512]{1,0:T(8,128)(2,1)}, bf16[512,512]{1,0:T(8,128)(2,1)}, u32[]{:S(2)}, u32[]{:S(2)}) collective-permute-start(bf16[512,512]{1,0:T(8,128)(2,1)} %get-tuple-element.145), channel_id=1, source_target_pairs={{0,2},{2,0},{4,6},{6,4},{8,10},{10,8},{12,14},{14,12},{16,18},{18,... | collective-permute-start | bytes 1572872 | tf_op jit(solution)/shard_map/ppermute | solution.py:595
  39.0 38.4 %collective-permute-start.4 = (bf16[512,512]{1,0:T(8,128)(2,1)}, bf16[512,512]{1,0:T(8,128)(2,1)}, u32[]{:S(2)}, u32[]{:S(2)}) collective-permute-start(bf16[512,512]{1,0:T(8,128)(2,1)} %get-tuple-element.144), channel_id=1, source_target_pairs={{0,4},{2,6},{4,0},{6,2},{8,12},{10,14},{12,8},{14,10},{16,20},{18,... | collective-permute-start | bytes 1572872 | tf_op jit(solution)/shard_map/ppermute | solution.py:595
  66.5 14.2 %collective-permute-start.5 = (bf16[512,512]{1,0:T(8,128)(2,1)}, bf16[512,512]{1,0:T(8,128)(2,1)S(1)}, u32[]{:S(2)}, u32[]{:S(2)}) collective-permute-start(bf16[512,512]{1,0:T(8,128)(2,1)} %get-tuple-element.143), channel_id=1, source_target_pairs={{0,6},{2,4},{4,2},{6,0},{8,14},{10,12},{12,10},{14,8},{16,22},{18,... | collective-permute-start | bytes 1572872 | tf_op jit(solution)/shard_map/ppermute | solution.py:595
  66.6 10.6 %collective-permute-start.6 = (f32[8,2304]{1,0:T(8,128)S(1)}, f32[8,2304]{1,0:T(8,128)S(1)}, u32[]{:S(2)}, u32[]{:S(2)}) collective-permute-start(f32[8,2304]{1,0:T(8,128)S(1)} %fusion.30), channel_id=1, source_target_pairs={{0,1},{1,0},{2,3},{3,2},{4,5},{5,4},{6,7},{7,6},{8,9},{9,8},{10,11... | collective-permute-start | bytes 221192 | tf_op jit(solution)/shard_map/ppermute | solution.py:592
  71.4 25.3 %collective-permute-start.11 = (bf16[1024,1024]{1,0:T(8,128)(2,1)}, bf16[1024,1024]{1,0:T(8,128)(2,1)}, u32[]{:S(2)}, u32[]{:S(2)}) collective-permute-start(bf16[1024,1024]{1,0:T(8,128)(2,1)} %get-tuple-element.98), channel_id=1, source_target_pairs={{0,1},{1,0},{2,3},{3,2},{4,5},{5,4},{6,7},{7,6},{8,9},{9,8},{10,11... | collective-permute-start | bytes 6291464 | tf_op jit(solution)/shard_map/ppermute | solution.py:592
  83.3 8.4 %collective-permute-start.10 = (bf16[1024,768]{1,0:T(8,128)(2,1)}, bf16[1024,768]{1,0:T(8,128)(2,1)}, u32[]{:S(2)}, u32[]{:S(2)}) collective-permute-start(bf16[1024,768]{1,0:T(8,128)(2,1)} %get-tuple-element.99), channel_id=1, source_target_pairs={{0,1},{1,0},{2,3},{3,2},{4,5},{5,4},{6,7},{7,6},{8,9},{9,8},{10,11... | collective-permute-start | bytes 4718600 | tf_op jit(solution)/shard_map/ppermute | solution.py:592
  83.8 35.8 %collective-permute-start.17 = (bf16[256,640]{1,0:T(8,128)(2,1)S(1)}, bf16[256,640]{1,0:T(8,128)(2,1)S(1)}, u32[]{:S(2)}, u32[]{:S(2)}) collective-permute-start(bf16[256,640]{1,0:T(8,128)(2,1)S(1)} %copy-done.18), channel_id=1, source_target_pairs={{0,2},{2,0},{4,6},{6,4},{8,10},{10,8},{12,14},{14,12},{16,18},{18,... | collective-permute-start | bytes 983048 | tf_op jit(solution)/shard_map/ppermute | solution.py:595
  84.3 35.3 %collective-permute-start.18 = (bf16[256,640]{1,0:T(8,128)(2,1)S(1)}, bf16[256,640]{1,0:T(8,128)(2,1)S(1)}, u32[]{:S(2)}, u32[]{:S(2)}) collective-permute-start(bf16[256,640]{1,0:T(8,128)(2,1)S(1)} %copy-done.17), channel_id=1, source_target_pairs={{0,4},{2,6},{4,0},{6,2},{8,12},{10,14},{12,8},{14,10},{16,20},{18,... | collective-permute-start | bytes 983048 | tf_op jit(solution)/shard_map/ppermute | solution.py:595
  89.0 30.6 %collective-permute-start.19 = (bf16[256,640]{1,0:T(8,128)(2,1)S(1)}, bf16[256,640]{1,0:T(8,128)(2,1)S(1)}, u32[]{:S(2)}, u32[]{:S(2)}) collective-permute-start(bf16[256,640]{1,0:T(8,128)(2,1)S(1)} %copy-done.16), channel_id=1, source_target_pairs={{0,6},{2,4},{4,2},{6,0},{8,14},{10,12},{12,10},{14,8},{16,22},{18,... | collective-permute-start | bytes 983048 | tf_op jit(solution)/shard_map/ppermute | solution.py:595
  94.0 14.1 %collective-permute-start.15 = (bf16[256,512]{1,0:T(8,128)(2,1)S(1)}, bf16[256,512]{1,0:T(8,128)(2,1)S(1)}, u32[]{:S(2)}, u32[]{:S(2)}) collective-permute-start(bf16[256,512]{1,0:T(8,128)(2,1)S(1)} %dynamic-slice_convert_fusion), channel_id=1, source_target_pairs={{0,16},{2,18},{4,20},{6,22},{8,24},{10,26},{12,28},{14,30},{16,0},... | collective-permute-start | bytes 786440 | tf_op jit(solution)/shard_map/ppermute | solution.py:595
  99.2 12.8 %collective-permute-start.12 = (bf16[128,1024]{1,0:T(8,128)(2,1)S(1)}, bf16[128,1024]{1,0:T(8,128)(2,1)S(1)}, u32[]{:S(2)}, u32[]{:S(2)}) collective-permute-start(bf16[128,1024]{1,0:T(8,128)(2,1)S(1)} %dynamic-slice_convert_fusion.1), channel_id=1, source_target_pairs={{0,8},{2,10},{4,12},{6,14},{8,0},{10,2},{12,4},{14,6},{16,24},{18,... | collective-permute-start | bytes 786440 | tf_op jit(solution)/shard_map/ppermute | solution.py:595
  122.7 8.9 %collective-permute-start.22 = (bf16[1024,640]{1,0:T(8,128)(2,1)}, bf16[1024,640]{1,0:T(8,128)(2,1)S(1)}, u32[]{:S(2)}, u32[]{:S(2)}) collective-permute-start(bf16[1024,640]{1,0:T(8,128)(2,1)} %constant_dynamic-update-slice_fusion), channel_id=1, source_target_pairs={{0,1},{1,0},{2,3},{3,2},{4,5},{5,4},{6,7},{7,6},{8,9},{9,8},{10,11... | collective-permute-start | bytes 3932168 | tf_op jit(solution)/shard_map/ppermute | solution.py:592
  122.7 8.6 %collective-permute-start.20 = (bf16[64,1024]{1,0:T(8,128)(2,1)S(1)}, bf16[64,1024]{1,0:T(8,128)(2,1)S(1)}, u32[]{:S(2)}, u32[]{:S(2)}) collective-permute-start(bf16[64,1024]{1,0:T(8,128)(2,1)S(1)} %convert_add_fusion.6), channel_id=1, source_target_pairs={{0,16},{2,18},{4,20},{6,22},{8,24},{10,26},{12,28},{14,30},{16,0},... | collective-permute-start | bytes 393224 | tf_op jit(solution)/shard_map/ppermute | solution.py:595
  122.8 8.8 %collective-permute-start.21 = (bf16[128,512]{1,0:T(8,128)(2,1)S(1)}, bf16[128,512]{1,0:T(8,128)(2,1)S(1)}, u32[]{:S(2)}, u32[]{:S(2)}) collective-permute-start(bf16[128,512]{1,0:T(8,128)(2,1)S(1)} %convert_add_fusion.5), channel_id=1, source_target_pairs={{0,8},{2,10},{4,12},{6,14},{8,0},{10,2},{12,4},{14,6},{16,24},{18,... | collective-permute-start | bytes 393224 | tf_op jit(solution)/shard_map/ppermute | solution.py:595
  131.6 13.4 %collective-permute-start.23 = (bf16[128,1024]{1,0:T(8,128)(2,1)S(1)}, bf16[128,1024]{1,0:T(8,128)(2,1)S(1)}, u32[]{:S(2)}, u32[]{:S(2)}) collective-permute-start(bf16[128,1024]{1,0:T(8,128)(2,1)S(1)} %maximum_select_fusion.12), channel_id=1, source_target_pairs={{0,8},{2,10},{4,12},{6,14},{8,0},{10,2},{12,4},{14,6},{16,24},{18,... | collective-permute-start | bytes 786440 | tf_op jit(solution)/shard_map/ppermute | solution.py:595
  131.9 14.5 %collective-permute-start.24 = (bf16[256,512]{1,0:T(8,128)(2,1)S(1)}, bf16[256,512]{1,0:T(8,128)(2,1)S(1)}, u32[]{:S(2)}, u32[]{:S(2)}) collective-permute-start(bf16[256,512]{1,0:T(8,128)(2,1)S(1)} %maximum_select_fusion.13), channel_id=1, source_target_pairs={{0,16},{2,18},{4,20},{6,22},{8,24},{10,26},{12,28},{14,30},{16,0},... | collective-permute-start | bytes 786440 | tf_op jit(solution)/shard_map/ppermute | solution.py:595
  146.6 21.4 %collective-permute-start.25 = (bf16[256,1024]{1,0:T(8,128)(2,1)S(1)}, bf16[256,1024]{1,0:T(8,128)(2,1)S(1)}, u32[]{:S(2)}, u32[]{:S(2)}) collective-permute-start(bf16[256,1024]{1,0:T(8,128)(2,1)S(1)} %maximum_select_fusion.8), channel_id=1, source_target_pairs={{0,4},{2,6},{4,0},{6,2},{8,12},{10,14},{12,8},{14,10},{16,20},{18,... | collective-permute-start | bytes 1572872 | tf_op jit(solution)/shard_map/ppermute | solution.py:595
  147.7 17.8 %collective-permute-start.27 = (bf16[584,512]{1,0:T(8,128)(2,1)S(1)}, bf16[584,512]{1,0:T(8,128)(2,1)S(1)}, u32[]{:S(2)}, u32[]{:S(2)}) collective-permute-start(bf16[584,512]{1,0:T(8,128)(2,1)S(1)} %pad_maximum_fusion.3), channel_id=1, source_target_pairs={{0,2},{2,0},{4,6},{6,4},{8,10},{10,8},{12,14},{14,12},{16,18},{18,... | collective-permute-start | bytes 1794056 | tf_op jit(solution)/shard_map/ppermute | solution.py:595
  148.3 11.7 %collective-permute-start.33 = (bf16[160,512]{1,0:T(8,128)(2,1)S(1)}, bf16[160,512]{1,0:T(8,128)(2,1)S(1)}, u32[]{:S(2)}, u32[]{:S(2)}) collective-permute-start(bf16[160,512]{1,0:T(8,128)(2,1)S(1)} %dynamic-slice_convert_fusion.2), channel_id=1, source_target_pairs={{0,16},{2,18},{4,20},{6,22},{8,24},{10,26},{12,28},{14,30},{16,0},... | collective-permute-start | bytes 491528 | tf_op jit(solution)/shard_map/ppermute | solution.py:595
  166.4 10.1 %collective-permute-start.32 = (bf16[160,512]{1,0:T(8,128)(2,1)S(1)}, bf16[160,512]{1,0:T(8,128)(2,1)S(1)}, u32[]{:S(2)}, u32[]{:S(2)}) collective-permute-start(bf16[160,512]{1,0:T(8,128)(2,1)S(1)} %maximum_select_fusion.14), channel_id=1, source_target_pairs={{0,8},{2,10},{4,12},{6,14},{8,0},{10,2},{12,4},{14,6},{16,24},{18,... | collective-permute-start | bytes 491528 | tf_op jit(solution)/shard_map/ppermute | solution.py:595
  168.7 21.4 %collective-permute-start.26 = (bf16[512,1024]{1,0:T(8,128)(2,1)S(1)}, bf16[512,1024]{1,0:T(8,128)(2,1)S(1)}, u32[]{:S(2)}, u32[]{:S(2)}) collective-permute-start(bf16[512,1024]{1,0:T(8,128)(2,1)S(1)} %maximum_select_fusion.4), channel_id=1, source_target_pairs={{0,2},{2,0},{4,6},{6,4},{8,10},{10,8},{12,14},{14,12},{16,18},{18,... | collective-permute-start | bytes 3145736 | tf_op jit(solution)/shard_map/ppermute | solution.py:595
  172.6 9.6 %collective-permute-start.36 = (bf16[232,512]{1,0:T(8,128)(2,1)S(1)}, bf16[232,512]{1,0:T(8,128)(2,1)S(1)}, u32[]{:S(2)}, u32[]{:S(2)}) collective-permute-start(bf16[232,512]{1,0:T(8,128)(2,1)S(1)} %pad_maximum_fusion.5), channel_id=1, source_target_pairs={{0,16},{2,18},{4,20},{6,22},{8,24},{10,26},{12,28},{14,30},{16,0},... | collective-permute-start | bytes 712712 | tf_op jit(solution)/shard_map/ppermute | solution.py:595
  174.9 22.4 %collective-permute-start.28 = (bf16[1024,512]{1,0:T(8,128)(2,1)S(1)}, bf16[1024,512]{1,0:T(8,128)(2,1)S(1)}, u32[]{:S(2)}, u32[]{:S(2)}) collective-permute-start(bf16[1024,512]{1,0:T(8,128)(2,1)S(1)} %maximum_select_fusion.5), channel_id=1, source_target_pairs={{0,4},{2,6},{4,0},{6,2},{8,12},{10,14},{12,8},{14,10},{16,20},{18,... | collective-permute-start | bytes 3145736 | tf_op jit(solution)/shard_map/ppermute | solution.py:595
  198.2 12.5 %collective-permute-start.37 = (bf16[392,512]{1,0:T(8,128)(2,1)S(1)}, bf16[392,512]{1,0:T(8,128)(2,1)S(1)}, u32[]{:S(2)}, u32[]{:S(2)}) collective-permute-start(bf16[392,512]{1,0:T(8,128)(2,1)S(1)} %pad_maximum_fusion.4), channel_id=1, source_target_pairs={{0,4},{2,6},{4,0},{6,2},{8,12},{10,14},{12,8},{14,10},{16,20},{18,... | collective-permute-start | bytes 1204232 | tf_op jit(solution)/shard_map/ppermute | solution.py:595
  199.8 10.6 %collective-permute-start.38 = (bf16[320,512]{1,0:T(8,128)(2,1)S(1)}, bf16[320,512]{1,0:T(8,128)(2,1)S(1)}, u32[]{:S(2)}, u32[]{:S(2)}) collective-permute-start(bf16[320,512]{1,0:T(8,128)(2,1)S(1)} %maximum_select_fusion.11), channel_id=1, source_target_pairs={{0,2},{2,0},{4,6},{6,4},{8,10},{10,8},{12,14},{14,12},{16,18},{18,... | collective-permute-start | bytes 983048 | tf_op jit(solution)/shard_map/ppermute | solution.py:595
  211.1 10.7 %collective-permute-start.39 = (bf16[640,512]{1,0:T(8,128)(2,1)S(1)}, bf16[640,512]{1,0:T(8,128)(2,1)S(1)}, u32[]{:S(2)}, u32[]{:S(2)}) collective-permute-start(bf16[640,512]{1,0:T(8,128)(2,1)S(1)} %maximum_select_fusion.6.first), channel_id=1, source_target_pairs={{0,2},{2,0},{4,6},{6,4},{8,10},{10,8},{12,14},{14,12},{16,18},{18,... | collective-permute-start | bytes 1966088 | tf_op jit(solution)/shard_map/ppermute | solution.py:595
  211.5 10.6 %collective-permute-start.40 = (bf16[640,512]{1,0:T(8,128)(2,1)S(1)}, bf16[640,512]{1,0:T(8,128)(2,1)S(1)}, u32[]{:S(2)}, u32[]{:S(2)}) collective-permute-start(bf16[640,512]{1,0:T(8,128)(2,1)S(1)} %maximum_select_fusion.7.second), channel_id=1, source_target_pairs={{0,4},{2,6},{4,0},{6,2},{8,12},{10,14},{12,8},{14,10},{16,20},{18,... | collective-permute-start | bytes 1966088 | tf_op jit(solution)/shard_map/ppermute | solution.py:595
  (37 other events, 223.6 us)

commit v4 on v3

--- a/solution.py
+++ b/solution.py
@@ -20,6 +20,7 @@
 QUARTERS = 4
 LATE = INNER // QUARTERS + NSTATE
 LANES = 128
+HEAD_SUMS = 1024
 
 epsilon = 1e-05
 highest = lax.Precision.HIGHEST
@@ -238,8 +239,8 @@
 
 def backward_kernel(
     len_ref, raw_ref, head_ref, sig_ref, bc_ref, conv_ref, convbc_ref, dheads_ref, heads_ref, par_ref, parbc_ref,
-    dx_ref, dr_ref, late_ref, parg_ref, parbcg_ref, headg_ref,
-    joined, step_s, run_s, runt_s, maps_s, score_s, cross_s, dscore_s, dcross_s, dstep_s, ddecay_s,
+    gaing_ref, dx_ref, dr_ref, late_ref, total_ref,
+    joined, step_s, run_s, runt_s, maps_s, score_s, cross_s, dscore_s, dcross_s, dstep_s, ddecay_s, dskip_s,
 ):
     step = pl.program_id(0)
 
@@ -261,6 +262,9 @@
         dcross_s[...] = jnp.zeros_like(dcross_s)
         dstep_s[...] = jnp.zeros_like(dstep_s)
         ddecay_s[...] = jnp.zeros_like(ddecay_s)
+        dskip_s[...] = jnp.zeros_like(dskip_s)
+        total_ref[...] = jnp.zeros_like(total_ref)
+        total_ref[5:6, :INNER] = gaing_ref[...]
 
     par = par_ref[...]
     summed = conv_ref[...]
@@ -309,11 +313,10 @@
     dhead_in = jnp.concatenate(sizes, axis=1) * dscaled + par[6:7] * dheads
 
     def store(row, value):
-        parg_ref[row : row + 1, :] = value
-
-    store(5, jnp.zeros((1, WIDE), f32))
-    store(6, jnp.sum(dheads * head_in, axis=0, keepdims=True))
-    store(7, jnp.zeros((1, WIDE), f32))
+        total_ref[row : row + 1, pl.ds(pl.multiple_of(step * WIDE, WIDE), WIDE)] = value
+
+    dskip = jnp.broadcast_to(jnp.sum(dheads * head_in, axis=0, keepdims=True), (8, WIDE))
+    dskip_s[...] += mm(dskip, sums, precision=highest)
     dx = conv_back(dhead_in * slope, sig_ref[...], par, joined, store).astype(bf16)
     dx_ref[...] = dx
     late_ref[step // 2, :, pl.ds(pl.multiple_of(lax.rem(step, 2) * WIDE, WIDE), WIDE)] = dx
@@ -337,10 +340,8 @@
         slope = opened * (1.0 + summed * (1.0 - opened))
 
         def store(row, value):
-            parbcg_ref[row : row + 1, :] = value
-
-        for row in (5, 6, 7):
-            store(row, jnp.zeros((1, WIDE), f32))
+            total_ref[row : row + 1, INNER:] = value
+
         grad = jnp.concatenate([dwrite, dread], axis=1) * slope
         dmaps = conv_back(grad, bc_ref[...], parbc_ref[...], joined, store).astype(bf16)
         dr_ref[:, :WIDE] = dmaps
@@ -358,9 +359,13 @@
         dr_ref[:, WIDE:] = dshifted.astype(bf16)
         late_ref[2, :, 2 * WIDE :] = dshifted.astype(bf16)
         late_ref[3, :, 2 * WIDE :] = jnp.zeros_like(dshifted, bf16)
-        headg_ref[...] = jnp.zeros_like(headg_ref)
-        headg_ref[0:1, :] = jnp.sum(dshifted, axis=0, keepdims=True)
-        headg_ref[1:2, :] = jnp.sum(decay * ddecay, axis=0, keepdims=True)
+        head_sums = (
+            jnp.sum(dshifted, axis=0, keepdims=True),
+            jnp.sum(decay * ddecay, axis=0, keepdims=True),
+            dskip_s[0:1, :],
+        )
+        for at, sums_of in enumerate(head_sums):
+            total_ref[6:7, HEAD_SUMS + at * LANES : HEAD_SUMS + (at + 1) * LANES] = sums_of
 
 
 def whole(shape):
@@ -417,13 +422,13 @@
             pltpu.VMEM((2, BLOCK, BLOCK), f32), pltpu.VMEM((BLOCK, BLOCK), bf16),
             state, state, state, state, narrow, narrow,
         ],
-        compiler_params=params(28),
+        compiler_params=params(25),
         cost_estimate=pl.CostEstimate(flops=15_000_000_000, bytes_accessed=16_000_000, transcendentals=3_000_000),
         name="mixer_forward",
     )(lengths, raw, head, projected, projected, projected, gated_grad, par, par, gain)
 
 
-def run_backward(lengths, raw, head, projected, conv, convbc, dheads, heads, par):
+def run_backward(lengths, raw, head, projected, conv, convbc, dheads, heads, par, gain_g):
     rows = projected.shape[0]
     narrow = pltpu.VMEM((rows, LANES), f32)
     square = pltpu.VMEM((2, BLOCK, BLOCK), f32)
@@ -439,23 +444,25 @@
             columns(rows), whole((rows, WIDE)), columns(rows), columns(rows),
             columns(8),
             fixed_columns(8, INNER // WIDE),
+            whole((1, INNER)),
         ],
         out_specs=[
-            columns(rows), whole((rows, WIDE + LANES)), whole((QUARTERS, rows, LATE)), columns(8), whole((8, WIDE)), whole((8, LANES)),
+            columns(rows), whole((rows, WIDE + LANES)), whole((QUARTERS, rows, LATE)), whole((8, CONVDIM)),
         ],
         out_shape=[
             shape(rows, INNER, bf16), shape(rows, WIDE + LANES, bf16),
-            jax.ShapeDtypeStruct((QUARTERS, rows, LATE), bf16), shape(8, INNER), shape(8, WIDE), shape(8, LANES),
+            jax.ShapeDtypeStruct((QUARTERS, rows, LATE), bf16), shape(8, CONVDIM),
         ],
         scratch_shapes=[
             pltpu.VMEM((CONV_WIDTH - 1, rows, LANES), f32),
             narrow, narrow, pltpu.VMEM((STEPS, 8, rows), f32), pltpu.VMEM((rows, WIDE), f32),
             square, pltpu.VMEM((BLOCK, BLOCK), bf16), square, pltpu.VMEM((BLOCK, BLOCK), f32), narrow, narrow,
+            pltpu.VMEM((8, LANES), f32),
         ],
-        compiler_params=params(20),
+        compiler_params=params(12),
         cost_estimate=pl.CostEstimate(flops=20_000_000_000, bytes_accessed=16_000_000, transcendentals=3_000_000),
         name="mixer_backward",
-    )(lengths, raw, head, projected, projected, conv, convbc, dheads, heads, par, par)
+    )(lengths, raw, head, projected, projected, conv, convbc, dheads, heads, par, par, gain_g)
 
 
 def normalized(value, gain):
@@ -486,56 +493,76 @@
     )(lengths, tokens, cotangent)
 
 
-def known_kernel(core_ref, gain_ref, first, second, third, fourth, mine_ref, theirs_ref, up_ref):
-    half = mine_ref.shape[1]
+def known_kernel(gain_ref, first, second, third, fourth, normed_ref, up_ref):
     for at, ref in enumerate((first, second, third, fourth)):
         count = ref.shape[0] // 2
         rows = slice(at * count, (at + 1) * count)
-        unused, normed = normalized(ref[:count].astype(f32), gain_ref[...])
-        low, high = normed[:, :half], normed[:, half:]
-        is_first = core_ref[0] == 0
-        mine_ref[rows] = jnp.where(is_first, low, high)
-        theirs_ref[rows] = jnp.where(is_first, high, low)
+        unused, normed_ref[rows] = normalized(ref[:count].astype(f32), gain_ref[...])
         up_ref[rows] = ref[count:]
 
 
-def run_known(core, gain, known):
-    count, model = known[0].shape[0] // 2, known[0].shape[1]
-    every = QUARTERS * count
+def run_known(gain, known):
+    every, model = QUARTERS * known[0].shape[0] // 2, known[0].shape[1]
     return pl.pallas_call(
         known_kernel,
-        in_specs=[pl.BlockSpec(memory_space=pltpu.SMEM)] + [pl.BlockSpec(memory_space=pltpu.VMEM)] * 5,
-        out_specs=[pl.BlockSpec(memory_space=pltpu.VMEM)] * 3,
-        out_shape=[shape(every, model // 2, bf16), shape(every, model // 2, bf16), shape(every, model, bf16)],
-        compiler_params=pltpu.CompilerParams(vmem_limit_bytes=32 * 1024 * 1024),
+        in_specs=[pl.BlockSpec(memory_space=pltpu.VMEM)] * 5,
+        out_specs=[pl.BlockSpec(memory_space=pltpu.VMEM)] * 2,
+        out_shape=[shape(every, model, bf16)] * 2,
+        compiler_params=pltpu.CompilerParams(vmem_limit_bytes=24 * 1024 * 1024),
         cost_estimate=pl.CostEstimate(flops=1, bytes_accessed=1, transcendentals=0),
         name="known_rows",
-    )(core, gain, *known)
-
-
-def early_kernel(core_ref, first, second, third, fourth, send_ref, own_ref):
-    gate = 2 * WIDE
-    for at, ref in enumerate((first, second, third, fourth)):
-        count = ref.shape[0] // 2
-        rows = slice(at * count, (at + 1) * count)
-        low, high = ref[count:, :WIDE], ref[count:, WIDE:]
-        is_first = core_ref[0] == 0
-        send_ref[rows, :gate] = ref[:count]
-        send_ref[rows, gate:] = jnp.where(is_first, high, low)
-        own_ref[rows] = jnp.where(is_first, low, high)
-
-
-def run_early(core, got):
-    every = QUARTERS * got[0].shape[0] // 2
+    )(gain, *known)
+
+
+def parted(core_ref, low, high, mine_ref, theirs_ref):
+    is_first = core_ref[0] == 0
+    mine_ref[...] = jnp.where(is_first, low, high)
+    theirs_ref[...] = jnp.where(is_first, high, low).astype(bf16)
+
+
+def early_kernel(core_ref, normed_ref, up_ref, *refs):
+    got, (gate_ref, gate_o_ref, out_ref, out_o_ref) = refs[:QUARTERS], refs[QUARTERS:]
+    count = got[0].shape[0] // 2
+    gate = mm(jnp.concatenate([ref[:count] for ref in got], axis=0), normed_ref[...], ROWS)
+    half = gate_ref.shape[1]
+    parted(core_ref, gate[:, :half], gate[:, half:], gate_ref, gate_o_ref)
+    out = mm(jnp.concatenate([ref[count:] for ref in got], axis=0), up_ref[...], ROWS)
+    parted(core_ref, out[:WIDE], out[WIDE:], out_ref, out_o_ref)
+
+
+def run_early(core, normed, up, got):
+    model = normed.shape[1]
     return pl.pallas_call(
         early_kernel,
-        in_specs=[pl.BlockSpec(memory_space=pltpu.SMEM)] + [pl.BlockSpec(memory_space=pltpu.VMEM)] * 4,
+        in_specs=[pl.BlockSpec(memory_space=pltpu.SMEM)] + [pl.BlockSpec(memory_space=pltpu.VMEM)] * 6,
+        out_specs=[pl.BlockSpec(memory_space=pltpu.VMEM)] * 4,
+        out_shape=[
+            shape(2 * WIDE, model // 2), shape(2 * WIDE, model // 2, bf16), shape(WIDE, model), shape(WIDE, model, bf16),
+        ],
+        compiler_params=pltpu.CompilerParams(vmem_limit_bytes=24 * 1024 * 1024),
+        cost_estimate=pl.CostEstimate(flops=1, bytes_accessed=1, transcendentals=0),
+        name="early_products",
+    )(core, normed, up, *got)
+
+
+def late_kernel(core_ref, normed_ref, *refs):
+    got, (late_ref, late_o_ref) = refs[:QUARTERS], refs[QUARTERS:]
+    late = mm(jnp.concatenate([ref[...] for ref in got], axis=0), normed_ref[...], ROWS)
+    half = late_ref.shape[1]
+    parted(core_ref, late[:, :half], late[:, half:], late_ref, late_o_ref)
+
+
+def run_late(core, normed, got):
+    model = normed.shape[1]
+    return pl.pallas_call(
+        late_kernel,
+        in_specs=[pl.BlockSpec(memory_space=pltpu.SMEM)] + [pl.BlockSpec(memory_space=pltpu.VMEM)] * 5,
         out_specs=[pl.BlockSpec(memory_space=pltpu.VMEM)] * 2,
-        out_shape=[shape(every, 3 * WIDE, bf16), shape(every, WIDE, bf16)],
-        compiler_params=pltpu.CompilerParams(vmem_limit_bytes=32 * 1024 * 1024),
+        out_shape=[shape(LATE, model // 2), shape(LATE, model // 2, bf16)],
+        compiler_params=pltpu.CompilerParams(vmem_limit_bytes=24 * 1024 * 1024),
         cost_estimate=pl.CostEstimate(flops=1, bytes_accessed=1, transcendentals=0),
-        name="early_factors",
-    )(core, *got)
+        name="late_products",
+    )(core, normed, *got)
 
 
 def finish_kernel(side_ref, base_ref, first, first_got, second, second_got, out_ref, rows_s, sems):
@@ -721,15 +748,14 @@
 
         early_sent = quarters(leaving)
         early_got = [early_sent[0], *(across(early_sent[flip], flip) for flip in (1, 2, 3))]
-        dx, dr, late, par_g, parbc_g, head_g = run_backward(
-            lengths, raw, head, projected, conv, convbc, dheads, heads, par
+        dx, dr, late, total = run_backward(
+            lengths, raw, head, projected, conv, convbc, dheads, heads, par, gain_g
         )
 
         late_sent = quarters(late)
-        late_sent, known = lax.optimization_barrier((late_sent, known))
+        late_sent, known, dx, dr, dgate, gated = lax.optimization_barrier((late_sent, known, dx, dr, dgate, gated))
         place = core.astype(jnp.int32)[None]
-        known_m, known_t, known_up = run_known(place, norm_scale[None], known)
-        known_o, known_up_o = swap(known_t), swap(known_up)
+        known_normed, known_up = run_known(norm_scale[None], known)
         gated_m, gated_o = mine(gated, half_inner), theirs(gated, half_inner)
         branch = mm(gated_m, out_weight) + mm(gated_o, out_other)
         live = (jnp.arange(rows, dtype=jnp.int32) < jnp.sum(lengths))[:, None]
@@ -744,36 +770,21 @@
         )
         gain_grad = jnp.sum(normed_grad * inputs * scale, axis=0)
 
-        skip_g = jnp.sum(par_g[6].reshape(HEADS, HEADDIM), axis=1)
-        tail = jnp.concatenate([gain_grad, head_g[0, :HEADS], head_g[1, :HEADS], skip_g])
-        total = jnp.concatenate(
-            [
-                jnp.concatenate([par_g[:5], parbc_g[:5]], axis=1),
-                jnp.pad(gain_g, ((0, 0), (0, CONVDIM - INNER))),
-                jnp.pad(tail, (0, CONVDIM - tail.shape[0]))[None],
-                jnp.zeros((1, CONVDIM), f32),
-            ],
-            axis=0,
-        )
-        smalls = (total + swap(total)).reshape(-1, half_model)
-        early_got, output, input_grad, smalls = lax.optimization_barrier((early_got, output, input_grad, smalls))
+        total = lax.dynamic_update_slice(total, gain_grad[None], (6, 0))
+        early_got, output, input_grad, total = lax.optimization_barrier((early_got, output, input_grad, total))
         late_got = [late_sent[0], *(across(late_sent[flip], flip) for flip in (1, 2, 3))]
-        early_m, early_out_m = run_early(place, early_got)
-        early_o = swap(early_m)
-        gate_cols = 2 * WIDE
-        early = (
-            mm(early_out_m, known_up, ROWS) + mm(early_o[:, gate_cols:], known_up_o, ROWS),
-            mm(early_m[:, :gate_cols], known_m, ROWS) + mm(early_o[:, :gate_cols], known_o, ROWS),
-        )
+        gate_mine, gate_theirs, out_mine, out_theirs = run_early(place, known_normed, known_up, early_got)
+        early = (out_mine + swap(out_theirs).astype(f32), gate_mine + swap(gate_theirs).astype(f32))
         early, _ = pair_step(early, 0)
         early, _ = pair_step(early, 1)
-        early, late_got = lax.optimization_barrier((early, late_got))
+        early, late_got, total = lax.optimization_barrier((early, late_got, total))
+        smalls = (total + swap(total)).reshape(-1, half_model)
         early, _ = pair_step(early, 2)
-        late_all = jnp.concatenate(late_got, axis=0)
-        late_all_o = swap(late_all)
-        early, late_all, late_all_o = lax.optimization_barrier((early, late_all, late_all_o))
+        late_mine, late_theirs = run_late(place, known_normed, late_got)
+        late_theirs = swap(late_theirs)
+        early, late_mine, late_theirs = lax.optimization_barrier((early, late_mine, late_theirs))
         early, _ = pair_step(early, 3)
-        late_grad = mm(late_all, known_m, ROWS) + mm(late_all_o, known_o, ROWS)
+        late_grad = late_mine + late_theirs.astype(f32)
         early, late_grad = lax.optimization_barrier((early, late_grad))
         half_late = LATE // 2
         late_parts = (late_grad[:half_late], late_grad[half_late:])
@@ -801,9 +812,9 @@
             own(6, 0, half_model),
             lax.dynamic_slice_in_dim(total[:4], core * half_conv, half_conv, axis=1).T,
             own(4, 0, half_conv),
-            own(6, model, half_heads),
-            own(6, model + HEADS, half_heads),
-            own(6, model + 2 * HEADS, half_heads),
+            own(6, HEAD_SUMS, half_heads),
+            own(6, HEAD_SUMS + LANES, half_heads),
+            own(6, HEAD_SUMS + 2 * LANES, half_heads),
             own(5, 0, half_inner),
         )
         in_grad, small_grads = lax.optimization_barrier((in_grad, small_grads))

time: 226 us -> 219 us (0.969)
  matrix products: 34.7 us -> 23 us
  waiting for transfers between devices: 76.7 us -> 80.1 us
  other arithmetic: 16.5 us -> 18.9 us
  local copies, waits for them, and re-layouts: 13.2 us -> 10.9 us
    dot_general x14 -> x8, matrix products: 34.7 us -> 23 us  [mm(): lax.dot_general(left, right, (dims, ((), ())), precision=precision, prefe...]
    ppermute x33, waiting for transfers between devices: 76.7 us -> 80.1 us  [across(): lax.ppermute(value, 'rep', [(place, place ^ flip) for place in range(reps)])]
    unnamed x63 -> x68, local copies, waits for them, and re-layouts: 5.79 us -> 3.94 us
    pallas_call x1 -> x2, Pallas kernels: 4.67 us -> 4.12 us  [the longest x1 2.57 us: run_known(): pl.pallas_call(known_kernel, in_specs=[pl.BlockSpec(memory_space=pltpu.VM...]
  transfers between devices with their start and end apart: 41 -> 40, of which waited for: 21 -> 20; matrix products, arithmetic and copies ran while one was open for 25% -> 22% of each run, Pallas kernels for 17% -> 15%
where the time goes in v4:
time: 219 us
  waiting for transfers between devices  80.1 us (37%)
  starting transfers between devices  42.4 us (19%)
  Pallas kernels  41.3 us (19%)
  matrix products  23 us (11%)
  other arithmetic  18.9 us (9%)
  local copies, waits for them, and re-layouts  10.9 us (5%)
    ppermute x33, waiting for transfers between devices, across(): lax.ppermute(value, 'rep', [(place, place ^ flip) for place in range(reps)])  80.1 us
    ppermute x33, starting transfers between devices, across(): lax.ppermute(value, 'rep', [(place, place ^ flip) for place in range(reps)])  40.3 us
    dot_general x8, matrix products, mm(): lax.dot_general(left, right, (dims, ((), ())), precision=precision, prefe...  23 us
    pallas_call x1, Pallas kernels, run_backward(): pl.pallas_call(backward_kernel, grid=(STEPS,), in_specs=[pl.BlockSpec(mem...  18.4 us
    pallas_call x1, Pallas kernels, run_forward(): pl.pallas_call(forward_kernel, grid=(STEPS,), in_specs=[pl.BlockSpec(memo...  11 us
    convert_element_type x1, other arithmetic, shards(): in_grad = jnp.concatenate([*turned(early[1]), jnp.zeros((STEP_COL + HEADS...  4.87 us
  transfers between devices with their start and end apart: 40, of which 20 were waited for; matrix products, arithmetic and copies ran while one was open for 22% of the time, Pallas kernels for 15%

profile of v4, /device:TPU:0, one launch (start us, length us, event | category | flops | bytes accessed | tf_op | source)
XLA Modules:
  0.0 218.6 jit_solution(2266465175994797022)
XLA Ops:
  4.6 2.6 %collective-permute-start.6 = (bf16[512,1024]{1,0:T(8,128)(2,1)S(1)}, bf16[512,1024]{1,0:T(8,128)(2,1)S(1)}, u32[]{:S(2)}, u32[]{:S(2)}) collective-permute-start(bf16[512,1024]{1,0:T(8,128)(2,1)S(1)} %known_pack.1.first), channel_id=1, source_target_pairs={{0,2},{2,0},{4,6},{6,4},{8,10},{10,8},{12,14},{14,12},{16,18},{18,... | collective-permute-start | bytes 3145736 | tf_op jit(solution)/shard_map/ppermute | solution.py:622
  10.4 3.3 %fusion.16 = f32[256,1024]{1,0:T(8,128)} fusion(bf16[1024,1024]{1,0:T(8,128)(2,1)} %param.22, bf16[512,1024]{1,0:T(8,128)(2,1)S(1)} %known_pack.1.first), kind=kOutput, calls=%fused_computation.52 | convolution fusion | flops 536870912 | bytes 3670016 | tf_op jit(solution)/shard_map/dot_general | solution.py:32
  15.7 3.7 %fusion.19 = f32[256,4384]{1,0:T(8,128)S(1)} fusion(bf16[512,4384]{0,1:T(8,128)(2,1)} %param.15, bf16[256,1024]{1,0:T(8,128)(2,1)S(1)} %fusion.4, s32[]{:T(128)S(6)} %select_n.234), kind=kOutput, calls=%fused_computation.72 | convolution fusion | flops 1149239296 | bytes 9240580 | tf_op jit(solution)/shard_map/dot_general | solution.py:32
  19.5 2.4 %fusion.14 = f32[256,1024]{1,0:T(8,128)S(1)} fusion(bf16[1024,1024]{1,0:T(8,128)(2,1)} %collective-permute-done.2, bf16[512,1024]{1,0:T(8,128)(2,1)S(1)} %known_pack.1.first), kind=kOutput, calls=%fused_computation.50 | convolution fusion | flops 536870912 | bytes 3670016 | tf_op jit(solution)/shard_map/dot_general | solution.py:32
  22.2 3.7 %convolution_add_fusion.sig_ref.bc_ref.gate_ref = f32[256,4384]{1,0:T(8,128)S(1)} fusion(f32[256,4384]{1,0:T(8,128)S(1)} %fusion.19, bf16[512,4384]{0,1:T(8,128)(2,1)} %collective-permute-done.1, bf16[256,1024]{1,0:T(8,128)(2,1)S(1)} %fusion.4, s32[]{:T(128)S(6)} %select_n.235), kind=kOutput, calls=%fused_computation | convolution fusion | flops 1150361600 | bytes 13828100 | tf_op jit(solution)/shard_map/dot_general | solution.py:32
  26.0 11.0 %mixer_forward.1 = (bf16[256,2048]{1,0:T(8,128)(2,1)S(1)}, bf16[256,2048]{1,0:T(8,128)(2,1)S(1)}, bf16[4,512,512]{2,1,0:T(8,128)(2,1)S(1)}, f32[256,2048]{1,0:T(...) custom-call(s32[1,4]{1,0:T(1,128)S(1)} %copy-done.9, ...), custom_call_target="tpu_custom_call" | custom-call | flops 15000000512 | bytes 16000000 | tf_op jit(solution)/shard_map/mixer_forward/pallas_call | solution.py:395
  42.0 18.4 %mixer_backward.1 = (bf16[256,2048]{1,0:T(8,128)(2,1)S(1)}, bf16[256,384]{1,0:T(8,128)(2,1)S(1)}, bf16[4,256,640]{2,1,0:T(8,128)(2,1)S(1)}, f32[8,2304]{1,0:T(8,128)S(1)}) custom-call(s32[1,4]{1,0:T(1,128)S(1)} %copy-done.9, f32[256,128]{1,0:T(8,128)S(1)} %pad.25.raw_ref, f32[8,128]{1,0:T(8,128)S(1)} %select_maximum_fusion.3.head_ref, ...), custom_call_target="tpu_custom_call" | custom-call | flops 20000000000 | bytes 16000000 | tf_op jit(solution)/shard_map/mixer_backward/pallas_call | solution.py:435
  62.9 3.9 %fusion.9 = f32[256,512]{1,0:T(8,128)S(1)} fusion(bf16[512,4384]{0,1:T(8,128)(2,1)} %collective-permute-done.1, bf16[256,288]{1,0:T(8,128)(2,1)S(1)} %bitcast.68, bf16[256,2048]{1,0:T(8,128)(2,1)S(1)} %get-tuple-element.92, bf16[256,2048]{1,0:T(8,128)(2,1)S(1)} %get-tuple-element.91), kind=kOutput, calls=%fused_computation.28 | convolution fusion | flops 1155973120 | bytes 7258112 | tf_op jit(solution)/shard_map/dot_general | solution.py:32
  68.5 2.6 %known_rows.1 = (bf16[1024,1024]{1,0:T(8,128)(2,1)S(1)}, bf16[1024,1024]{1,0:T(8,128)(2,1)S(1)}) custom-call(f32[1,1024]{1,0:T(1,128)S(1)} %bitcast.64, bf16[512,1024]{1,0:T(8,128)(2,1)S(1)} %known_pack.1.first, bf16[512,1024]{1,0:T(8,128)(2,1)S(1)} %collective-permute-done.6.second, bf16[512,1024]{1,0:T(8,128)(2,1)} %collective-permute-done.7.third, ...), custom_call_target="tpu_custom_call" | custom-call | flops 1 | bytes 1 | tf_op jit(solution)/shard_map/known_rows/pallas_call | solution.py:506
  71.2 3.1 %fusion.11 = f32[256,1024]{1,0:T(8,128)S(1)} fusion(bf16[1024,1024]{1,0:T(8,128)(2,1)} %collective-permute-done.2, bf16[256,2048]{1,0:T(8,128)(2,1)S(1)} %copy-done.7, s32[]{:T(128)S(6)} %select_n.243), kind=kOutput, calls=%fused_computation.43 | convolution fusion | flops 536870912 | bytes 3670020 | tf_op jit(solution)/shard_map/dot_general | solution.py:32
  77.9 4.2 %early_products.1 = (f32[512,512]{1,0:T(8,128)S(1)}, bf16[512,512]{1,0:T(8,128)(2,1)}, f32[256,1024]{1,0:T(8,128)S(1)}, bf16[256,1024]{1,0:T(8,128)(2,1)S(1)}) custom-call(s32[1]{0:T(128)} %bitcast.23.core_ref, bf16[1024,1024]{1,0:T(8,128)(2,1)S(1)} %get-tuple-element.101.normed_ref, bf16[1024,1024]{1,0:T(8,128)(2,1)S(1)} %get-tuple-element.102.up_ref, ...), custom_call_target="tpu_custom_call" | custom-call | flops 1 | bytes 1 | tf_op jit(solution)/shard_map/early_products/pallas_call | solution.py:535
  87.3 3.1 %collective-permute-start.13 = (bf16[256,512]{1,0:T(8,128)(2,1)S(1)}, bf16[256,512]{1,0:T(8,128)(2,1)S(1)}, u32[]{:S(2)}, u32[]{:S(2)}) collective-permute-start(bf16[256,512]{1,0:T(8,128)(2,1)S(1)} %dynamic-slice_convert_fusion), channel_id=1, source_target_pairs={{0,16},{2,18},{4,20},{6,22},{8,24},{10,26},{12,28},{14,30},{16,0},... | collective-permute-start | bytes 786440 | tf_op jit(solution)/shard_map/ppermute | solution.py:622
  92.3 9.5 %collective-permute-done.13 = bf16[256,512]{1,0:T(8,128)(2,1)S(1)} collective-permute-done((bf16[256,512]{1,0:T(8,128)(2,1)S(1)}, bf16[256,512]{1,0:T(8,128)(2,1)S(1)}, u32[]{:S(2)}, u32[]{:S(2)}) %collective-permute-start.13) | collective-permute-done | bytes 262176 | tf_op jit(solution)/shard_map/ppermute | solution.py:622
  102.7 3.4 %collective-permute-start.11 = (bf16[64,1024]{1,0:T(8,128)(2,1)S(1)}, bf16[64,1024]{1,0:T(8,128)(2,1)S(1)}, u32[]{:S(2)}, u32[]{:S(2)}) collective-permute-start(bf16[64,1024]{1,0:T(8,128)(2,1)S(1)} %dynamic-slice_convert_fusion.5), channel_id=1, source_target_pairs={{0,16},{2,18},{4,20},{6,22},{8,24},{10,26},{12,28},{14,30},{16,0},... | collective-permute-start | bytes 393224 | tf_op jit(solution)/shard_map/ppermute | solution.py:622
  106.1 2.7 %collective-permute-done.14 = bf16[128,512]{1,0:T(8,128)(2,1)S(1)} collective-permute-done((bf16[128,512]{1,0:T(8,128)(2,1)S(1)}, bf16[128,512]{1,0:T(8,128)(2,1)S(1)}, u32[]{:S(2)}, u32[]{:S(2)}) %collective-permute-start.14) | collective-permute-done | bytes 131104 | tf_op jit(solution)/shard_map/ppermute | solution.py:622
  108.8 3.5 %collective-permute-done.11 = bf16[64,1024]{1,0:T(8,128)(2,1)S(1)} collective-permute-done((bf16[64,1024]{1,0:T(8,128)(2,1)S(1)}, bf16[64,1024]{1,0:T(8,128)(2,1)S(1)}, u32[]{:S(2)}, u32[]{:S(2)}) %collective-permute-start.11) | collective-permute-done | bytes 131104 | tf_op jit(solution)/shard_map/ppermute | solution.py:622
  114.7 2.9 %collective-permute-start.19 = (bf16[128,512]{1,0:T(8,128)(2,1)S(1)}, bf16[128,512]{1,0:T(8,128)(2,1)S(1)}, u32[]{:S(2)}, u32[]{:S(2)}) collective-permute-start(bf16[128,512]{1,0:T(8,128)(2,1)S(1)} %convert_add_fusion.8), channel_id=1, source_target_pairs={{0,8},{2,10},{4,12},{6,14},{8,0},{10,2},{12,4},{14,6},{16,24},{18,... | collective-permute-start | bytes 393224 | tf_op jit(solution)/shard_map/ppermute | solution.py:622
  117.7 6.1 %collective-permute-done.18 = bf16[64,1024]{1,0:T(8,128)(2,1)S(1)} collective-permute-done((bf16[64,1024]{1,0:T(8,128)(2,1)S(1)}, bf16[64,1024]{1,0:T(8,128)(2,1)S(1)}, u32[]{:S(2)}, u32[]{:S(2)}) %collective-permute-start.18) | collective-permute-done | bytes 131104 | tf_op jit(solution)/shard_map/ppermute | solution.py:622
  126.4 10.2 %collective-permute-done.21 = bf16[128,1024]{1,0:T(8,128)(2,1)S(1)} collective-permute-done((bf16[128,1024]{1,0:T(8,128)(2,1)S(1)}, bf16[128,1024]{1,0:T(8,128)(2,1)S(1)}, u32[]{:S(2)}, u32[]{:S(2)}) %collective-permute-start.21) | collective-permute-done | bytes 262176 | tf_op jit(solution)/shard_map/ppermute | solution.py:622
  136.7 2.1 collective-permute-done.22
  144.5 3.0 %collective-permute-done.28 = bf16[160,512]{1,0:T(8,128)(2,1)S(1)} collective-permute-done((bf16[160,512]{1,0:T(8,128)(2,1)S(1)}, bf16[160,512]{1,0:T(8,128)(2,1)S(1)}, u32[]{:S(2)}, u32[]{:S(2)}) %collective-permute-start.28) | collective-permute-done | bytes 163872 | tf_op jit(solution)/shard_map/ppermute | solution.py:622
  147.6 6.6 %collective-permute-done.32 = bf16[160,512]{1,0:T(8,128)(2,1)S(1)} collective-permute-done((bf16[160,512]{1,0:T(8,128)(2,1)S(1)}, bf16[160,512]{1,0:T(8,128)(2,1)S(1)}, u32[]{:S(2)}, u32[]{:S(2)}) %collective-permute-start.32) | collective-permute-done | bytes 163872 | tf_op jit(solution)/shard_map/ppermute | solution.py:622
  156.5 3.2 %collective-permute-done.33 = bf16[80,512]{1,0:T(8,128)(2,1)S(1)} collective-permute-done((bf16[80,512]{1,0:T(8,128)(2,1)S(1)}, bf16[80,512]{1,0:T(8,128)(2,1)S(1)}, u32[]{:S(2)}, u32[]{:S(2)}) %collective-permute-start.33) | collective-permute-done | bytes 81952 | tf_op jit(solution)/shard_map/ppermute | solution.py:622
  165.2 3.2 %collective-permute-start.35 = (bf16[232,512]{1,0:T(8,128)(2,1)S(1)}, bf16[232,512]{1,0:T(8,128)(2,1)S(1)}, u32[]{:S(2)}, u32[]{:S(2)}) collective-permute-start(bf16[232,512]{1,0:T(8,128)(2,1)S(1)} %pad_maximum_fusion.5), channel_id=1, source_target_pairs={{0,16},{2,18},{4,20},{6,22},{8,24},{10,26},{12,28},{14,30},{16,0},... | collective-permute-start | bytes 712712 | tf_op jit(solution)/shard_map/ppermute | solution.py:622
  169.6 5.5 %collective-permute-done.35 = bf16[232,512]{1,0:T(8,128)(2,1)S(1)} collective-permute-done((bf16[232,512]{1,0:T(8,128)(2,1)S(1)}, bf16[232,512]{1,0:T(8,128)(2,1)S(1)}, u32[]{:S(2)}, u32[]{:S(2)}) %collective-permute-start.35) | collective-permute-done | bytes 237600 | tf_op jit(solution)/shard_map/ppermute | solution.py:622
  175.3 8.5 %collective-permute-done.24 = bf16[512,1024]{1,0:T(8,128)(2,1)S(1)} collective-permute-done((bf16[512,1024]{1,0:T(8,128)(2,1)S(1)}, bf16[512,1024]{1,0:T(8,128)(2,1)S(1)}, u32[]{:S(2)}, u32[]{:S(2)}) %collective-permute-start.24) | collective-permute-done | bytes 1048608 | tf_op jit(solution)/shard_map/ppermute | solution.py:622
  184.8 6.2 %collective-permute-done.27 = bf16[1024,512]{1,0:T(8,128)(2,1)S(1)} collective-permute-done((bf16[1024,512]{1,0:T(8,128)(2,1)S(1)}, bf16[1024,512]{1,0:T(8,128)(2,1)S(1)}, u32[]{:S(2)}, u32[]{:S(2)}) %collective-permute-start.27) | collective-permute-done | bytes 1048608 | tf_op jit(solution)/shard_map/ppermute | solution.py:622
  193.2 4.9 %convert_element_type.177.base_ref = f32[4384,512]{1,0:T(8,128)} convert(bf16[4384,512]{1,0:T(8,128)(2,1)S(1)} %broadcast_dynamic-update-slice_fusion) | non-fusion elementwise | flops 2244608 | bytes 13467648 | tf_op jit(solution)/shard_map/convert_element_type | solution.py:805
  198.1 2.5 %convert_element_type.182 = f32[1024,1024]{1,0:T(8,128)} convert(bf16[1024,1024]{1,0:T(8,128)(2,1)S(1)} %maximum_select_fusion.1) | non-fusion elementwise | flops 1048576 | bytes 6291456 | tf_op jit(solution)/shard_map/convert_element_type | solution.py:801
  200.6 2.8 %collective-permute-done.37 = bf16[320,512]{1,0:T(8,128)(2,1)S(1)} collective-permute-done((bf16[320,512]{1,0:T(8,128)(2,1)S(1)}, bf16[320,512]{1,0:T(8,128)(2,1)S(1)}, u32[]{:S(2)}, u32[]{:S(2)}) %collective-permute-start.37) | collective-permute-done | bytes 327712 | tf_op jit(solution)/shard_map/ppermute | solution.py:622
  209.0 6.3 %collective-permute-done.38.first_got = bf16[640,512]{1,0:T(8,128)(2,1)S(1)} collective-permute-done((bf16[640,512]{1,0:T(8,128)(2,1)S(1)}, bf16[640,512]{1,0:T(8,128)(2,1)S(1)}, u32[]{:S(2)}, u32[]{:S(2)}) %collective-permute-start.38) | collective-permute-done | bytes 655392 | tf_op jit(solution)/shard_map/ppermute | solution.py:622
  215.5 2.9 %late_rows.1 = f32[4384,512]{1,0:T(8,128)} custom-call(s32[2]{0:T(128)S(1)} %pad_add_fusion.side_ref, f32[4384,512]{1,0:T(8,128)} %convert_element_type.177.base_ref, bf16[640,512]{1,0:T(8,128)(2,1)S(1)} %maximum_select_fusion.6.first, bf16[640,512]{1,0:T(8,128)(2,1)S(1)} %collective-permute-done.38.first_got, ...), custom_call_target="tpu_custom_call", output_to_operand_aliasing={{}: (1, {})} | custom-call | flops 1 | bytes 8000000 | tf_op jit(solution)/shard_map/late_rows/pallas_call | solution.py:597
  (238 shorter events, 58.8 us)
Async XLA Ops:
  0.6 21.6 %collective-permute-start.1 = (bf16[512,4384]{0,1:T(8,128)(2,1)}, bf16[512,4384]{0,1:T(8,128)(2,1)}, u32[]{:S(2)}, u32[]{:S(2)}) collective-permute-start(bf16[512,4384]{0,1:T(8,128)(2,1)} %param.15), channel_id=1, source_target_pairs={{0,1},{1,0},{2,3},{3,2},{4,5},{5,4},{6,7},{7,6},{8,9},{9,8},{10,11... | collective-permute-start | bytes 13467656 | tf_op jit(solution)/shard_map/ppermute | solution.py:619
  4.6 56.8 %collective-permute-start.6 = (bf16[512,1024]{1,0:T(8,128)(2,1)S(1)}, bf16[512,1024]{1,0:T(8,128)(2,1)S(1)}, u32[]{:S(2)}, u32[]{:S(2)}) collective-permute-start(bf16[512,1024]{1,0:T(8,128)(2,1)S(1)} %known_pack.1.first), channel_id=1, source_target_pairs={{0,2},{2,0},{4,6},{6,4},{8,10},{10,8},{12,14},{14,12},{16,18},{18,... | collective-permute-start | bytes 3145736 | tf_op jit(solution)/shard_map/ppermute | solution.py:622
  7.2 54.3 %collective-permute-start.7 = (bf16[512,1024]{1,0:T(8,128)(2,1)S(1)}, bf16[512,1024]{1,0:T(8,128)(2,1)}, u32[]{:S(2)}, u32[]{:S(2)}) collective-permute-start(bf16[512,1024]{1,0:T(8,128)(2,1)S(1)} %known_pack.1.first), channel_id=1, source_target_pairs={{0,4},{2,6},{4,0},{6,2},{8,12},{10,14},{12,8},{14,10},{16,20},{18,... | collective-permute-start | bytes 3145736 | tf_op jit(solution)/shard_map/ppermute | solution.py:622
  9.1 10.5 %collective-permute-start.2 = (bf16[1024,1024]{1,0:T(8,128)(2,1)}, bf16[1024,1024]{1,0:T(8,128)(2,1)}, u32[]{:S(2)}, u32[]{:S(2)}) collective-permute-start(bf16[1024,1024]{1,0:T(8,128)(2,1)} %param.22), channel_id=1, source_target_pairs={{0,1},{1,0},{2,3},{3,2},{4,5},{5,4},{6,7},{7,6},{8,9},{9,8},{10,11... | collective-permute-start | bytes 6291464 | tf_op jit(solution)/shard_map/ppermute | solution.py:619
  14.9 46.5 %collective-permute-start.8 = (bf16[512,1024]{1,0:T(8,128)(2,1)S(1)}, bf16[512,1024]{1,0:T(8,128)(2,1)}, u32[]{:S(2)}, u32[]{:S(2)}) collective-permute-start(bf16[512,1024]{1,0:T(8,128)(2,1)S(1)} %known_pack.1.first), channel_id=1, source_target_pairs={{0,6},{2,4},{4,2},{6,0},{8,14},{10,12},{12,10},{14,8},{16,22},{18,... | collective-permute-start | bytes 3145736 | tf_op jit(solution)/shard_map/ppermute | solution.py:622
  38.5 39.4 %collective-permute-start.3 = (bf16[512,512]{1,0:T(8,128)(2,1)}, bf16[512,512]{1,0:T(8,128)(2,1)}, u32[]{:S(2)}, u32[]{:S(2)}) collective-permute-start(bf16[512,512]{1,0:T(8,128)(2,1)} %get-tuple-element.157), channel_id=1, source_target_pairs={{0,2},{2,0},{4,6},{6,4},{8,10},{10,8},{12,14},{14,12},{16,18},{18,... | collective-permute-start | bytes 1572872 | tf_op jit(solution)/shard_map/ppermute | solution.py:622
  40.4 37.4 %collective-permute-start.4 = (bf16[512,512]{1,0:T(8,128)(2,1)}, bf16[512,512]{1,0:T(8,128)(2,1)}, u32[]{:S(2)}, u32[]{:S(2)}) collective-permute-start(bf16[512,512]{1,0:T(8,128)(2,1)} %get-tuple-element.156), channel_id=1, source_target_pairs={{0,4},{2,6},{4,0},{6,2},{8,12},{10,14},{12,8},{14,10},{16,20},{18,... | collective-permute-start | bytes 1572872 | tf_op jit(solution)/shard_map/ppermute | solution.py:622
  61.4 16.4 %collective-permute-start.5 = (bf16[512,512]{1,0:T(8,128)(2,1)}, bf16[512,512]{1,0:T(8,128)(2,1)}, u32[]{:S(2)}, u32[]{:S(2)}) collective-permute-start(bf16[512,512]{1,0:T(8,128)(2,1)} %get-tuple-element.155), channel_id=1, source_target_pairs={{0,6},{2,4},{4,2},{6,0},{8,14},{10,12},{12,10},{14,8},{16,22},{18,... | collective-permute-start | bytes 1572872 | tf_op jit(solution)/shard_map/ppermute | solution.py:622
  82.1 8.4 %collective-permute-start.9 = (bf16[256,1024]{1,0:T(8,128)(2,1)S(1)}, bf16[256,1024]{1,0:T(8,128)(2,1)S(1)}, u32[]{:S(2)}, u32[]{:S(2)}) collective-permute-start(bf16[256,1024]{1,0:T(8,128)(2,1)S(1)} %get-tuple-element.108), channel_id=1, source_target_pairs={{0,1},{1,0},{2,3},{3,2},{4,5},{5,4},{6,7},{7,6},{8,9},{9,8},{10,11... | collective-permute-start | bytes 1572872 | tf_op jit(solution)/shard_map/ppermute | solution.py:619
  82.6 29.8 %collective-permute-start.15 = (bf16[256,640]{1,0:T(8,128)(2,1)}, bf16[256,640]{1,0:T(8,128)(2,1)S(1)}, u32[]{:S(2)}, u32[]{:S(2)}) collective-permute-start(bf16[256,640]{1,0:T(8,128)(2,1)} %get-tuple-element.112), channel_id=1, source_target_pairs={{0,2},{2,0},{4,6},{6,4},{8,10},{10,8},{12,14},{14,12},{16,18},{18,... | collective-permute-start | bytes 983048 | tf_op jit(solution)/shard_map/ppermute | solution.py:622
  84.5 27.9 %collective-permute-start.16 = (bf16[256,640]{1,0:T(8,128)(2,1)}, bf16[256,640]{1,0:T(8,128)(2,1)S(1)}, u32[]{:S(2)}, u32[]{:S(2)}) collective-permute-start(bf16[256,640]{1,0:T(8,128)(2,1)} %get-tuple-element.113), channel_id=1, source_target_pairs={{0,4},{2,6},{4,0},{6,2},{8,12},{10,14},{12,8},{14,10},{16,20},{18,... | collective-permute-start | bytes 983048 | tf_op jit(solution)/shard_map/ppermute | solution.py:622
  86.1 26.4 %collective-permute-start.17 = (bf16[256,640]{1,0:T(8,128)(2,1)}, bf16[256,640]{1,0:T(8,128)(2,1)S(1)}, u32[]{:S(2)}, u32[]{:S(2)}) collective-permute-start(bf16[256,640]{1,0:T(8,128)(2,1)} %get-tuple-element.114), channel_id=1, source_target_pairs={{0,6},{2,4},{4,2},{6,0},{8,14},{10,12},{12,10},{14,8},{16,22},{18,... | collective-permute-start | bytes 983048 | tf_op jit(solution)/shard_map/ppermute | solution.py:622
  87.3 14.5 %collective-permute-start.13 = (bf16[256,512]{1,0:T(8,128)(2,1)S(1)}, bf16[256,512]{1,0:T(8,128)(2,1)S(1)}, u32[]{:S(2)}, u32[]{:S(2)}) collective-permute-start(bf16[256,512]{1,0:T(8,128)(2,1)S(1)} %dynamic-slice_convert_fusion), channel_id=1, source_target_pairs={{0,16},{2,18},{4,20},{6,22},{8,24},{10,26},{12,28},{14,30},{16,0},... | collective-permute-start | bytes 786440 | tf_op jit(solution)/shard_map/ppermute | solution.py:622
  90.7 11.9 %collective-permute-start.10 = (bf16[128,1024]{1,0:T(8,128)(2,1)S(1)}, bf16[128,1024]{1,0:T(8,128)(2,1)S(1)}, u32[]{:S(2)}, u32[]{:S(2)}) collective-permute-start(bf16[128,1024]{1,0:T(8,128)(2,1)S(1)} %dynamic-slice_convert_fusion.1), channel_id=1, source_target_pairs={{0,8},{2,10},{4,12},{6,14},{8,0},{10,2},{12,4},{14,6},{16,24},{18,... | collective-permute-start | bytes 786440 | tf_op jit(solution)/shard_map/ppermute | solution.py:622
  102.7 9.7 %collective-permute-start.11 = (bf16[64,1024]{1,0:T(8,128)(2,1)S(1)}, bf16[64,1024]{1,0:T(8,128)(2,1)S(1)}, u32[]{:S(2)}, u32[]{:S(2)}) collective-permute-start(bf16[64,1024]{1,0:T(8,128)(2,1)S(1)} %dynamic-slice_convert_fusion.5), channel_id=1, source_target_pairs={{0,16},{2,18},{4,20},{6,22},{8,24},{10,26},{12,28},{14,30},{16,0},... | collective-permute-start | bytes 393224 | tf_op jit(solution)/shard_map/ppermute | solution.py:622
  114.0 10.0 %collective-permute-start.20 = (bf16[640,512]{1,0:T(8,128)(2,1)S(1)}, bf16[640,512]{1,0:T(8,128)(2,1)S(1)}, u32[]{:S(2)}, u32[]{:S(2)}) collective-permute-start(bf16[640,512]{1,0:T(8,128)(2,1)S(1)} %get-tuple-element.123), channel_id=1, source_target_pairs={{0,1},{1,0},{2,3},{3,2},{4,5},{5,4},{6,7},{7,6},{8,9},{9,8},{10,11... | collective-permute-start | bytes 1966088 | tf_op jit(solution)/shard_map/ppermute | solution.py:619
  114.7 9.1 %collective-permute-start.18 = (bf16[64,1024]{1,0:T(8,128)(2,1)S(1)}, bf16[64,1024]{1,0:T(8,128)(2,1)S(1)}, u32[]{:S(2)}, u32[]{:S(2)}) collective-permute-start(bf16[64,1024]{1,0:T(8,128)(2,1)S(1)} %convert_add_fusion.9), channel_id=1, source_target_pairs={{0,16},{2,18},{4,20},{6,22},{8,24},{10,26},{12,28},{14,30},{16,0},... | collective-permute-start | bytes 393224 | tf_op jit(solution)/shard_map/ppermute | solution.py:622
  114.7 9.3 %collective-permute-start.19 = (bf16[128,512]{1,0:T(8,128)(2,1)S(1)}, bf16[128,512]{1,0:T(8,128)(2,1)S(1)}, u32[]{:S(2)}, u32[]{:S(2)}) collective-permute-start(bf16[128,512]{1,0:T(8,128)(2,1)S(1)} %convert_add_fusion.8), channel_id=1, source_target_pairs={{0,8},{2,10},{4,12},{6,14},{8,0},{10,2},{12,4},{14,6},{16,24},{18,... | collective-permute-start | bytes 393224 | tf_op jit(solution)/shard_map/ppermute | solution.py:622
  124.0 12.5 %collective-permute-start.21 = (bf16[128,1024]{1,0:T(8,128)(2,1)S(1)}, bf16[128,1024]{1,0:T(8,128)(2,1)S(1)}, u32[]{:S(2)}, u32[]{:S(2)}) collective-permute-start(bf16[128,1024]{1,0:T(8,128)(2,1)S(1)} %maximum_select_fusion.12), channel_id=1, source_target_pairs={{0,8},{2,10},{4,12},{6,14},{8,0},{10,2},{12,4},{14,6},{16,24},{18,... | collective-permute-start | bytes 786440 | tf_op jit(solution)/shard_map/ppermute | solution.py:622
  124.1 14.7 %collective-permute-start.22 = (bf16[256,512]{1,0:T(8,128)(2,1)S(1)}, bf16[256,512]{1,0:T(8,128)(2,1)S(1)}, u32[]{:S(2)}, u32[]{:S(2)}) collective-permute-start(bf16[256,512]{1,0:T(8,128)(2,1)S(1)} %maximum_select_fusion.13), channel_id=1, source_target_pairs={{0,16},{2,18},{4,20},{6,22},{8,24},{10,26},{12,28},{14,30},{16,0},... | collective-permute-start | bytes 786440 | tf_op jit(solution)/shard_map/ppermute | solution.py:622
  139.0 23.1 %collective-permute-start.23 = (bf16[256,1024]{1,0:T(8,128)(2,1)S(1)}, bf16[256,1024]{1,0:T(8,128)(2,1)S(1)}, u32[]{:S(2)}, u32[]{:S(2)}) collective-permute-start(bf16[256,1024]{1,0:T(8,128)(2,1)S(1)} %maximum_select_fusion.8), channel_id=1, source_target_pairs={{0,4},{2,6},{4,0},{6,2},{8,12},{10,14},{12,8},{14,10},{16,20},{18,... | collective-permute-start | bytes 1572872 | tf_op jit(solution)/shard_map/ppermute | solution.py:622
  140.9 18.8 %collective-permute-start.26 = (bf16[584,512]{1,0:T(8,128)(2,1)S(1)}, bf16[584,512]{1,0:T(8,128)(2,1)S(1)}, u32[]{:S(2)}, u32[]{:S(2)}) collective-permute-start(bf16[584,512]{1,0:T(8,128)(2,1)S(1)} %pad_maximum_fusion.3), channel_id=1, source_target_pairs={{0,2},{2,0},{4,6},{6,4},{8,10},{10,8},{12,14},{14,12},{16,18},{18,... | collective-permute-start | bytes 1794056 | tf_op jit(solution)/shard_map/ppermute | solution.py:622
  142.5 11.8 %collective-permute-start.32 = (bf16[160,512]{1,0:T(8,128)(2,1)S(1)}, bf16[160,512]{1,0:T(8,128)(2,1)S(1)}, u32[]{:S(2)}, u32[]{:S(2)}) collective-permute-start(bf16[160,512]{1,0:T(8,128)(2,1)S(1)} %dynamic-slice_convert_fusion.2), channel_id=1, source_target_pairs={{0,16},{2,18},{4,20},{6,22},{8,24},{10,26},{12,28},{14,30},{16,0},... | collective-permute-start | bytes 491528 | tf_op jit(solution)/shard_map/ppermute | solution.py:622
  147.6 7.6 %collective-permute-start.29 = (bf16[80,512]{1,0:T(8,128)(2,1)S(1)}, bf16[80,512]{1,0:T(8,128)(2,1)S(1)}, u32[]{:S(2)}, u32[]{:S(2)}) collective-permute-start(bf16[80,512]{1,0:T(8,128)(2,1)S(1)} %dynamic-slice_convert_fusion.7), channel_id=1, source_target_pairs={{0,16},{2,18},{4,20},{6,22},{8,24},{10,26},{12,28},{14,30},{16,0},... | collective-permute-start | bytes 245768 | tf_op jit(solution)/shard_map/ppermute | solution.py:622
  161.6 7.8 %collective-permute-start.31 = (bf16[160,512]{1,0:T(8,128)(2,1)S(1)}, bf16[160,512]{1,0:T(8,128)(2,1)S(1)}, u32[]{:S(2)}, u32[]{:S(2)}) collective-permute-start(bf16[160,512]{1,0:T(8,128)(2,1)S(1)} %maximum_select_fusion.14), channel_id=1, source_target_pairs={{0,8},{2,10},{4,12},{6,14},{8,0},{10,2},{12,4},{14,6},{16,24},{18,... | collective-permute-start | bytes 491528 | tf_op jit(solution)/shard_map/ppermute | solution.py:622
  162.6 21.2 %collective-permute-start.24 = (bf16[512,1024]{1,0:T(8,128)(2,1)S(1)}, bf16[512,1024]{1,0:T(8,128)(2,1)S(1)}, u32[]{:S(2)}, u32[]{:S(2)}) collective-permute-start(bf16[512,1024]{1,0:T(8,128)(2,1)S(1)} %maximum_select_fusion.4), channel_id=1, source_target_pairs={{0,2},{2,0},{4,6},{6,4},{8,10},{10,8},{12,14},{14,12},{16,18},{18,... | collective-permute-start | bytes 3145736 | tf_op jit(solution)/shard_map/ppermute | solution.py:622
  165.2 9.9 %collective-permute-start.35 = (bf16[232,512]{1,0:T(8,128)(2,1)S(1)}, bf16[232,512]{1,0:T(8,128)(2,1)S(1)}, u32[]{:S(2)}, u32[]{:S(2)}) collective-permute-start(bf16[232,512]{1,0:T(8,128)(2,1)S(1)} %pad_maximum_fusion.5), channel_id=1, source_target_pairs={{0,16},{2,18},{4,20},{6,22},{8,24},{10,26},{12,28},{14,30},{16,0},... | collective-permute-start | bytes 712712 | tf_op jit(solution)/shard_map/ppermute | solution.py:622
  168.9 22.1 %collective-permute-start.27 = (bf16[1024,512]{1,0:T(8,128)(2,1)S(1)}, bf16[1024,512]{1,0:T(8,128)(2,1)S(1)}, u32[]{:S(2)}, u32[]{:S(2)}) collective-permute-start(bf16[1024,512]{1,0:T(8,128)(2,1)S(1)} %maximum_select_fusion.5), channel_id=1, source_target_pairs={{0,4},{2,6},{4,0},{6,2},{8,12},{10,14},{12,8},{14,10},{16,20},{18,... | collective-permute-start | bytes 3145736 | tf_op jit(solution)/shard_map/ppermute | solution.py:622
  192.1 12.1 %collective-permute-start.36 = (bf16[392,512]{1,0:T(8,128)(2,1)S(1)}, bf16[392,512]{1,0:T(8,128)(2,1)S(1)}, u32[]{:S(2)}, u32[]{:S(2)}) collective-permute-start(bf16[392,512]{1,0:T(8,128)(2,1)S(1)} %pad_maximum_fusion.4), channel_id=1, source_target_pairs={{0,4},{2,6},{4,0},{6,2},{8,12},{10,14},{12,8},{14,10},{16,20},{18,... | collective-permute-start | bytes 1204232 | tf_op jit(solution)/shard_map/ppermute | solution.py:622
  192.7 10.6 %collective-permute-start.37 = (bf16[320,512]{1,0:T(8,128)(2,1)S(1)}, bf16[320,512]{1,0:T(8,128)(2,1)S(1)}, u32[]{:S(2)}, u32[]{:S(2)}) collective-permute-start(bf16[320,512]{1,0:T(8,128)(2,1)S(1)} %maximum_select_fusion.11), channel_id=1, source_target_pairs={{0,2},{2,0},{4,6},{6,4},{8,10},{10,8},{12,14},{14,12},{16,18},{18,... | collective-permute-start | bytes 983048 | tf_op jit(solution)/shard_map/ppermute | solution.py:622
  204.6 10.7 %collective-permute-start.38 = (bf16[640,512]{1,0:T(8,128)(2,1)S(1)}, bf16[640,512]{1,0:T(8,128)(2,1)S(1)}, u32[]{:S(2)}, u32[]{:S(2)}) collective-permute-start(bf16[640,512]{1,0:T(8,128)(2,1)S(1)} %maximum_select_fusion.6.first), channel_id=1, source_target_pairs={{0,2},{2,0},{4,6},{6,4},{8,10},{10,8},{12,14},{14,12},{16,18},{18,... | collective-permute-start | bytes 1966088 | tf_op jit(solution)/shard_map/ppermute | solution.py:622
  204.9 10.6 %collective-permute-start.39 = (bf16[640,512]{1,0:T(8,128)(2,1)S(1)}, bf16[640,512]{1,0:T(8,128)(2,1)S(1)}, u32[]{:S(2)}, u32[]{:S(2)}) collective-permute-start(bf16[640,512]{1,0:T(8,128)(2,1)S(1)} %maximum_select_fusion.7.second), channel_id=1, source_target_pairs={{0,4},{2,6},{4,0},{6,2},{8,12},{10,14},{12,8},{14,10},{16,20},{18,... | collective-permute-start | bytes 1966088 | tf_op jit(solution)/shard_map/ppermute | solution.py:622
  (40 other events, 215.7 us)
